TPU v7x, 768 devices: a whole 4x8x12 slice. The times are simulated.
768 devices in a mesh: dp: 32 (over y, x), tensor: 24 (over z, core).
Axes of the slice: x: 4, y: 8, z: 12, core: 2. Of those that a mesh axis runs over, the one named last changes fastest.
Arguments:
- rollout: bfloat16 [8192, 6144], P('dp', 'tensor'), may hold values from -100 to 100
- lengths: int32 [32, 32], replicated, may hold values from 1 to 8, as said below
- packing: int32 [1024], replicated, may hold values from 0 to 1023, as said below
- norm_gain: float32 [6144], replicated, may hold values from 0.5 to 4
- query_weight: bfloat16 [6144, 6144], P(None, 'tensor'), may hold values from -0.078125 to 0.078125
- keyval_weight: bfloat16 [6144, 1536], P(None, 'tensor'), may hold values from -0.078125 to 0.078125
- out_weight: bfloat16 [6144, 6144], P('tensor'), may hold values from -0.078125 to 0.078125
Outputs:
- layer_out: bfloat16 [8192, 6144], P('dp', 'tensor')
Inputs may be any that keep to these rules, and one draw needn't show every extreme that they name: lengths[s, k] is the number of tokens of response k of source s; some response has 8 tokens in every draw. `packing`: a permutation of 0 .. 1023; response r comes from source r // 32; every owner receives exactly 32 responses, exactly 1 of them from each source.
All inputs are finite; a program needn't handle non-finite values.
Results may differ from a plain program's by a relative error of at most 0.015.
Values may be sent and summed in bfloat16 or wider, within the bound.
No kernel may reach another device: no remote copies, remote signals or barrier semaphores. Data moves between devices by JAX's collectives and lax.ppermute only.
A program may use at most 64 MiB of HBM per device.

v0:
```python
import math

import jax
import jax.numpy as jnp
from jax import lax
from jax.sharding import PartitionSpec as P

D = 6144
HD = 128
HQ_DEV = 2
GROUP = 8
MAXLEN = 8


epsilon = 1e-05
rope_base = 500000.0


def owner_map(lengths, packing, owner_id, pack_len):
    per_source = lengths.shape[1]
    chosen = lax.dynamic_slice_in_dim(packing, owner_id * per_source, per_source)
    ordered = jnp.take(lengths.reshape(-1), chosen)
    doc_start = jnp.cumsum(ordered) - ordered
    places = jnp.arange(pack_len, dtype=jnp.int32)
    inside = (places[:, None] >= doc_start[None, :]) & (
        places[:, None] < (doc_start + ordered)[None, :]
    )
    is_valid = jnp.any(inside, axis=1)
    slot_of = jnp.sum(
        jnp.where(inside, jnp.arange(per_source, dtype=jnp.int32)[None, :], 0), axis=1
    )
    response = jnp.take(chosen, slot_of)
    position = jnp.where(is_valid, places - jnp.take(doc_start, slot_of), 0)
    doc_id = jnp.where(is_valid, slot_of, per_source)
    return (response, position, doc_id, is_valid)


def rotate(values, position, head_dim):
    half_dim = head_dim // 2
    frequency = rope_base ** (-jnp.arange(half_dim, dtype=jnp.float32) * 2.0 / head_dim)
    angles = position.astype(jnp.float32)[:, None] * frequency[None, :]
    cosine = jnp.concatenate([jnp.cos(angles), jnp.cos(angles)], axis=1)[:, None, :]
    sine_table = jnp.concatenate([jnp.sin(angles), jnp.sin(angles)], axis=1)[:, None, :]
    turned = jnp.concatenate([-values[..., half_dim:], values[..., :half_dim]], axis=-1)
    return values * cosine + turned * sine_table


def body(rollout, lengths, packing, norm_gain, query_weight, keyval_weight, out_weight):
    owner_id = lax.axis_index("dp")
    tensor_index = lax.axis_index("tensor")
    tensor_count = lax.axis_size("tensor")
    source_count = lax.axis_size("dp")
    pack_len = rollout.shape[0]
    feature_share = rollout.shape[1]
    per_source = lengths.shape[1]
    response, position, doc_id, is_valid = owner_map(lengths, packing, owner_id, pack_len)
    source_start = jnp.cumsum(lengths, axis=1) - lengths
    cap_rows = max(1, per_source // source_count) * MAXLEN
    spot_of = jnp.argsort(packing)
    target = (spot_of // per_source).reshape(source_count, per_source)
    rank_in = (spot_of % per_source).reshape(source_count, per_source)
    earlier = (target[:, None, :] == target[:, :, None]) & (
        rank_in[:, None, :] < rank_in[:, :, None]
    )
    pair_start = jnp.sum(jnp.where(earlier, lengths[:, None, :], 0), axis=2)
    my_target = lax.dynamic_index_in_dim(target, owner_id, 0, keepdims=False)
    my_pair = lax.dynamic_index_in_dim(pair_start, owner_id, 0, keepdims=False)
    my_length = lax.dynamic_index_in_dim(lengths, owner_id, 0, keepdims=False)
    my_start = lax.dynamic_index_in_dim(source_start, owner_id, 0, keepdims=False)
    owners = jnp.arange(source_count, dtype=jnp.int32)[:, None, None]
    slots = jnp.arange(cap_rows, dtype=jnp.int32)[None, :, None]
    match = (
        (my_target[None, None, :] == owners)
        & (slots >= my_pair[None, None, :])
        & (slots < (my_pair + my_length)[None, None, :])
    )
    row_of = jnp.sum(
        jnp.where(match, my_start[None, None, :] + slots - my_pair[None, None, :], 0), axis=2
    )
    has_row = jnp.any(match, axis=2)
    fetched = jnp.take(rollout, row_of.reshape(-1), axis=0).reshape(
        source_count, cap_rows, feature_share
    )
    outgoing = jnp.where(has_row[..., None], fetched, jnp.zeros((), rollout.dtype))
    incoming = lax.all_to_all(outgoing, "dp", split_axis=0, concat_axis=0, tiled=True)
    slot_index = (
        response // per_source * cap_rows + jnp.take(pair_start.reshape(-1), response) + position
    )
    arrived = jnp.take(incoming.reshape(source_count * cap_rows, feature_share), slot_index, axis=0)
    packed = jnp.where(is_valid[:, None], arrived, jnp.zeros((), rollout.dtype))
    widened = lax.all_gather(packed, "tensor", axis=1, tiled=True).astype(jnp.float32)
    scaled = (widened * norm_gain[None, :]).astype(jnp.bfloat16)
    query_acc = jnp.dot(scaled, query_weight, preferred_element_type=jnp.float32)
    keyval_acc = jnp.dot(scaled, keyval_weight, preferred_element_type=jnp.float32)
    squares = jnp.sum(widened * widened, axis=1)
    query_acc, keyval_acc, squares = (query_acc, keyval_acc, squares)
    inverse = lax.rsqrt(squares / D + epsilon)
    queries = query_acc * inverse[:, None]
    keyval_share = (keyval_acc * inverse[:, None]).astype(jnp.bfloat16)
    keyval_all = lax.all_gather(keyval_share, "tensor", axis=1, tiled=True)
    kv_count = keyval_weight.shape[1] * tensor_count // (2 * HD)
    shared_head = tensor_index * HQ_DEV // GROUP
    keys = lax.dynamic_slice_in_dim(keyval_all, shared_head * HD, HD, 1)
    values = lax.dynamic_slice_in_dim(keyval_all, (kv_count + shared_head) * HD, HD, 1)
    q_rot = rotate(queries.reshape(pack_len, HQ_DEV, HD), position, HD).astype(jnp.bfloat16)
    k_rot = rotate(keys.astype(jnp.float32)[:, None, :], position, HD)[:, 0, :].astype(jnp.bfloat16)
    scores = jnp.einsum(
        "qhd,kd->hqk", q_rot, k_rot, preferred_element_type=jnp.float32
    ) / math.sqrt(HD)
    places = jnp.arange(pack_len, dtype=jnp.int32)
    allowed = (doc_id[:, None] == doc_id[None, :]) & (places[None, :] <= places[:, None])
    masked = jnp.where(allowed[None], scores, -jnp.inf)
    row_max = jnp.max(masked, axis=2, keepdims=True)
    exponent = jnp.exp(masked - row_max)
    weights = (exponent / jnp.sum(exponent, axis=2, keepdims=True)).astype(jnp.bfloat16)
    context = jnp.einsum("hqk,kd->qhd", weights, values, preferred_element_type=jnp.float32)
    context = context.astype(jnp.bfloat16).reshape(pack_len, HQ_DEV * HD)
    partial_sum = jnp.dot(context, out_weight, preferred_element_type=jnp.float32)
    summed = lax.psum_scatter(
        partial_sum.astype(jnp.bfloat16), "tensor", scatter_dimension=1, tiled=True
    ).astype(jnp.float32)
    result = jnp.where(is_valid[:, None], summed + packed.astype(jnp.float32), 0.0)
    return result.astype(jnp.bfloat16)


def solution(mesh):
    in_specs = (
        P("dp", "tensor"),
        P(),
        P(),
        P(),
        P(None, "tensor"),
        P(None, "tensor"),
        P("tensor", None),
    )
    out_specs = P("dp", "tensor")
    return jax.shard_map(body, mesh=mesh, in_specs=in_specs, out_specs=out_specs, check_vma=False)
```

profile of v0, /device:TPU:2, one launch (start us, length us, event | category | flops | bytes accessed | tf_op | source)
XLA Modules:
  0.0 286.4 jit_solution(12658647741150831338)
XLA Ops:
  6.5 5.2 %sort.17 = (s32[1024]{0:T(1024)}, s32[1024]{0:T(1024)S(1)}) sort(s32[1024]{0:T(1024)} %param.13, s32[1024]{0:T(1024)S(1)} %iota.55), dimensions={0}, to_apply=%region_2.3 | sort | flops 10240 | bytes 16384 | tf_op jit(solution)/shard_map/jit(argsort)/sort | solution.py:59
  11.9 0.9 reduce_window_sum.18
  12.8 1.6 select_reduce_fusion
  17.3 1.9 gather_fusion.2
  19.2 0.8 bitcast_select_fusion
  20.0 13.1 %all-to-all-start = ((bf16[32,8,256]{2,1,0:T(8,128)(2,1)}), bf16[32,8,256]{2,1,0:T(8,128)(2,1)S(1)}, u32[]{:S(2)}, u32[]{:S(2)}) async-start(bf16[32,8,256]{2,1,0:T(8,128)(2,1)} %bitcast_select_fusion), calls=%async_computation | async-start | bytes 262144 | tf_op jit(solution)/shard_map/all_to_all | solution.py:85
  33.1 0.8 reshape.289
  38.8 19.8 %add_select_fusion.2 = (s32[256]{0:T(256)S(1)}, s32[256]{0:T(256)S(1)}) fusion(s32[]{:T(128)} %bitcast.32, s32[]{:T(128)} %bitcast.31, s32[]{:T(128)} %bitcast.30, s32[]{:T(128)} %bitcast.29, s32[]{:T(128)} %bitcast.28, s32[]{:T(128)} %bitcast.27, s32[]{:T(128)} %bitcast.26, s32[]{:T(128)} %bitcast.25, s32[]{:T(128)} %bitcast.24, s32[]{:T(128)} %bitcast.23, ...), kind=kLoop, calls=%fused_computation.83 | loop fusion | flops 18432 | bytes 3200 | tf_op jit(solution)/shard_map/jit(_take)/jit(_where)/select_n | solution.py:87
  58.6 1.4 gather_fusion.1
  60.0 20.0 %fusion.55 = (f32[256]{0:T(256)S(1)}, s32[256]{0:T(256)S(1)}) fusion(pred[256]{0:T(512)(128)(4,1)S(1)} %fusion.32, s32[]{:T(128)} %bitcast.64, s32[]{:T(128)} %bitcast.63, s32[]{:T(128)} %bitcast.62, s32[]{:T(128)} %bitcast.61, s32[]{:T(128)} %bitcast.60, s32[]{:T(128)} %bitcast.59, s32[]{:T(128)} %bitcast.58, s32[]{:T(128)} %bitcast.57, s32[]{:T(128)} %bitcast.56, ...), kind=kLoop, calls=%fused_computation.144 | loop fusion | flops 18432 | bytes 3456 | tf_op jit(solution)/shard_map/convert_element_type | solution.py:41
  80.0 1.2 gather_fusion.3
  81.2 0.8 select_select_fusion
  83.8 66.5 %all-gather.2.cloned.1.call-done = bf16[256,6144]{1,0:T(8,128)(2,1)} async-done(((bf16[256,256]{1,0:T(8,128)(2,1)}), bf16[256,6144]{1,0:T(8,128)(2,1)}) %all-gather.2.cloned.1.call-update) | async-done | bytes 3145744 | tf_op jit(solution)/shard_map/all_gather | solution.py:91
  150.3 2.7 fusion.2
  153.2 3.5 %fusion.11 = f32[256,256]{0,1:T(8,128)S(1)} fusion(bf16[6144,256]{1,0:T(8,128)(2,1)} %param.15, bf16[256,6144]{1,0:T(8,128)(2,1)S(1)} %copy-done.1, f32[6144]{0:T(1024)} %param.14, f32[256]{0:T(256)S(1)} %add_rsqrt_fusion), kind=kOutput, calls=%fused_computation.17 | convolution fusion | flops 810090496 | bytes 6579200 | tf_op jit(solution)/shard_map/dot_general | solution.py:93
  156.7 1.1 fusion.17
  157.8 24.8 %all_gather.7 = bf16[256,1536]{0,1:T(8,128)(2,1)S(1)} all-gather(bf16[256,64]{0,1:T(8,128)(2,1)S(1)} %fusion.17), channel_id=1, replica_groups=mesh['dp'=32,'tensor'=24] {'tensor'}, dimensions={1}, use_global_device_ids=true | all-gather | bytes 819200 | tf_op jit(solution)/shard_map/all_gather | solution.py:100
  182.7 0.9 copy-done.2
  184.3 1.3 fusion.62
  185.6 2.0 fusion.10
  187.6 1.5 convolution_convert_fusion.1
  189.1 2.7 convolution_convert_fusion
  191.8 86.0 %reduce-scatter.2.cloned.1.call-done = bf16[256,256]{1,0:T(8,128)(2,1)} async-done(((bf16[256,6144]{1,0:T(8,128)(2,1)}), bf16[256,256]{1,0:T(8,128)(2,1)}) %reduce-scatter.2.cloned.1.call-update) | async-done | bytes 131088 | tf_op jit(solution)/shard_map/reduce_scatter | solution.py:119
  277.8 1.7 select_convert_fusion
  (60 shorter events, 10.5 us)
Async XLA Ops:
  6.5 182.6 %copy-start = (bf16[256,6144]{1,0:T(8,128)(2,1)S(1)}, bf16[256,6144]{1,0:T(8,128)(2,1)}, u32[]{:S(2)}) copy-start(bf16[256,6144]{1,0:T(8,128)(2,1)} %param.17) | copy-start | bytes 9437188
  20.0 60.1 %all-to-all-start = ((bf16[32,8,256]{2,1,0:T(8,128)(2,1)}), bf16[32,8,256]{2,1,0:T(8,128)(2,1)S(1)}, u32[]{:S(2)}, u32[]{:S(2)}) async-start(bf16[32,8,256]{2,1,0:T(8,128)(2,1)} %bitcast_select_fusion), calls=%async_computation | async-start | bytes 262144 | tf_op jit(solution)/shard_map/all_to_all | solution.py:85
  33.0 117.3 %all-gather.2.cloned.1.call-start = ((), (), s32[]{:S(2)}) async-start(), calls=%async_computation.2 | async-start | bytes 3276800 | tf_op jit(solution)/shard_map/all_gather | solution.py:91
  82.0 195.8 %reduce-scatter.2.cloned.1.call-start = ((), (), s32[]{:S(2)}) async-start(), calls=%async_computation.3 | async-start | bytes 3276800 | tf_op jit(solution)/shard_map/reduce_scatter | solution.py:119
  150.3 2.8 copy-start.1
  153.2 3.5 %copy-start.4 = (bf16[6144,64]{0,1:T(8,128)(2,1)S(1)}, bf16[6144,64]{0,1:T(8,128)(2,1)}, u32[]{:S(2)}) copy-start(bf16[6144,64]{0,1:T(8,128)(2,1)} %param.16) | copy-start | bytes 2359300
  153.2 3.5 %copy-start.5 = (f32[6144]{0:T(1024)S(1)}, f32[6144]{0:T(1024)}, u32[]{:S(2)}) copy-start(f32[6144]{0:T(1024)} %param.14) | copy-start | bytes 73732
  156.7 27.5 %copy-start.3 = (f32[256,128]{0,1:T(8,128)S(1)}, f32[256,128]{0,1:T(8,128)}, u32[]{:S(2)}) copy-start(f32[256,128]{0,1:T(8,128)} %get-tuple-element.95) | copy-start | bytes 393220
  182.7 0.9 copy-start.2
Sparse Core Ops, SparseCore 0:
  82.1 68.1 all-gather.1
  192.0 85.8 reduce-scatter.1
where the time goes:
time: 288 us; the launch traced here: 286 us
  waiting for transfers between devices  153 us (53%)
  other arithmetic  60 us (21%)
  blocking collectives  24.8 us (9%)
  between operations  13.7 us (5%)
  starting transfers between devices  13.1 us (5%)
  matrix products  12.1 us (4%)
  local copies, waits for them, and re-layouts  10.1 us (4%)
    reduce_scatter x1, waiting for transfers between devices, body(): lax.psum_scatter(partial_sum.astype(jnp.bfloat16), 'tensor', scatter_dime...  86 us
    all_gather x1, waiting for transfers between devices, body(): lax.all_gather(packed, 'tensor', axis=1, tiled=True).astype(jnp.float32)  66.5 us
    all_gather x1, blocking collectives, body(): keyval_all = lax.all_gather(keyval_share, 'tensor', axis=1, tiled=True)  24.8 us
    convert_element_type x1, other arithmetic, rotate(): angles = position.astype(jnp.float32)[:, None] * frequency[None, :]  20 us
    select_n x1, other arithmetic, body(): jnp.take(pair_start.reshape(-1), response)  19.8 us
    all_to_all x1, starting transfers between devices, body(): lax.all_to_all(outgoing, 'dp', split_axis=0, concat_axis=0, tiled=True)  13.1 us
  transfers between devices with their start and end apart: 3, of which 2 were waited for; matrix products, arithmetic and copies ran while one was open for 17% of the time, Pallas kernels for 0%

commit v1 on v0

v1 whole, which is shorter than its diff:
```python
import functools
import math

import jax
import jax.numpy as jnp
from jax import lax
from jax.experimental import pallas as pl
from jax.experimental.pallas import tpu as pltpu
from jax.sharding import PartitionSpec as P

D = 6144
HD = 128
MAXLEN = 8
NZ = 12
NT = 24
FS = 256
RPS = 32
KVS = 64
EPS = 1e-05
ROPE_BASE = 500000.0
AG_ROWS = 168
VMEM = 40 * 1024 * 1024

Z_GROUPS = [[z * 2 + c for z in range(NZ)] for c in range(2)]
SWAP = [(t, t ^ 1) for t in range(NT)]


def kv_round(i):
    pairs = []
    for t in range(NT):
        j = t % 2 + 2 * (t >= NT // 2)
        g = (t % (NT // 2)) // 2
        pairs.append((t, 4 * g + (i + j) % 4))
    return pairs


def swap(v):
    return lax.ppermute(v, "tensor", SWAP)


def qkv_kernel(core, mine, theirs, gain_a, gain_b, wq_a, wq_b, wk_a, wk_b, q_out, kv_out, q_acc, kv_acc, sq_acc):
    step = pl.program_id(0)

    @pl.when(step == 0)
    def _():
        q_acc[...] = jnp.zeros_like(q_acc)
        kv_acc[...] = jnp.zeros_like(kv_acc)
        sq_acc[...] = jnp.zeros_like(sq_acc)

    for x_ref, gain, wq, wk in ((mine, gain_a, wq_a, wk_a), (theirs, gain_b, wq_b, wk_b)):
        x = x_ref[0].astype(jnp.float32)
        square = x * x
        sq_acc[...] += square[:, :128] + square[:, 128:]
        scaled = (x * gain[0]).astype(jnp.bfloat16)
        q_acc[...] += jnp.dot(scaled, wq[...], preferred_element_type=jnp.float32)
        kv_acc[...] += lax.dot_general(
            scaled, wk[...], (((1,), (1,)), ((), ())), preferred_element_type=jnp.float32
        )

    @pl.when(step == NZ - 1)
    def _():
        inverse = lax.rsqrt(jnp.sum(sq_acc[...], axis=1, keepdims=True) / D + EPS)
        q_out[...] = q_acc[...] * inverse
        kv_out[...] = (kv_acc[...] * inverse).astype(jnp.bfloat16)


def project(core, mine, theirs, gain, wq, wk_t):
    rows = mine.shape[1]
    own = lambda i, c: (2 * i + c[0], 0)
    sib = lambda i, c: (2 * i + 1 - c[0], 0)
    own3 = lambda i, c: (2 * i + c[0], 0, 0)
    sib3 = lambda i, c: (2 * i + 1 - c[0], 0, 0)
    own_t = lambda i, c: (0, 2 * i + c[0])
    sib_t = lambda i, c: (0, 2 * i + 1 - c[0])
    block = lambda i, c: (i, 0, 0)
    whole = lambda i, c: (0, 0)
    gain3 = gain.reshape(NT, 1, FS)
    return pl.pallas_call(
        qkv_kernel,
        grid_spec=pltpu.PrefetchScalarGridSpec(
            num_scalar_prefetch=1,
            grid=(NZ,),
            in_specs=[
                pl.BlockSpec((1, rows, FS), block),
                pl.BlockSpec((1, rows, FS), block),
                pl.BlockSpec((1, 1, FS), own3),
                pl.BlockSpec((1, 1, FS), sib3),
                pl.BlockSpec((FS, FS), own),
                pl.BlockSpec((FS, FS), sib),
                pl.BlockSpec((KVS, FS), own_t),
                pl.BlockSpec((KVS, FS), sib_t),
            ],
            out_specs=[pl.BlockSpec((rows, FS), whole), pl.BlockSpec((rows, KVS), whole)],
            scratch_shapes=[
                pltpu.VMEM((rows, FS), jnp.float32),
                pltpu.VMEM((rows, KVS), jnp.float32),
                pltpu.VMEM((rows, 128), jnp.float32),
            ],
        ),
        out_shape=[
            jax.ShapeDtypeStruct((rows, FS), jnp.float32),
            jax.ShapeDtypeStruct((rows, KVS), jnp.bfloat16),
        ],
        compiler_params=pltpu.CompilerParams(vmem_limit_bytes=VMEM),
        cost_estimate=pl.CostEstimate(
            flops=2 * rows * D * (FS + KVS), bytes_accessed=2 * D * (rows + FS + KVS), transcendentals=rows
        ),
        name="project",
    )(core, mine, theirs, gain3, gain3, wq, wq, wk_t, wk_t)


def attention_kernel(order, q_ref, r0, r1, r2, r3, cos_ref, sin_ref, col_ref, row_ref, out_ref):
    rows = q_ref.shape[0]
    m = order[0]
    got = [r[...].astype(jnp.float32) for r in (r0, r1, r2, r3)]

    def piece(j):
        at = lax.rem(m - j + 4, 4)
        out = got[0]
        for i in range(1, 4):
            out = jnp.where(at == i, got[i], out)
        return out

    keys = jnp.concatenate([piece(0), piece(1)], axis=1)
    values = jnp.concatenate([piece(2), piece(3)], axis=1).astype(jnp.bfloat16)
    cosine = cos_ref[...]
    sine = sin_ref[...]

    def turn(v):
        turned = jnp.concatenate([-v[:, HD // 2 :], v[:, : HD // 2]], axis=1)
        return (v * cosine + turned * sine).astype(jnp.bfloat16)

    k_rot = turn(keys)
    doc_q = col_ref[...]
    doc_k = row_ref[...]
    place_q = lax.broadcasted_iota(jnp.int32, (rows, rows), 0)
    place_k = lax.broadcasted_iota(jnp.int32, (rows, rows), 1)
    allowed = (doc_q == doc_k) & (place_k <= place_q)
    for h in range(2):
        q_rot = turn(q_ref[:, h * HD : (h + 1) * HD])
        scores = lax.dot_general(
            q_rot, k_rot, (((1,), (1,)), ((), ())), preferred_element_type=jnp.float32
        ) / math.sqrt(HD)
        masked = jnp.where(allowed, scores, -jnp.inf)
        exponent = jnp.exp(masked - jnp.max(masked, axis=1, keepdims=True))
        weights = (exponent / jnp.sum(exponent, axis=1, keepdims=True)).astype(jnp.bfloat16)
        context = jnp.dot(weights, values, preferred_element_type=jnp.float32)
        out_ref[:, h * HD : (h + 1) * HD] = context.astype(jnp.bfloat16)


def attend(order, q, pieces, cosine, sine, doc):
    rows = q.shape[0]
    vm = pl.BlockSpec(memory_space=pltpu.VMEM)
    return pl.pallas_call(
        attention_kernel,
        in_specs=[pl.BlockSpec(memory_space=pltpu.SMEM)] + [vm] * 9,
        out_specs=vm,
        out_shape=jax.ShapeDtypeStruct((rows, FS), jnp.bfloat16),
        compiler_params=pltpu.CompilerParams(vmem_limit_bytes=VMEM),
        cost_estimate=pl.CostEstimate(
            flops=8 * rows * rows * HD, bytes_accessed=4 * rows * FS, transcendentals=2 * rows * rows
        ),
        name="attend",
    )(order, q, *pieces, cosine, sine, doc[:, None], doc[None, :])


def out_kernel(core, mine, theirs, w_mine, w_theirs, out_ref):
    total = jnp.dot(mine[...], w_mine[...], preferred_element_type=jnp.float32)
    total += jnp.dot(theirs[...], w_theirs[...], preferred_element_type=jnp.float32)
    out_ref[0] = total.astype(jnp.bfloat16)


def out_project(core, mine, theirs, w_mine, w_theirs):
    rows = mine.shape[0]
    return pl.pallas_call(
        out_kernel,
        grid_spec=pltpu.PrefetchScalarGridSpec(
            num_scalar_prefetch=1,
            grid=(NZ,),
            in_specs=[
                pl.BlockSpec((rows, FS), lambda i, c: (0, 0)),
                pl.BlockSpec((rows, FS), lambda i, c: (0, 0)),
                pl.BlockSpec((FS, FS), lambda i, c: (0, 2 * i + c[0])),
                pl.BlockSpec((FS, FS), lambda i, c: (0, i)),
            ],
            out_specs=pl.BlockSpec((1, rows, FS), lambda i, c: (i, 0, 0)),
        ),
        out_shape=jax.ShapeDtypeStruct((NZ, rows, FS), jnp.bfloat16),
        compiler_params=pltpu.CompilerParams(vmem_limit_bytes=VMEM),
        cost_estimate=pl.CostEstimate(
            flops=4 * rows * FS * D // 2, bytes_accessed=2 * D * (rows + 2 * FS), transcendentals=0
        ),
        name="out_project",
    )(core, mine, theirs, w_mine, w_theirs)


def gather_rows(x):
    rows = x.shape[0]
    first = min(rows, AG_ROWS)
    rest = None
    if rows > first:
        tail = jnp.broadcast_to(x[first:][None], (NZ, rows - first, FS))
        rest = lax.all_to_all(
            tail, "tensor", split_axis=0, concat_axis=0, tiled=True, axis_index_groups=Z_GROUPS
        )
    got = lax.all_gather(x[:first], "tensor", axis=0, axis_index_groups=Z_GROUPS)
    if rest is None:
        return got
    return jnp.concatenate([got, rest], axis=1)


def layer(rows, rollout, lengths, packing, norm_gain, query_weight, keyval_weight, out_weight):
    source = lax.axis_index("dp")
    tensor_index = lax.axis_index("tensor")
    core = (tensor_index % 2).astype(jnp.int32).reshape(1)
    x = rollout[:rows]

    ow4 = out_weight.reshape(FS, NZ, 2, FS)
    send = lax.dynamic_index_in_dim(ow4, 1 - core[0], 2, keepdims=False).reshape(FS, NZ * FS)
    ow_theirs = swap(send)

    mine = gather_rows(x)
    theirs = swap(mine)
    q, keyval = project(core, mine, theirs, norm_gain, query_weight, keyval_weight.T)
    pieces = [lax.ppermute(keyval, "tensor", kv_round(i)) for i in range(4)]

    my_len = lax.dynamic_index_in_dim(lengths, source, 0, keepdims=False)
    earlier = jnp.arange(RPS)[None, :] < jnp.arange(RPS)[:, None]
    start = jnp.sum(jnp.where(earlier, my_len[None, :], 0), axis=1)
    places = jnp.arange(rows, dtype=jnp.int32)
    doc = jnp.sum((places[:, None] >= (start + my_len)[None, :]).astype(jnp.int32), axis=1)
    begun = jnp.max(jnp.where(start[None, :] <= places[:, None], start[None, :], 0), axis=1)
    position = jnp.where(doc < RPS, places - begun, 0)
    frequency = ROPE_BASE ** (-jnp.arange(HD // 2, dtype=jnp.float32) * 2.0 / HD)
    angles = position.astype(jnp.float32)[:, None] * jnp.concatenate([frequency, frequency])[None, :]
    context = attend(
        (tensor_index % 4).astype(jnp.int32).reshape(1), q, pieces, jnp.cos(angles), jnp.sin(angles), doc
    )

    partial = out_project(core, context, swap(context), out_weight, ow_theirs)
    parts = lax.all_to_all(
        partial, "tensor", split_axis=0, concat_axis=0, tiled=True, axis_index_groups=Z_GROUPS
    )
    result = (jnp.sum(parts.astype(jnp.float32), axis=0) + x.astype(jnp.float32)).astype(jnp.bfloat16)

    pack = packing.reshape(RPS, RPS)
    of_mine = pack // RPS == source
    which = jnp.sum(jnp.where(of_mine, pack % RPS, 0), axis=1)
    chosen = which[:, None] == jnp.arange(RPS)[None, :]
    o_start = jnp.sum(jnp.where(chosen, start[None, :], 0), axis=1)
    o_len = jnp.sum(jnp.where(chosen, my_len[None, :], 0), axis=1)
    slot = jnp.arange(MAXLEN, dtype=jnp.int32)
    row_of = jnp.where(slot[None, :] < o_len[:, None], o_start[:, None] + slot[None, :], -1).reshape(-1)
    pick = (row_of[:, None] == places[None, :]).astype(jnp.bfloat16)
    outgoing = jnp.dot(pick, result, preferred_element_type=jnp.float32).astype(jnp.bfloat16)
    return outgoing


def body(rollout, lengths, packing, norm_gain, query_weight, keyval_weight, out_weight):
    owner = lax.axis_index("dp")
    total = rollout.shape[0]
    outgoing = layer(
        total, rollout, lengths, packing, norm_gain, query_weight, keyval_weight, out_weight
    )
    incoming = lax.all_to_all(
        outgoing.reshape(RPS, MAXLEN, FS), "dp", split_axis=0, concat_axis=0, tiled=True
    ).reshape(RPS * MAXLEN, FS)

    chosen = lax.dynamic_index_in_dim(packing.reshape(RPS, RPS), owner, 0, keepdims=False)
    from_source = chosen // RPS
    is_source = from_source[:, None] == jnp.arange(RPS)[None, :]
    of_source = jnp.sum(jnp.where(is_source[:, :, None], lengths[None], 0), axis=1)
    is_k = (chosen % RPS)[:, None] == jnp.arange(RPS)[None, :]
    length = jnp.sum(jnp.where(is_k, of_source, 0), axis=1)
    earlier = jnp.arange(RPS)[None, :] < jnp.arange(RPS)[:, None]
    start = jnp.sum(jnp.where(earlier, length[None, :], 0), axis=1)
    places = jnp.arange(total, dtype=jnp.int32)
    inside = (places[:, None] >= start[None, :]) & (places[:, None] < (start + length)[None, :])
    valid = jnp.any(inside, axis=1)
    at = jnp.sum(jnp.where(inside, from_source[None, :] * MAXLEN + places[:, None] - start[None, :], 0), axis=1)
    at = jnp.where(valid, at, -1)
    pick = (at[:, None] == jnp.arange(RPS * MAXLEN)[None, :]).astype(jnp.bfloat16)
    return jnp.dot(pick, incoming, preferred_element_type=jnp.float32).astype(jnp.bfloat16)


def solution(mesh):
    in_specs = (
        P("dp", "tensor"),
        P(),
        P(),
        P(),
        P(None, "tensor"),
        P(None, "tensor"),
        P("tensor", None),
    )
    out_specs = P("dp", "tensor")
    return jax.shard_map(body, mesh=mesh, in_specs=in_specs, out_specs=out_specs, check_vma=False)
```

time: 288 us -> 220 us (0.76)
  the two profiles are of different devices: /device:TPU:2 before, /device:TPU:8 now
where the time goes in v1:
time: 220 us; the launch traced here: 219 us
  waiting for transfers between devices  77.5 us (35%)
  starting transfers between devices  52.1 us (24%)
  blocking collectives  45.6 us (21%)
  Pallas kernels  18.5 us (8%)
  local copies, waits for them, and re-layouts  17.5 us (8%)
  other arithmetic  5.84 us (3%)
    all_to_all x1, waiting for transfers between devices, layer(): lax.all_to_all(partial, 'tensor', split_axis=0, concat_axis=0, tiled=True...  57.3 us
    all_gather x1, blocking collectives, gather_rows(): lax.all_gather(x[:first], 'tensor', axis=0, axis_index_groups=Z_GROUPS)  45.6 us
    all_to_all x1, starting transfers between devices, gather_rows(): lax.all_to_all(tail, 'tensor', split_axis=0, concat_axis=0, tiled=True, a...  15.2 us
    all_to_all x1, starting transfers between devices, layer(): lax.all_to_all(partial, 'tensor', split_axis=0, concat_axis=0, tiled=True...  11 us
    all_to_all x1, starting transfers between devices, body(): lax.all_to_all(outgoing.reshape(RPS, MAXLEN, FS), 'dp', split_axis=0, con...  10.2 us
    ppermute x4, starting transfers between devices, layer(): pieces = [lax.ppermute(keyval, 'tensor', kv_round(i)) for i in range(4)]  9.61 us
    unnamed x27, local copies, waits for them, and re-layouts  9.49 us
    all_to_all x1, waiting for transfers between devices, body(): lax.all_to_all(outgoing.reshape(RPS, MAXLEN, FS), 'dp', split_axis=0, con...  9.45 us
  transfers between devices with their start and end apart: 10, of which 5 were waited for; matrix products, arithmetic and copies ran while one was open for 5% of the time, Pallas kernels for 5%

profile of v1, /device:TPU:8, one launch (start us, length us, event | category | flops | bytes accessed | tf_op | source)
XLA Modules:
  0.0 219.1 jit_solution(15078436938881279696)
XLA Ops:
  1.7 15.2 %all-to-all-start = ((bf16[12,88,256]{2,1,0:T(8,128)(2,1)}), bf16[12,88,256]{2,1,0:T(8,128)(2,1)S(1)}, u32[]{:S(2)}, u32[]{:S(2)}) async-start(bf16[12,88,256]{2,1,0:T(8,128)(2,1)} %broadcast_in_dim.134), calls=%async_computation | async-start | bytes 1081344 | tf_op jit(solution)/shard_map/all_to_all | solution.py:203
  16.9 45.6 %all-gather = bf16[2016,256]{1,0:T(8,128)(2,1)} all-gather(bf16[168,256]{1,0:T(8,128)(2,1)S(1)} %slice-done), channel_id=2, replica_groups={{0,2,4,6,8,10,12,14,16,18,20,22},{1,3,5,7,9,11,13,15,17,19,21,23},{24,2..., dimensions={0}, use_global_device_ids=true | all-gather | bytes 1118208 | tf_op jit(solution)/shard_map/all_gather | solution.py:206
  63.3 2.8 %pad_maximum_fusion.mine = bf16[12,256,256]{2,1,0:T(8,128)(2,1)} fusion(bf16[12,88,256]{2,1,0:T(8,128)(2,1)} %copy-done.7, bf16[12,168,256]{2,1,0:T(8,128)(2,1)} %bitcast.44), kind=kLoop, calls=%fused_computation.1 | loop fusion | flops 3145728 | bytes 3145728 | tf_op jit(solution)/shard_map/concatenate | solution.py:209
  66.1 1.9 collective-permute-start
  68.1 2.8 %copy.15 = bf16[256,6144]{0,1:T(8,128)(2,1)} copy(bf16[256,6144]{1,0:T(8,128)(2,1)S(1)} %copy-done) | data formatting | bytes 6291456 | tf_op args[6]
  70.9 2.7 %constant_dynamic-slice_fusion.1 = bf16[256,12,1,256]{0,3,2,1:T(8,128)(2,1)} fusion(bf16[256,12,2,256]{0,3,2,1:T(8,128)(2,1)} %bitcast.42, s32[]{:T(128)S(6)} %select_n.132), kind=kLoop, calls=%fused_computation.57 | loop fusion | bytes 3145732 | tf_op jit(solution)/shard_map/jit(dynamic_index_in_dim)/dynamic_slice | solution.py:219
  73.5 2.6 %copy.16 = bf16[256,3072]{1,0:T(8,128)(2,1)} copy(bf16[256,3072]{0,1:T(8,128)(2,1)} %bitcast.43) | data formatting | bytes 3145728 | tf_op jit(solution)/shard_map/reshape | solution.py:219
  76.2 2.4 %collective-permute-start.6 = (bf16[256,3072]{1,0:T(8,128)(2,1)}, bf16[256,3072]{1,0:T(8,128)(2,1)}, u32[]{:S(2)}, u32[]{:S(2)}) collective-permute-start(bf16[256,3072]{1,0:T(8,128)(2,1)} %copy.16), channel_id=1, source_target_pairs={{0,1},{1,0},{2,3},{3,2},{4,5},{5,4},{6,7},{7,6},{8,9},{9,8},{10,11... | collective-permute-start | bytes 4718600 | tf_op jit(solution)/shard_map/ppermute | solution.py:38
  80.5 1.9 copy-done.1
  83.5 9.0 %project.1 = (f32[256,256]{1,0:T(8,128)S(1)}, bf16[256,64]{1,0:T(8,128)(2,1)}) custom-call(s32[1]{0:T(128)} %bitcast.3.core, bf16[12,256,256]{2,1,0:T(8,128)(2,1)} %pad_maximum_fusion.mine, bf16[12,256,256]{2,1,0:T(8,128)(2,1)} %collective-permute-done.theirs, f32[24,1,256]{2,1,0:T(1,128)S(1)} %bitcast.38, f32[24,1,256]{2,1,0:T(1,128)S(1)} %bitcast.39, ...), custom_call_target="tpu_custom_call" | custom-call | flops 1006632960 | bytes 7077888 | tf_op jit(solution)/shard_map/project/pallas_call | solution.py:78
  93.2 3.1 %collective-permute-start.4 = (bf16[256,64]{1,0:T(8,128)(2,1)}, bf16[256,64]{1,0:T(8,128)(2,1)}, u32[]{:S(2)}, u32[]{:S(2)}) collective-permute-start(bf16[256,64]{1,0:T(8,128)(2,1)} %get-tuple-element.8), channel_id=1, source_target_pairs={{0,3},{1,0},{2,7},{3,4},{4,11},{5,8},{6,15},{7,12},{8,19},{9,16},{... | collective-permute-start | bytes 98312 | tf_op jit(solution)/shard_map/ppermute | solution.py:225
  96.3 2.5 %collective-permute-start.3 = (bf16[256,64]{1,0:T(8,128)(2,1)}, bf16[256,64]{1,0:T(8,128)(2,1)}, u32[]{:S(2)}, u32[]{:S(2)}) collective-permute-start(bf16[256,64]{1,0:T(8,128)(2,1)} %get-tuple-element.8), channel_id=1, source_target_pairs={{0,2},{1,3},{2,6},{3,7},{4,10},{5,11},{6,14},{7,15},{8,18},{9,19},... | collective-permute-start | bytes 98312 | tf_op jit(solution)/shard_map/ppermute | solution.py:225
  98.8 1.9 collective-permute-start.2
  100.7 2.1 collective-permute-start.1
  103.6 6.3 %collective-permute-done.3.r2 = bf16[256,64]{1,0:T(8,128)(2,1)} collective-permute-done((bf16[256,64]{1,0:T(8,128)(2,1)}, bf16[256,64]{1,0:T(8,128)(2,1)}, u32[]{:S(2)}, u32[]{:S(2)}) %collective-permute-start.3) | collective-permute-done | bytes 32800 | tf_op jit(solution)/shard_map/ppermute | solution.py:225
  109.9 3.0 %collective-permute-done.2.r1 = bf16[256,64]{1,0:T(8,128)(2,1)} collective-permute-done((bf16[256,64]{1,0:T(8,128)(2,1)}, bf16[256,64]{1,0:T(8,128)(2,1)}, u32[]{:S(2)}, u32[]{:S(2)}) %collective-permute-start.2) | collective-permute-done | bytes 32800 | tf_op jit(solution)/shard_map/ppermute | solution.py:225
  113.9 2.2 attend.1.mine
  116.0 1.9 collective-permute-start.5
  118.0 1.3 collective-permute-done.5.theirs
  119.3 7.3 %out_project.1 = bf16[12,256,256]{2,1,0:T(8,128)(2,1)S(1)} custom-call(s32[1]{0:T(128)} %bitcast.3.core, bf16[256,256]{1,0:T(8,128)(2,1)S(1)} %attend.1.mine, bf16[256,256]{1,0:T(8,128)(2,1)S(1)} %collective-permute-done.5.theirs, bf16[256,6144]{1,0:T(8,128)(2,1)S(1)} %copy-done, bf16[256,3072]{1,0:T(8,128)(2,1)} %collective-permute-done.6.w_theirs), custom_call_target="tpu_custom_call" | custom-call | flops 805306368 | bytes 9437184 | tf_op jit(solution)/shard_map/out_project/pallas_call | solution.py:175
  127.8 11.0 %all-to-all-start.1 = ((bf16[12,256,256]{2,1,0:T(8,128)(2,1)}), bf16[12,256,256]{2,1,0:T(8,128)(2,1)S(1)}, u32[]{:S(2)}, u32[]{:S(2)}) async-start(bf16[12,256,256]{2,1,0:T(8,128)(2,1)} %copy-done.2), calls=%async_computation.1 | async-start | bytes 3145728 | tf_op jit(solution)/shard_map/all_to_all | solution.py:241
  140.0 57.3 %all-to-all-done.1 = bf16[12,256,256]{2,1,0:T(8,128)(2,1)S(1)} async-done(((bf16[12,256,256]{2,1,0:T(8,128)(2,1)}), bf16[12,256,256]{2,1,0:T(8,128)(2,1)S(1)}, u32[]{:S(2)}, u32[]{:S(2)}) %all-to-all-start.1) | async-done | bytes 1572896 | tf_op jit(solution)/shard_map/all_to_all | solution.py:241
  198.5 10.2 %all-to-all-start.2 = ((bf16[32,8,256]{2,1,0:T(8,128)(2,1)}), bf16[32,8,256]{2,1,0:T(8,128)(2,1)S(1)}, u32[]{:S(2)}, u32[]{:S(2)}) async-start(bf16[32,8,256]{2,1,0:T(8,128)(2,1)} %fusion), calls=%async_computation.2 | async-start | bytes 262144 | tf_op jit(solution)/shard_map/all_to_all | solution.py:265
  208.8 9.4 %all-to-all-done.2 = bf16[32,8,256]{2,1,0:T(8,128)(2,1)S(1)} async-done(((bf16[32,8,256]{2,1,0:T(8,128)(2,1)}), bf16[32,8,256]{2,1,0:T(8,128)(2,1)S(1)}, u32[]{:S(2)}, u32[]{:S(2)}) %all-to-all-start.2) | async-done | bytes 131104 | tf_op jit(solution)/shard_map/all_to_all | solution.py:265
  (62 shorter events, 12.3 us)
Async XLA Ops:
  0.0 16.9 %slice-start = ((bf16[256,256]{1,0:T(8,128)(2,1)}), bf16[168,256]{1,0:T(8,128)(2,1)S(1)}, s32[]{:S(2)}) async-start(bf16[256,256]{1,0:T(8,128)(2,1)} %param.7), calls=%async_computation.3 | async-start | bytes 172032 | tf_op jit(solution)/shard_map/slice | solution.py:206
  1.7 60.8 %all-to-all-start = ((bf16[12,88,256]{2,1,0:T(8,128)(2,1)}), bf16[12,88,256]{2,1,0:T(8,128)(2,1)S(1)}, u32[]{:S(2)}, u32[]{:S(2)}) async-start(bf16[12,88,256]{2,1,0:T(8,128)(2,1)} %broadcast_in_dim.134), calls=%async_computation | async-start | bytes 1081344 | tf_op jit(solution)/shard_map/all_to_all | solution.py:203
  62.5 0.8 copy-start.7
  63.3 4.7 %copy-start = (bf16[256,6144]{1,0:T(8,128)(2,1)S(1)}, bf16[256,6144]{1,0:T(8,128)(2,1)}, u32[]{:S(2)}) copy-start(bf16[256,6144]{1,0:T(8,128)(2,1)} %w_mine.1) | copy-start | bytes 9437188
  66.1 14.3 %collective-permute-start = (bf16[12,256,256]{2,1,0:T(8,128)(2,1)}, bf16[12,256,256]{2,1,0:T(8,128)(2,1)}, u32[]{:S(2)}, u32[]{:S(2)}) collective-permute-start(bf16[12,256,256]{2,1,0:T(8,128)(2,1)} %pad_maximum_fusion.mine), channel_id=1, source_target_pairs={{0,1},{1,0},{2,3},{3,2},{4,5},{5,4},{6,7},{7,6},{8,9},{9,8},{10,11... | collective-permute-start | bytes 4718600 | tf_op jit(solution)/shard_map/ppermute | solution.py:38
  73.5 5.0 %copy-start.12 = (s32[1024]{0:T(1024)S(1)}, s32[1024]{0:T(1024)}, u32[]{:S(2)}) copy-start(s32[1024]{0:T(1024)} %param.9) | copy-start | bytes 12292
  73.5 6.9 %copy-start.6 = (f32[6144]{0:T(1024)S(1)}, f32[6144]{0:T(1024)}, u32[]{:S(2)}) copy-start(f32[6144]{0:T(1024)} %param.10) | copy-start | bytes 73732
  76.2 41.8 %collective-permute-start.6 = (bf16[256,3072]{1,0:T(8,128)(2,1)}, bf16[256,3072]{1,0:T(8,128)(2,1)}, u32[]{:S(2)}, u32[]{:S(2)}) collective-permute-start(bf16[256,3072]{1,0:T(8,128)(2,1)} %copy.16), channel_id=1, source_target_pairs={{0,1},{1,0},{2,3},{3,2},{4,5},{5,4},{6,7},{7,6},{8,9},{9,8},{10,11... | collective-permute-start | bytes 4718600 | tf_op jit(solution)/shard_map/ppermute | solution.py:38
  78.6 13.9 %copy-start.9 = (s32[32,32]{1,0:T(8,128)}, s32[32,32]{1,0:T(8,128)S(1)}, u32[]{:S(2)}) copy-start(s32[32,32]{1,0:T(8,128)S(1)} %reshape.158) | copy-start | bytes 12292
  80.5 1.9 copy-start.1
  82.4 1.1 copy-start.3
  92.5 0.7 copy-start.4
  93.2 10.3 %collective-permute-start.4 = (bf16[256,64]{1,0:T(8,128)(2,1)}, bf16[256,64]{1,0:T(8,128)(2,1)}, u32[]{:S(2)}, u32[]{:S(2)}) collective-permute-start(bf16[256,64]{1,0:T(8,128)(2,1)} %get-tuple-element.8), channel_id=1, source_target_pairs={{0,3},{1,0},{2,7},{3,4},{4,11},{5,8},{6,15},{7,12},{8,19},{9,16},{... | collective-permute-start | bytes 98312 | tf_op jit(solution)/shard_map/ppermute | solution.py:225
  96.3 13.6 %collective-permute-start.3 = (bf16[256,64]{1,0:T(8,128)(2,1)}, bf16[256,64]{1,0:T(8,128)(2,1)}, u32[]{:S(2)}, u32[]{:S(2)}) collective-permute-start(bf16[256,64]{1,0:T(8,128)(2,1)} %get-tuple-element.8), channel_id=1, source_target_pairs={{0,2},{1,3},{2,6},{3,7},{4,10},{5,11},{6,14},{7,15},{8,18},{9,19},... | collective-permute-start | bytes 98312 | tf_op jit(solution)/shard_map/ppermute | solution.py:225
  98.8 14.1 %collective-permute-start.2 = (bf16[256,64]{1,0:T(8,128)(2,1)}, bf16[256,64]{1,0:T(8,128)(2,1)}, u32[]{:S(2)}, u32[]{:S(2)}) collective-permute-start(bf16[256,64]{1,0:T(8,128)(2,1)} %get-tuple-element.8), channel_id=1, source_target_pairs={{0,1},{1,2},{2,5},{3,6},{4,9},{5,10},{6,13},{7,14},{8,17},{9,18},{... | collective-permute-start | bytes 98312 | tf_op jit(solution)/shard_map/ppermute | solution.py:225
  100.7 12.2 %collective-permute-start.1 = (bf16[256,64]{1,0:T(8,128)(2,1)}, bf16[256,64]{1,0:T(8,128)(2,1)}, u32[]{:S(2)}, u32[]{:S(2)}) collective-permute-start(bf16[256,64]{1,0:T(8,128)(2,1)} %get-tuple-element.8), channel_id=1, source_target_pairs={{0,0},{1,1},{2,4},{3,5},{4,8},{5,9},{6,12},{7,13},{8,16},{9,17},{1... | collective-permute-start | bytes 98312 | tf_op jit(solution)/shard_map/ppermute | solution.py:225
  112.9 1.0 copy-start.5
  116.0 3.2 %collective-permute-start.5 = (bf16[256,256]{1,0:T(8,128)(2,1)S(1)}, bf16[256,256]{1,0:T(8,128)(2,1)S(1)}, u32[]{:S(2)}, u32[]{:S(2)}) collective-permute-start(bf16[256,256]{1,0:T(8,128)(2,1)S(1)} %attend.1.mine), channel_id=1, source_target_pairs={{0,1},{1,0},{2,3},{3,2},{4,5},{5,4},{6,7},{7,6},{8,9},{9,8},{10,11... | collective-permute-start | bytes 393224 | tf_op jit(solution)/shard_map/ppermute | solution.py:38
  126.6 1.2 copy-start.2
  127.8 11.0 %copy-start.10 = (s32[32,32]{1,0:T(8,128)S(1)}, s32[32,32]{1,0:T(8,128)}, u32[]{:S(2)}) copy-start(s32[32,32]{1,0:T(8,128)} %copy-done.9) | copy-start | bytes 12292
  127.8 11.1 %copy-start.11 = (s32[32,32]{1,0:T(8,128)S(1)}, s32[32,32]{1,0:T(8,128)}, u32[]{:S(2)}) copy-start(s32[32,32]{1,0:T(8,128)} %param.8) | copy-start | bytes 12292
  127.8 69.6 %all-to-all-start.1 = ((bf16[12,256,256]{2,1,0:T(8,128)(2,1)}), bf16[12,256,256]{2,1,0:T(8,128)(2,1)S(1)}, u32[]{:S(2)}, u32[]{:S(2)}) async-start(bf16[12,256,256]{2,1,0:T(8,128)(2,1)} %copy-done.2), calls=%async_computation.1 | async-start | bytes 3145728 | tf_op jit(solution)/shard_map/all_to_all | solution.py:241
  138.8 58.8 %copy-start.8 = (bf16[256,256]{1,0:T(8,128)(2,1)S(1)}, bf16[256,256]{1,0:T(8,128)(2,1)}, u32[]{:S(2)}) copy-start(bf16[256,256]{1,0:T(8,128)(2,1)} %param.7) | copy-start | bytes 393220
  198.5 19.7 %all-to-all-start.2 = ((bf16[32,8,256]{2,1,0:T(8,128)(2,1)}), bf16[32,8,256]{2,1,0:T(8,128)(2,1)S(1)}, u32[]{:S(2)}, u32[]{:S(2)}) async-start(bf16[32,8,256]{2,1,0:T(8,128)(2,1)} %fusion), calls=%async_computation.2 | async-start | bytes 262144 | tf_op jit(solution)/shard_map/all_to_all | solution.py:265

commit v2 on v1

v2 whole, which is shorter than its diff:
```python
import functools
import math

import jax
import jax.numpy as jnp
from jax import lax
from jax.experimental import pallas as pl
from jax.experimental.pallas import tpu as pltpu
from jax.sharding import PartitionSpec as P

D = 6144
HD = 128
MAXLEN = 8
NZ = 12
NT = 24
FS = 256
RPS = 32
KVS = 64
EPS = 1e-05
ROPE_BASE = 500000.0
AG_ROWS = 168
VMEM = 40 * 1024 * 1024

Z_GROUPS = [[z * 2 + c for z in range(NZ)] for c in range(2)]
SWAP = [(t, t ^ 1) for t in range(NT)]


STEPS = 3
PER = NZ // STEPS
CAPS = (168, 176, 192, 256)


def kv_pairs(first):
    pairs = []
    for z in range(NZ):
        g, value = z % (NZ // 2), z // (NZ // 2)
        to = 2 * g + (value if first else 1 - value)
        pairs += [(2 * z + c, 2 * to + c) for c in range(2)]
    return pairs


def swap(v):
    return lax.ppermute(v, "tensor", SWAP)


def rows_of(refs, j, side):
    head, tail = refs
    x = head[j].astype(jnp.float32)
    if tail is not None:
        x = jnp.concatenate([x, tail[2 * j + side].astype(jnp.float32)], axis=0)
    return x


def kv_kernel(has_tail, core, mine, theirs, *rest):
    if has_tail:
        tail, *rest = rest
    else:
        tail = None
    gain, wk_m, wk_t, kv_out, inv_out, kv_acc, sq_acc = rest
    step = pl.program_id(0)
    c = core[0]

    @pl.when(step == 0)
    def _():
        kv_acc[...] = jnp.zeros_like(kv_acc)
        sq_acc[...] = jnp.zeros_like(sq_acc)

    total, squares = kv_acc[...], sq_acc[...]
    for j in range(PER):
        for x_ref, side in ((mine, c), (theirs, 1 - c)):
            x = rows_of((x_ref, tail), j, side)
            square = x * x
            squares += square[:, :128] + square[:, 128:]
            scaled = (x * gain[2 * j + side]).astype(jnp.bfloat16)
            at = pl.ds(pl.multiple_of((2 * j + side) * FS, FS), FS)
            w = jnp.concatenate([wk_m[:, at], wk_t[:, at]], axis=0)
            total += lax.dot_general(
                scaled, w, (((1,), (1,)), ((), ())), preferred_element_type=jnp.float32
            )
    kv_acc[...] = total
    sq_acc[...] = squares

    @pl.when(step == STEPS - 1)
    def _():
        inverse = lax.rsqrt(jnp.sum(squares, axis=1, keepdims=True) / D + EPS)
        out = total * inverse
        turned = jnp.concatenate([out[:, KVS:], out[:, :KVS]], axis=1)
        kv_out[...] = jnp.where(c == 0, out, turned).astype(jnp.bfloat16)
        inv_out[...] = jnp.broadcast_to(inverse, inv_out.shape)


def q_kernel(has_tail, core, mine, theirs, *rest):
    if has_tail:
        tail, *rest = rest
    else:
        tail = None
    gain, wq_m, wq_t, inv, q_out, q_acc = rest
    step = pl.program_id(0)
    c = core[0]

    @pl.when(step == 0)
    def _():
        q_acc[...] = jnp.zeros_like(q_acc)

    total = q_acc[...]
    for j in range(PER):
        for x_ref, wq, side in ((mine, wq_m, c), (theirs, wq_t, 1 - c)):
            x = rows_of((x_ref, tail), j, side)
            scaled = (x * gain[2 * j + side]).astype(jnp.bfloat16)
            total += jnp.dot(scaled, wq[j, 0], preferred_element_type=jnp.float32)
    q_acc[...] = total

    @pl.when(step == STEPS - 1)
    def _():
        for h in range(2):
            q_out[:, h * HD : (h + 1) * HD] = total[:, h * HD : (h + 1) * HD] * inv[...]


def x_specs(mine, tail):
    specs = [pl.BlockSpec((PER, mine.shape[1], FS), lambda i, c: (i, 0, 0))] * 2
    if tail is not None:
        specs.append(pl.BlockSpec((2 * PER, tail.shape[1], FS), lambda i, c: (i, 0, 0)))
    specs.append(pl.BlockSpec((2 * PER, 1, FS), lambda i, c: (i, 0, 0)))
    return specs


def project_kv(core, mine, theirs, tail, gain, wk_m, wk_t):
    rows = mine.shape[1] + (0 if tail is None else tail.shape[1])
    whole = pl.BlockSpec((rows, HD), lambda i, c: (0, 0))
    wk_spec = pl.BlockSpec((KVS, 2 * PER * FS), lambda i, c: (0, i))
    return pl.pallas_call(
        functools.partial(kv_kernel, tail is not None),
        grid_spec=pltpu.PrefetchScalarGridSpec(
            num_scalar_prefetch=1,
            grid=(STEPS,),
            in_specs=x_specs(mine, tail) + [wk_spec, wk_spec],
            out_specs=[whole, whole],
            scratch_shapes=[pltpu.VMEM((rows, HD), jnp.float32), pltpu.VMEM((rows, HD), jnp.float32)],
        ),
        out_shape=[
            jax.ShapeDtypeStruct((rows, HD), jnp.bfloat16),
            jax.ShapeDtypeStruct((rows, HD), jnp.float32),
        ],
        compiler_params=pltpu.CompilerParams(vmem_limit_bytes=VMEM),
        cost_estimate=pl.CostEstimate(
            flops=2 * rows * D * HD, bytes_accessed=2 * D * (rows + HD), transcendentals=rows
        ),
        name="project_kv",
    )(core, mine, theirs, *([] if tail is None else [tail]), gain, wk_m, wk_t)


def project_q(core, mine, theirs, tail, gain, wq, inverse):
    rows = inverse.shape[0]
    wq4 = wq.reshape(NZ, 2, FS, FS)
    return pl.pallas_call(
        functools.partial(q_kernel, tail is not None),
        grid_spec=pltpu.PrefetchScalarGridSpec(
            num_scalar_prefetch=1,
            grid=(STEPS,),
            in_specs=x_specs(mine, tail)
            + [
                pl.BlockSpec((PER, 1, FS, FS), lambda i, c: (i, c[0], 0, 0)),
                pl.BlockSpec((PER, 1, FS, FS), lambda i, c: (i, 1 - c[0], 0, 0)),
                pl.BlockSpec((rows, HD), lambda i, c: (0, 0)),
            ],
            out_specs=pl.BlockSpec((rows, FS), lambda i, c: (0, 0)),
            scratch_shapes=[pltpu.VMEM((rows, FS), jnp.float32)],
        ),
        out_shape=jax.ShapeDtypeStruct((rows, FS), jnp.float32),
        compiler_params=pltpu.CompilerParams(vmem_limit_bytes=VMEM),
        cost_estimate=pl.CostEstimate(
            flops=2 * rows * D * FS, bytes_accessed=2 * D * (rows + FS), transcendentals=0
        ),
        name="project_q",
    )(core, mine, theirs, *([] if tail is None else [tail]), gain, wq4, wq4, inverse)


def attention_kernel(odd, q_ref, first, second, cos_ref, sin_ref, col_ref, row_ref, out_ref):
    rows = q_ref.shape[0]
    one, two = first[...].astype(jnp.float32), second[...].astype(jnp.float32)
    swapped = odd[0] == 1
    keys = jnp.where(swapped, two, one)
    values = jnp.where(swapped, one, two).astype(jnp.bfloat16)
    cosine = cos_ref[...]
    sine = sin_ref[...]

    def turn(v):
        turned = jnp.concatenate([-v[:, HD // 2 :], v[:, : HD // 2]], axis=1)
        return (v * cosine + turned * sine).astype(jnp.bfloat16)

    k_rot = turn(keys)
    doc_q = col_ref[...]
    doc_k = row_ref[...]
    place_q = lax.broadcasted_iota(jnp.int32, (rows, rows), 0)
    place_k = lax.broadcasted_iota(jnp.int32, (rows, rows), 1)
    allowed = (doc_q == doc_k) & (place_k <= place_q)
    for h in range(2):
        q_rot = turn(q_ref[:, h * HD : (h + 1) * HD])
        scores = lax.dot_general(
            q_rot, k_rot, (((1,), (1,)), ((), ())), preferred_element_type=jnp.float32
        ) / math.sqrt(HD)
        masked = jnp.where(allowed, scores, -jnp.inf)
        exponent = jnp.exp(masked - jnp.max(masked, axis=1, keepdims=True))
        weights = (exponent / jnp.sum(exponent, axis=1, keepdims=True)).astype(jnp.bfloat16)
        context = jnp.dot(weights, values, preferred_element_type=jnp.float32)
        out_ref[:, h * HD : (h + 1) * HD] = context.astype(jnp.bfloat16)


def attend(odd, q, first, second, cosine, sine, doc):
    rows = q.shape[0]
    vm = pl.BlockSpec(memory_space=pltpu.VMEM)
    return pl.pallas_call(
        attention_kernel,
        in_specs=[pl.BlockSpec(memory_space=pltpu.SMEM)] + [vm] * 7,
        out_specs=vm,
        out_shape=jax.ShapeDtypeStruct((rows, FS), jnp.bfloat16),
        compiler_params=pltpu.CompilerParams(vmem_limit_bytes=VMEM),
        cost_estimate=pl.CostEstimate(
            flops=8 * rows * rows * HD, bytes_accessed=4 * rows * FS, transcendentals=2 * rows * rows
        ),
        name="attend",
    )(odd, q, first, second, cosine, sine, doc[:, None], doc[None, :])


def out_kernel(core, mine, theirs, *rest):
    w_mine, w_theirs, out_ref = rest[:PER], rest[PER : 2 * PER], rest[-1]
    for j in range(PER):
        total = jnp.dot(mine[...], w_mine[j][...], preferred_element_type=jnp.float32)
        total += jnp.dot(theirs[...], w_theirs[j][...], preferred_element_type=jnp.float32)
        out_ref[j] = total.astype(jnp.bfloat16)


def out_project(core, mine, theirs, w_mine, w_theirs):
    rows = mine.shape[0]
    context = pl.BlockSpec((rows, FS), lambda i, c: (0, 0))
    weights = [
        pl.BlockSpec((FS, FS), lambda i, c, j=j: (0, 2 * (PER * i + j) + c[0])) for j in range(PER)
    ]
    return pl.pallas_call(
        out_kernel,
        grid_spec=pltpu.PrefetchScalarGridSpec(
            num_scalar_prefetch=1,
            grid=(STEPS,),
            in_specs=[context, context] + weights + weights,
            out_specs=pl.BlockSpec((PER, rows, FS), lambda i, c: (i, 0, 0)),
        ),
        out_shape=jax.ShapeDtypeStruct((NZ, rows, FS), jnp.bfloat16),
        compiler_params=pltpu.CompilerParams(vmem_limit_bytes=VMEM),
        cost_estimate=pl.CostEstimate(
            flops=2 * rows * FS * D, bytes_accessed=D * (rows + 2 * FS), transcendentals=0
        ),
        name="out_project",
    )(core, mine, theirs, *[w_mine] * PER, *[w_theirs] * PER)


def gather_rows(x):
    rows = x.shape[0]
    tail = None
    if rows > AG_ROWS:
        last = jnp.broadcast_to(x[AG_ROWS:][None], (NT, rows - AG_ROWS, FS))
        tail = lax.all_to_all(last, "tensor", split_axis=0, concat_axis=0, tiled=True)
    return lax.all_gather(x[:AG_ROWS], "tensor", axis=0, axis_index_groups=Z_GROUPS), tail


def layer(rows, rollout, lengths, packing, norm_gain, query_weight, keyval_weight, out_weight):
    source = lax.axis_index("dp")
    tensor_index = lax.axis_index("tensor")
    core = (tensor_index % 2).astype(jnp.int32).reshape(1)
    x = rollout[:rows]

    mine, tail = gather_rows(x)
    theirs = swap(mine)
    gain = norm_gain.reshape(NT, 1, FS)
    wk = keyval_weight.T
    keyval, inverse = project_kv(core, mine, theirs, tail, gain, wk, swap(wk))
    first = lax.ppermute(keyval, "tensor", kv_pairs(True))
    second = lax.ppermute(keyval, "tensor", kv_pairs(False))
    q = project_q(core, mine, theirs, tail, gain, query_weight, inverse)

    my_len = lax.dynamic_index_in_dim(lengths, source, 0, keepdims=False)
    earlier = jnp.arange(RPS)[None, :] < jnp.arange(RPS)[:, None]
    start = jnp.sum(jnp.where(earlier, my_len[None, :], 0), axis=1)
    places = jnp.arange(rows, dtype=jnp.int32)
    doc = jnp.sum((places[:, None] >= (start + my_len)[None, :]).astype(jnp.int32), axis=1)
    begun = jnp.max(jnp.where(start[None, :] <= places[:, None], start[None, :], 0), axis=1)
    position = jnp.where(doc < RPS, places - begun, 0)
    frequency = ROPE_BASE ** (-jnp.arange(HD // 2, dtype=jnp.float32) * 2.0 / HD)
    angles = position.astype(jnp.float32)[:, None] * jnp.concatenate([frequency, frequency])[None, :]
    odd = (tensor_index // 2 % 2).astype(jnp.int32).reshape(1)
    context = attend(odd, q, first, second, jnp.cos(angles), jnp.sin(angles), doc)
    partial = out_project(core, context, swap(context), out_weight, swap(out_weight))
    parts = lax.all_to_all(
        partial, "tensor", split_axis=0, concat_axis=0, tiled=True, axis_index_groups=Z_GROUPS
    )
    result = (jnp.sum(parts.astype(jnp.float32), axis=0) + x.astype(jnp.float32)).astype(jnp.bfloat16)

    pack = packing.reshape(RPS, RPS)
    of_mine = pack // RPS == source
    which = jnp.sum(jnp.where(of_mine, pack % RPS, 0), axis=1)
    chosen = which[:, None] == jnp.arange(RPS)[None, :]
    o_start = jnp.sum(jnp.where(chosen, start[None, :], 0), axis=1)
    o_len = jnp.sum(jnp.where(chosen, my_len[None, :], 0), axis=1)
    slot = jnp.arange(MAXLEN, dtype=jnp.int32)
    row_of = jnp.where(slot[None, :] < o_len[:, None], o_start[:, None] + slot[None, :], -1).reshape(-1)
    pick = (row_of[:, None] == places[None, :]).astype(jnp.bfloat16)
    outgoing = jnp.dot(pick, result, preferred_element_type=jnp.float32).astype(jnp.bfloat16)
    return outgoing


def body(rollout, lengths, packing, norm_gain, query_weight, keyval_weight, out_weight):
    owner = lax.axis_index("dp")
    total = rollout.shape[0]
    longest = jnp.max(jnp.sum(lengths, axis=1))
    size = sum((longest > cap).astype(jnp.int32) for cap in CAPS[:-1])
    outgoing = lax.switch(
        size,
        [functools.partial(layer, cap) for cap in CAPS],
        rollout, lengths, packing, norm_gain, query_weight, keyval_weight, out_weight,
    )
    incoming = lax.all_to_all(
        outgoing.reshape(RPS, MAXLEN, FS), "dp", split_axis=0, concat_axis=0, tiled=True
    ).reshape(RPS * MAXLEN, FS)

    chosen = lax.dynamic_index_in_dim(packing.reshape(RPS, RPS), owner, 0, keepdims=False)
    from_source = chosen // RPS
    is_source = from_source[:, None] == jnp.arange(RPS)[None, :]
    of_source = jnp.sum(jnp.where(is_source[:, :, None], lengths[None], 0), axis=1)
    is_k = (chosen % RPS)[:, None] == jnp.arange(RPS)[None, :]
    length = jnp.sum(jnp.where(is_k, of_source, 0), axis=1)
    earlier = jnp.arange(RPS)[None, :] < jnp.arange(RPS)[:, None]
    start = jnp.sum(jnp.where(earlier, length[None, :], 0), axis=1)
    places = jnp.arange(total, dtype=jnp.int32)
    inside = (places[:, None] >= start[None, :]) & (places[:, None] < (start + length)[None, :])
    valid = jnp.any(inside, axis=1)
    at = jnp.sum(jnp.where(inside, from_source[None, :] * MAXLEN + places[:, None] - start[None, :], 0), axis=1)
    at = jnp.where(valid, at, -1)
    pick = (at[:, None] == jnp.arange(RPS * MAXLEN)[None, :]).astype(jnp.bfloat16)
    return jnp.dot(pick, incoming, preferred_element_type=jnp.float32).astype(jnp.bfloat16)


def solution(mesh):
    in_specs = (
        P("dp", "tensor"),
        P(),
        P(),
        P(),
        P(None, "tensor"),
        P(None, "tensor"),
        P("tensor", None),
    )
    out_specs = P("dp", "tensor")
    return jax.shard_map(body, mesh=mesh, in_specs=in_specs, out_specs=out_specs, check_vma=False)
```

time: 220 us -> 161 us (0.73)
  the two profiles are of different devices: /device:TPU:8 before, /device:TPU:64 now
where the time goes in v2:
time: 161 us; the launch traced here: 160 us
  waiting for transfers between devices  56.7 us (35%)
  starting transfers between devices  41.3 us (26%)
  blocking collectives  37 us (23%)
  Pallas kernels  9.41 us (6%)
  other arithmetic  6.49 us (4%)
  local copies, waits for them, and re-layouts  4.98 us (3%)
  between operations  2 us (1%)
  matrix products  1.78 us (1%)
    all_to_all x1, waiting for transfers between devices, layer(): lax.all_to_all(partial, 'tensor', split_axis=0, concat_axis=0, tiled=True...  41.9 us
    all_gather x1, blocking collectives, gather_rows(): lax.all_gather(x[:AG_ROWS], 'tensor', axis=0, axis_index_groups=Z_GROUPS)  37 us
    all_to_all x1, starting transfers between devices, body(): lax.all_to_all(outgoing.reshape(RPS, MAXLEN, FS), 'dp', split_axis=0, con...  9.95 us
    all_to_all x1, starting transfers between devices, layer(): lax.all_to_all(partial, 'tensor', split_axis=0, concat_axis=0, tiled=True...  9.07 us
    all_to_all x1, waiting for transfers between devices, body(): lax.all_to_all(outgoing.reshape(RPS, MAXLEN, FS), 'dp', split_axis=0, con...  8.14 us
    ppermute x4, starting transfers between devices, swap(): return lax.ppermute(v, 'tensor', SWAP)  7.81 us
    all_to_all x1, starting transfers between devices, gather_rows(): lax.all_to_all(last, 'tensor', split_axis=0, concat_axis=0, tiled=True)  7.1 us
    ppermute x1, starting transfers between devices, layer(): first = lax.ppermute(keyval, 'tensor', kv_pairs(True))  3.82 us
  transfers between devices with their start and end apart: 9, of which 5 were waited for; matrix products, arithmetic and copies ran while one was open for 6% of the time, Pallas kernels for 5%

profile of v2, /device:TPU:64, one launch (start us, length us, event | category | flops | bytes accessed | tf_op | source)
XLA Modules:
  0.0 159.9 jit_solution(1322634909367193676)
XLA Ops:
  3.4 135.1 %conditional.2 = (bf16[256,256]{1,0:T(8,128)(2,1)}) conditional(s32[]{:T(128)} %clamp.3, (s32[1024]{0:T(1024)}, s32[32,32]{1,0:T(8,128)}, bf16[256,256]{1,0:T(8,128)(2,1)}, f32[6144]{0:T(1024)}, bf16[6144,256]{1,0:T(8,128)(2,1)}, /*index=5*/bf16[6144,64]{0,1:T(8,128)(2,1)}, bf16[256,6144]{1,0:T(8,128)(2,1)}) %tuple.22, ...), branch_computations={%region_7.15_spmd, %region_15.23_spmd, %region_23.31_spmd, %region... | conditional | flops 2115812864 | bytes 82637312
  3.5 1.9 %collective-permute-start.11 = (bf16[256,6144]{1,0:T(8,128)(2,1)}, bf16[256,6144]{1,0:T(8,128)(2,1)S(1)}, u32[]{:S(2)}, u32[]{:S(2)}) collective-permute-start(bf16[256,6144]{1,0:T(8,128)(2,1)} %get-tuple-element.85.rest_0_.rest_1_.rest_2_.rest_3_), channel_id=1, source_target_pairs={{0,1},{1,0},{2,3},{3,2},{4,5},{5,4},{6,7},{7,6},{8,9},{9,8},{10,11... | collective-permute-start | bytes 9437192 | tf_op jit(solution)/shard_map/cond/branch_1_fun/ppermute | solution.py:43
  5.4 0.9 slice.23
  6.3 37.0 %all-gather.1 = bf16[2016,256]{1,0:T(8,128)(2,1)} all-gather(bf16[168,256]{1,0:T(8,128)(2,1)S(1)} %slice.23), channel_id=3, replica_groups={{0,2,4,6,8,10,12,14,16,18,20,22},{1,3,5,7,9,11,13,15,17,19,21,23},{24,2..., dimensions={0}, use_global_device_ids=true | all-gather | bytes 1118208 | tf_op jit(solution)/shard_map/cond/branch_1_fun/all_gather | solution.py:262
  43.3 1.9 %collective-permute-start.6 = (bf16[12,168,256]{2,1,0:T(8,128)(2,1)}, bf16[12,168,256]{2,1,0:T(8,128)(2,1)}, u32[]{:S(2)}, u32[]{:S(2)}) collective-permute-start(bf16[12,168,256]{2,1,0:T(8,128)(2,1)} %bitcast.14.mine), channel_id=1, source_target_pairs={{0,1},{1,0},{2,3},{3,2},{4,5},{5,4},{6,7},{7,6},{8,9},{9,8},{10,11... | collective-permute-start | bytes 3096584 | tf_op jit(solution)/shard_map/cond/branch_1_fun/ppermute | solution.py:43
  46.5 7.1 %all-to-all-start.1 = ((bf16[24,8,256]{2,1,0:T(8,128)(2,1)}), bf16[24,8,256]{2,1,0:T(8,128)(2,1)S(1)}, u32[]{:S(2)}, u32[]{:S(2)}) async-start(bf16[24,8,256]{2,1,0:T(8,128)(2,1)} %broadcast_in_dim.268), calls=%async_computation.1 | async-start | bytes 196608 | tf_op jit(solution)/shard_map/cond/branch_1_fun/all_to_all | solution.py:261
  53.6 2.1 %collective-permute-start.7 = (bf16[64,6144]{1,0:T(8,128)(2,1)}, bf16[64,6144]{1,0:T(8,128)(2,1)}, u32[]{:S(2)}, u32[]{:S(2)}) collective-permute-start(bf16[64,6144]{1,0:T(8,128)(2,1)} %bitcast.102), channel_id=1, source_target_pairs={{0,1},{1,0},{2,3},{3,2},{4,5},{5,4},{6,7},{7,6},{8,9},{9,8},{10,11... | collective-permute-start | bytes 2359304 | tf_op jit(solution)/shard_map/cond/branch_1_fun/ppermute | solution.py:43
  58.7 1.0 multiply_sine_fusion.1
  59.7 3.4 %all-to-all-done.1.rest_0_ = bf16[24,8,256]{2,1,0:T(8,128)(2,1)S(1)} async-done(((bf16[24,8,256]{2,1,0:T(8,128)(2,1)}), bf16[24,8,256]{2,1,0:T(8,128)(2,1)S(1)}, u32[]{:S(2)}, u32[]{:S(2)}) %all-to-all-start.1) | async-done | bytes 98336 | tf_op jit(solution)/shard_map/cond/branch_1_fun/all_to_all | solution.py:261
  63.1 3.6 %project_kv.5 = (bf16[176,128]{1,0:T(8,128)(2,1)S(1)}, f32[176,128]{1,0:T(8,128)S(1)}) custom-call(s32[1]{0:T(128)} %bitcast.12.core, bf16[12,168,256]{2,1,0:T(8,128)(2,1)} %bitcast.14.mine, bf16[12,168,256]{2,1,0:T(8,128)(2,1)} %collective-permute-done.6.theirs, bf16[24,8,256]{2,1,0:T(8,128)(2,1)S(1)} %all-to-all-done.1.rest_0_, ...), custom_call_target="tpu_custom_call" | custom-call | flops 276824064 | bytes 3735552 | tf_op jit(solution)/shard_map/cond/branch_1_fun/project_kv/pallas_call | solution.py:131
  66.7 3.8 %collective-permute-start.8 = (bf16[176,128]{1,0:T(8,128)(2,1)S(1)}, bf16[176,128]{1,0:T(8,128)(2,1)S(1)}, u32[]{:S(2)}, u32[]{:S(2)}) collective-permute-start(bf16[176,128]{1,0:T(8,128)(2,1)S(1)} %get-tuple-element.84), channel_id=1, source_target_pairs={{0,0},{1,1},{2,4},{3,5},{4,8},{5,9},{6,12},{7,13},{8,16},{9,17},{1... | collective-permute-start | bytes 135176 | tf_op jit(solution)/shard_map/cond/branch_1_fun/ppermute | solution.py:276
  70.5 3.6 %collective-permute-start.9 = (bf16[176,128]{1,0:T(8,128)(2,1)S(1)}, bf16[176,128]{1,0:T(8,128)(2,1)S(1)}, u32[]{:S(2)}, u32[]{:S(2)}) collective-permute-start(bf16[176,128]{1,0:T(8,128)(2,1)S(1)} %get-tuple-element.84), channel_id=1, source_target_pairs={{0,2},{1,3},{2,6},{3,7},{4,10},{5,11},{6,14},{7,15},{8,18},{9,19},... | collective-permute-start | bytes 135176 | tf_op jit(solution)/shard_map/cond/branch_1_fun/ppermute | solution.py:277
  74.1 3.1 %project_q.5.q_ref = f32[176,256]{1,0:T(8,128)S(1)} custom-call(s32[1]{0:T(128)} %bitcast.12.core, bf16[12,168,256]{2,1,0:T(8,128)(2,1)} %bitcast.14.mine, bf16[12,168,256]{2,1,0:T(8,128)(2,1)} %collective-permute-done.6.theirs, bf16[24,8,256]{2,1,0:T(8,128)(2,1)S(1)} %all-to-all-done.1.rest_0_, f32[24,1,256]{2,1,0:T(1,128)S(1)} %bitcast.111, ...), custom_call_target="tpu_custom_call" | custom-call | flops 553648128 | bytes 5308416 | tf_op jit(solution)/shard_map/cond/branch_1_fun/project_q/pallas_call | solution.py:155
  77.2 2.0 %collective-permute-done.8.first = bf16[176,128]{1,0:T(8,128)(2,1)S(1)} collective-permute-done((bf16[176,128]{1,0:T(8,128)(2,1)S(1)}, bf16[176,128]{1,0:T(8,128)(2,1)S(1)}, u32[]{:S(2)}, u32[]{:S(2)}) %collective-permute-start.8) | collective-permute-done | bytes 45088 | tf_op jit(solution)/shard_map/cond/branch_1_fun/ppermute | solution.py:276
  79.2 1.0 attend.5.mine
  80.2 1.9 %collective-permute-start.10 = (bf16[176,256]{1,0:T(8,128)(2,1)S(1)}, bf16[176,256]{1,0:T(8,128)(2,1)S(1)}, u32[]{:S(2)}, u32[]{:S(2)}) collective-permute-start(bf16[176,256]{1,0:T(8,128)(2,1)S(1)} %attend.5.mine), channel_id=1, source_target_pairs={{0,1},{1,0},{2,3},{3,2},{4,5},{5,4},{6,7},{7,6},{8,9},{9,8},{10,11... | collective-permute-start | bytes 270344 | tf_op jit(solution)/shard_map/cond/branch_1_fun/ppermute | solution.py:43
  82.1 1.3 collective-permute-done.10.theirs
  83.4 1.8 %out_project.5 = bf16[12,176,256]{2,1,0:T(8,128)(2,1)S(1)} custom-call(s32[1]{0:T(128)} %bitcast.12.core, bf16[176,256]{1,0:T(8,128)(2,1)S(1)} %attend.5.mine, bf16[176,256]{1,0:T(8,128)(2,1)S(1)} %collective-permute-done.10.theirs, bf16[256,6144]{1,0:T(8,128)(2,1)S(1)} %copy-done.7, bf16[256,6144]{1,0:T(8,128)(2,1)S(1)} %copy-done.7, ...), custom_call_target="tpu_custom_call" | custom-call | flops 553648128 | bytes 4227072 | tf_op jit(solution)/shard_map/cond/branch_1_fun/out_project/pallas_call | solution.py:239
  85.1 1.0 copy-done.2
  86.1 9.1 %all-to-all-start.2 = ((bf16[12,176,256]{2,1,0:T(8,128)(2,1)}), bf16[12,176,256]{2,1,0:T(8,128)(2,1)S(1)}, u32[]{:S(2)}, u32[]{:S(2)}) async-start(bf16[12,176,256]{2,1,0:T(8,128)(2,1)} %copy-done.2), calls=%async_computation.2 | async-start | bytes 2162688 | tf_op jit(solution)/shard_map/cond/branch_1_fun/all_to_all | solution.py:292
  95.6 41.9 %all-to-all-done.2 = bf16[12,176,256]{2,1,0:T(8,128)(2,1)S(1)} async-done(((bf16[12,176,256]{2,1,0:T(8,128)(2,1)}), bf16[12,176,256]{2,1,0:T(8,128)(2,1)S(1)}, u32[]{:S(2)}, u32[]{:S(2)}) %all-to-all-start.2) | async-done | bytes 1081376 | tf_op jit(solution)/shard_map/cond/branch_1_fun/all_to_all | solution.py:292
  138.5 10.0 %all-to-all-start.7 = ((bf16[32,8,256]{2,1,0:T(8,128)(2,1)}), bf16[32,8,256]{2,1,0:T(8,128)(2,1)S(1)}, u32[]{:S(2)}, u32[]{:S(2)}) async-start(bf16[32,8,256]{2,1,0:T(8,128)(2,1)} %bitcast.82), calls=%async_computation.7 | async-start | bytes 262144 | tf_op jit(solution)/shard_map/all_to_all | solution.py:320
  149.4 0.9 select_reduce_fusion.16
  150.9 8.1 %all-to-all-done.7 = bf16[32,8,256]{2,1,0:T(8,128)(2,1)S(1)} async-done(((bf16[32,8,256]{2,1,0:T(8,128)(2,1)}), bf16[32,8,256]{2,1,0:T(8,128)(2,1)S(1)}, u32[]{:S(2)}, u32[]{:S(2)}) %all-to-all-start.7) | async-done | bytes 131104 | tf_op jit(solution)/shard_map/all_to_all | solution.py:320
  (48 shorter events, 9.5 us)
Async XLA Ops:
  3.4 52.3 %copy-start.23 = (s32[1024]{0:T(1024)S(1)}, s32[1024]{0:T(1024)}, u32[]{:S(2)}) copy-start(s32[1024]{0:T(1024)} %get-tuple-element.77) | copy-start | bytes 12292 | tf_op jit(solution)/shard_map/conditional
  3.5 59.6 %copy-start.20 = (f32[6144]{0:T(1024)S(1)}, f32[6144]{0:T(1024)}, u32[]{:S(2)}) copy-start(f32[6144]{0:T(1024)} %get-tuple-element.80) | copy-start | bytes 73732 | tf_op jit(solution)/shard_map/conditional
  3.5 79.9 %collective-permute-start.11 = (bf16[256,6144]{1,0:T(8,128)(2,1)}, bf16[256,6144]{1,0:T(8,128)(2,1)S(1)}, u32[]{:S(2)}, u32[]{:S(2)}) collective-permute-start(bf16[256,6144]{1,0:T(8,128)(2,1)} %get-tuple-element.85.rest_0_.rest_1_.rest_2_.rest_3_), channel_id=1, source_target_pairs={{0,1},{1,0},{2,3},{3,2},{4,5},{5,4},{6,7},{7,6},{8,9},{9,8},{10,11... | collective-permute-start | bytes 9437192 | tf_op jit(solution)/shard_map/cond/branch_1_fun/ppermute | solution.py:43
  43.3 19.8 %collective-permute-start.6 = (bf16[12,168,256]{2,1,0:T(8,128)(2,1)}, bf16[12,168,256]{2,1,0:T(8,128)(2,1)}, u32[]{:S(2)}, u32[]{:S(2)}) collective-permute-start(bf16[12,168,256]{2,1,0:T(8,128)(2,1)} %bitcast.14.mine), channel_id=1, source_target_pairs={{0,1},{1,0},{2,3},{3,2},{4,5},{5,4},{6,7},{7,6},{8,9},{9,8},{10,11... | collective-permute-start | bytes 3096584 | tf_op jit(solution)/shard_map/cond/branch_1_fun/ppermute | solution.py:43
  46.5 16.6 %all-to-all-start.1 = ((bf16[24,8,256]{2,1,0:T(8,128)(2,1)}), bf16[24,8,256]{2,1,0:T(8,128)(2,1)S(1)}, u32[]{:S(2)}, u32[]{:S(2)}) async-start(bf16[24,8,256]{2,1,0:T(8,128)(2,1)} %broadcast_in_dim.268), calls=%async_computation.1 | async-start | bytes 196608 | tf_op jit(solution)/shard_map/cond/branch_1_fun/all_to_all | solution.py:261
  53.6 9.5 %collective-permute-start.7 = (bf16[64,6144]{1,0:T(8,128)(2,1)}, bf16[64,6144]{1,0:T(8,128)(2,1)}, u32[]{:S(2)}, u32[]{:S(2)}) collective-permute-start(bf16[64,6144]{1,0:T(8,128)(2,1)} %bitcast.102), channel_id=1, source_target_pairs={{0,1},{1,0},{2,3},{3,2},{4,5},{5,4},{6,7},{7,6},{8,9},{9,8},{10,11... | collective-permute-start | bytes 2359304 | tf_op jit(solution)/shard_map/cond/branch_1_fun/ppermute | solution.py:43
  63.1 11.0 %copy-start.11 = (bf16[6144,256]{1,0:T(8,128)(2,1)S(1)}, bf16[6144,256]{1,0:T(8,128)(2,1)}, u32[]{:S(2)}) copy-start(bf16[6144,256]{1,0:T(8,128)(2,1)} %get-tuple-element.81) | copy-start | bytes 9437188 | tf_op jit(solution)/shard_map/conditional
  66.7 12.5 %collective-permute-start.8 = (bf16[176,128]{1,0:T(8,128)(2,1)S(1)}, bf16[176,128]{1,0:T(8,128)(2,1)S(1)}, u32[]{:S(2)}, u32[]{:S(2)}) collective-permute-start(bf16[176,128]{1,0:T(8,128)(2,1)S(1)} %get-tuple-element.84), channel_id=1, source_target_pairs={{0,0},{1,1},{2,4},{3,5},{4,8},{5,9},{6,12},{7,13},{8,16},{9,17},{1... | collective-permute-start | bytes 135176 | tf_op jit(solution)/shard_map/cond/branch_1_fun/ppermute | solution.py:276
  70.5 8.7 %collective-permute-start.9 = (bf16[176,128]{1,0:T(8,128)(2,1)S(1)}, bf16[176,128]{1,0:T(8,128)(2,1)S(1)}, u32[]{:S(2)}, u32[]{:S(2)}) collective-permute-start(bf16[176,128]{1,0:T(8,128)(2,1)S(1)} %get-tuple-element.84), channel_id=1, source_target_pairs={{0,2},{1,3},{2,6},{3,7},{4,10},{5,11},{6,14},{7,15},{8,18},{9,19},... | collective-permute-start | bytes 135176 | tf_op jit(solution)/shard_map/cond/branch_1_fun/ppermute | solution.py:277
  74.1 9.3 %copy-start.7 = (bf16[256,6144]{1,0:T(8,128)(2,1)S(1)}, bf16[256,6144]{1,0:T(8,128)(2,1)}, u32[]{:S(2)}) copy-start(bf16[256,6144]{1,0:T(8,128)(2,1)} %get-tuple-element.85.rest_0_.rest_1_.rest_2_.rest_3_) | copy-start | bytes 9437188 | tf_op jit(solution)/shard_map/conditional
  80.2 3.2 %collective-permute-start.10 = (bf16[176,256]{1,0:T(8,128)(2,1)S(1)}, bf16[176,256]{1,0:T(8,128)(2,1)S(1)}, u32[]{:S(2)}, u32[]{:S(2)}) collective-permute-start(bf16[176,256]{1,0:T(8,128)(2,1)S(1)} %attend.5.mine), channel_id=1, source_target_pairs={{0,1},{1,0},{2,3},{3,2},{4,5},{5,4},{6,7},{7,6},{8,9},{9,8},{10,11... | collective-permute-start | bytes 270344 | tf_op jit(solution)/shard_map/cond/branch_1_fun/ppermute | solution.py:43
  85.1 1.0 copy-start.2
  86.1 9.1 %copy-start.26 = (s32[32]{0:T(128)S(1)}, s32[32]{0:T(128)}, u32[]{:S(2)}) copy-start(s32[32]{0:T(128)} %get-tuple-element.120) | copy-start | bytes 388 | tf_op jit(solution)/shard_map/conditional
  86.1 51.5 %copy-start.15 = (bf16[256,256]{1,0:T(8,128)(2,1)S(1)}, bf16[256,256]{1,0:T(8,128)(2,1)}, u32[]{:S(2)}) copy-start(bf16[256,256]{1,0:T(8,128)(2,1)} %get-tuple-element.79) | copy-start | bytes 393220 | tf_op jit(solution)/shard_map/conditional
  86.1 51.4 %all-to-all-start.2 = ((bf16[12,176,256]{2,1,0:T(8,128)(2,1)}), bf16[12,176,256]{2,1,0:T(8,128)(2,1)S(1)}, u32[]{:S(2)}, u32[]{:S(2)}) async-start(bf16[12,176,256]{2,1,0:T(8,128)(2,1)} %copy-done.2), calls=%async_computation.2 | async-start | bytes 2162688 | tf_op jit(solution)/shard_map/cond/branch_1_fun/all_to_all | solution.py:292
  138.5 20.5 %all-to-all-start.7 = ((bf16[32,8,256]{2,1,0:T(8,128)(2,1)}), bf16[32,8,256]{2,1,0:T(8,128)(2,1)S(1)}, u32[]{:S(2)}, u32[]{:S(2)}) async-start(bf16[32,8,256]{2,1,0:T(8,128)(2,1)} %bitcast.82), calls=%async_computation.7 | async-start | bytes 262144 | tf_op jit(solution)/shard_map/all_to_all | solution.py:320

commit v3 on v2

--- a/solution.py
+++ b/solution.py
@@ -3,6 +3,7 @@
 
 import jax
 import jax.numpy as jnp
+import numpy as np
 from jax import lax
 from jax.experimental import pallas as pl
 from jax.experimental.pallas import tpu as pltpu
@@ -19,15 +20,46 @@
 EPS = 1e-05
 ROPE_BASE = 500000.0
 AG_ROWS = 168
-VMEM = 40 * 1024 * 1024
+VMEM = 56 * 1024 * 1024
 
 Z_GROUPS = [[z * 2 + c for z in range(NZ)] for c in range(2)]
+FAR = 4
+FAR_GROUPS = [[(3 * k + r) * 2 + c for k in range(FAR)] for r in range(3) for c in range(2)]
 SWAP = [(t, t ^ 1) for t in range(NT)]
 
 
 STEPS = 3
 PER = NZ // STEPS
 CAPS = (168, 176, 192, 256)
+
+
+def rope_tables():
+    frequency = ROPE_BASE ** (-np.arange(HD // 2) * 2.0 / HD)
+    angles = np.arange(MAXLEN)[:, None] * np.concatenate([frequency, frequency])[None, :]
+    sign = np.where(np.arange(HD) < HD // 2, -1.0, 1.0)[None, :]
+    return np.cos(angles).astype(np.float32), (np.sin(angles) * sign).astype(np.float32)
+
+
+def turn(v, cosine, sine):
+    turned = jnp.concatenate([v[:, HD // 2 :], v[:, : HD // 2]], axis=1)
+    return (v * cosine + turned * sine).astype(jnp.bfloat16)
+
+
+def documents(lengths, source, rows):
+    own = lengths[pl.ds(source, 1), :].astype(jnp.float32)
+    first = lax.broadcasted_iota(jnp.int32, (RPS, RPS), 0)
+    second = lax.broadcasted_iota(jnp.int32, (RPS, RPS), 1)
+    column = jnp.sum(jnp.where(first == second, own, 0.0), axis=1, keepdims=True)
+    end = jnp.sum(jnp.where(first <= second, column, 0.0), axis=0, keepdims=True)
+    end_column = jnp.sum(jnp.where(second <= first, own, 0.0), axis=1, keepdims=True)
+    start = end - own
+    place = lax.broadcasted_iota(jnp.int32, (rows, RPS), 0).astype(jnp.float32)
+    doc = jnp.sum(jnp.where(place >= end, 1.0, 0.0), axis=1, keepdims=True)
+    begun = jnp.max(jnp.where(start <= place, start, 0.0), axis=1, keepdims=True)
+    position = jnp.where(doc < RPS, place[:, :1] - begun, 0.0)
+    along = lax.broadcasted_iota(jnp.int32, (RPS, rows), 1).astype(jnp.float32)
+    doc_row = jnp.sum(jnp.where(along >= end_column, 1.0, 0.0), axis=0, keepdims=True)
+    return doc, position, doc_row
 
 
 def kv_pairs(first):
@@ -94,13 +126,27 @@
         tail, *rest = rest
     else:
         tail = None
-    gain, wq_m, wq_t, inv, q_out, q_acc = rest
+    gain, wq_m, wq_t, inv, lengths, cos_t, sin_t, q_out, cos_out, sin_out, bias_out, q_acc = rest
     step = pl.program_id(0)
     c = core[0]
+    rows = q_acc.shape[0]
 
     @pl.when(step == 0)
     def _():
         q_acc[...] = jnp.zeros_like(q_acc)
+        doc, position, doc_row = documents(lengths, core[3], rows)
+        cosine = jnp.broadcast_to(cos_t[0:1], (rows, HD))
+        sine = jnp.broadcast_to(sin_t[0:1], (rows, HD))
+        for m in range(1, MAXLEN):
+            here = jnp.broadcast_to(position == m, (rows, HD))
+            cosine = jnp.where(here, cos_t[m : m + 1], cosine)
+            sine = jnp.where(here, sin_t[m : m + 1], sine)
+        cos_out[...] = cosine
+        sin_out[...] = sine
+        place_q = lax.broadcasted_iota(jnp.int32, (rows, rows), 0)
+        place_k = lax.broadcasted_iota(jnp.int32, (rows, rows), 1)
+        allowed = (doc == doc_row) & (place_k <= place_q)
+        bias_out[...] = jnp.where(allowed, 0.0, -jnp.inf)
 
     total = q_acc[...]
     for j in range(PER):
@@ -113,7 +159,8 @@
     @pl.when(step == STEPS - 1)
     def _():
         for h in range(2):
-            q_out[:, h * HD : (h + 1) * HD] = total[:, h * HD : (h + 1) * HD] * inv[...]
+            head = total[:, h * HD : (h + 1) * HD] * inv[...]
+            q_out[:, h * HD : (h + 1) * HD] = turn(head, cos_out[...], sin_out[...])
 
 
 def x_specs(mine, tail):
@@ -149,9 +196,11 @@
     )(core, mine, theirs, *([] if tail is None else [tail]), gain, wk_m, wk_t)
 
 
-def project_q(core, mine, theirs, tail, gain, wq, inverse):
+def project_q(core, mine, theirs, tail, gain, wq, inverse, lengths):
     rows = inverse.shape[0]
     wq4 = wq.reshape(NZ, 2, FS, FS)
+    whole = lambda i, c: (0, 0)
+    cos_t, sin_t = rope_tables()
     return pl.pallas_call(
         functools.partial(q_kernel, tail is not None),
         grid_spec=pltpu.PrefetchScalarGridSpec(
@@ -161,57 +210,57 @@
             + [
                 pl.BlockSpec((PER, 1, FS, FS), lambda i, c: (i, c[0], 0, 0)),
                 pl.BlockSpec((PER, 1, FS, FS), lambda i, c: (i, 1 - c[0], 0, 0)),
-                pl.BlockSpec((rows, HD), lambda i, c: (0, 0)),
+                pl.BlockSpec((rows, HD), whole),
+                pl.BlockSpec((RPS, RPS), whole),
+                pl.BlockSpec((MAXLEN, HD), whole),
+                pl.BlockSpec((MAXLEN, HD), whole),
             ],
-            out_specs=pl.BlockSpec((rows, FS), lambda i, c: (0, 0)),
+            out_specs=[
+                pl.BlockSpec((rows, FS), whole),
+                pl.BlockSpec((rows, HD), whole),
+                pl.BlockSpec((rows, HD), whole),
+                pl.BlockSpec((rows, rows), whole),
+            ],
             scratch_shapes=[pltpu.VMEM((rows, FS), jnp.float32)],
         ),
-        out_shape=jax.ShapeDtypeStruct((rows, FS), jnp.float32),
+        out_shape=[
+            jax.ShapeDtypeStruct((rows, FS), jnp.bfloat16),
+            jax.ShapeDtypeStruct((rows, HD), jnp.float32),
+            jax.ShapeDtypeStruct((rows, HD), jnp.float32),
+            jax.ShapeDtypeStruct((rows, rows), jnp.float32),
+        ],
         compiler_params=pltpu.CompilerParams(vmem_limit_bytes=VMEM),
         cost_estimate=pl.CostEstimate(
             flops=2 * rows * D * FS, bytes_accessed=2 * D * (rows + FS), transcendentals=0
         ),
         name="project_q",
-    )(core, mine, theirs, *([] if tail is None else [tail]), gain, wq4, wq4, inverse)
-
-
-def attention_kernel(odd, q_ref, first, second, cos_ref, sin_ref, col_ref, row_ref, out_ref):
-    rows = q_ref.shape[0]
+    )(core, mine, theirs, *([] if tail is None else [tail]), gain, wq4, wq4, inverse,
+      lengths, cos_t, sin_t)
+
+
+def attention_kernel(core, q_ref, first, second, cos_ref, sin_ref, bias_ref, out_ref):
     one, two = first[...].astype(jnp.float32), second[...].astype(jnp.float32)
-    swapped = odd[0] == 1
+    swapped = core[2] == 1
     keys = jnp.where(swapped, two, one)
     values = jnp.where(swapped, one, two).astype(jnp.bfloat16)
-    cosine = cos_ref[...]
-    sine = sin_ref[...]
-
-    def turn(v):
-        turned = jnp.concatenate([-v[:, HD // 2 :], v[:, : HD // 2]], axis=1)
-        return (v * cosine + turned * sine).astype(jnp.bfloat16)
-
-    k_rot = turn(keys)
-    doc_q = col_ref[...]
-    doc_k = row_ref[...]
-    place_q = lax.broadcasted_iota(jnp.int32, (rows, rows), 0)
-    place_k = lax.broadcasted_iota(jnp.int32, (rows, rows), 1)
-    allowed = (doc_q == doc_k) & (place_k <= place_q)
+    k_rot = turn(keys, cos_ref[...], sin_ref[...])
     for h in range(2):
-        q_rot = turn(q_ref[:, h * HD : (h + 1) * HD])
         scores = lax.dot_general(
-            q_rot, k_rot, (((1,), (1,)), ((), ())), preferred_element_type=jnp.float32
-        ) / math.sqrt(HD)
-        masked = jnp.where(allowed, scores, -jnp.inf)
+            q_ref[:, h * HD : (h + 1) * HD], k_rot, (((1,), (1,)), ((), ())), preferred_element_type=jnp.float32
+        )
+        masked = scores * (1 / math.sqrt(HD)) + bias_ref[...]
         exponent = jnp.exp(masked - jnp.max(masked, axis=1, keepdims=True))
         weights = (exponent / jnp.sum(exponent, axis=1, keepdims=True)).astype(jnp.bfloat16)
         context = jnp.dot(weights, values, preferred_element_type=jnp.float32)
         out_ref[:, h * HD : (h + 1) * HD] = context.astype(jnp.bfloat16)
 
 
-def attend(odd, q, first, second, cosine, sine, doc):
+def attend(core, q, first, second, cosine, sine, bias):
     rows = q.shape[0]
     vm = pl.BlockSpec(memory_space=pltpu.VMEM)
     return pl.pallas_call(
         attention_kernel,
-        in_specs=[pl.BlockSpec(memory_space=pltpu.SMEM)] + [vm] * 7,
+        in_specs=[pl.BlockSpec(memory_space=pltpu.SMEM)] + [vm] * 6,
         out_specs=vm,
         out_shape=jax.ShapeDtypeStruct((rows, FS), jnp.bfloat16),
         compiler_params=pltpu.CompilerParams(vmem_limit_bytes=VMEM),
@@ -219,38 +268,59 @@
             flops=8 * rows * rows * HD, bytes_accessed=4 * rows * FS, transcendentals=2 * rows * rows
         ),
         name="attend",
-    )(odd, q, first, second, cosine, sine, doc[:, None], doc[None, :])
-
-
-def out_kernel(core, mine, theirs, *rest):
-    w_mine, w_theirs, out_ref = rest[:PER], rest[PER : 2 * PER], rest[-1]
-    for j in range(PER):
-        total = jnp.dot(mine[...], w_mine[j][...], preferred_element_type=jnp.float32)
-        total += jnp.dot(theirs[...], w_theirs[j][...], preferred_element_type=jnp.float32)
-        out_ref[j] = total.astype(jnp.bfloat16)
-
-
-def out_project(core, mine, theirs, w_mine, w_theirs):
+    )(core, q, first, second, cosine, sine, bias)
+
+
+def out_kernel(place, mine, theirs, *rest):
+    w_mine, w_theirs, outs = rest[:FAR], rest[FAR : 2 * FAR], rest[2 * FAR :]
+    for at, out in enumerate(outs):
+
+        @pl.when(pl.program_id(0) == at)
+        def _():
+            for k in range(FAR):
+                total = jnp.dot(mine[...], w_mine[k][...], preferred_element_type=jnp.float32)
+                total += jnp.dot(theirs[...], w_theirs[k][...], preferred_element_type=jnp.float32)
+                out[k] = total.astype(jnp.bfloat16)
+
+
+def out_project(place, mine, theirs, w_mine, w_theirs, shifts):
     rows = mine.shape[0]
-    context = pl.BlockSpec((rows, FS), lambda i, c: (0, 0))
+    context = pl.BlockSpec((rows, FS), lambda i, p: (0, 0))
+    first = shifts[0]
     weights = [
-        pl.BlockSpec((FS, FS), lambda i, c, j=j: (0, 2 * (PER * i + j) + c[0])) for j in range(PER)
+        pl.BlockSpec((FS, FS), lambda i, p, k=k: (0, 2 * (3 * k + lax.rem(p[1] + first + i, 3)) + p[0]))
+        for k in range(FAR)
     ]
     return pl.pallas_call(
         out_kernel,
         grid_spec=pltpu.PrefetchScalarGridSpec(
             num_scalar_prefetch=1,
-            grid=(STEPS,),
+            grid=(len(shifts),),
             in_specs=[context, context] + weights + weights,
-            out_specs=pl.BlockSpec((PER, rows, FS), lambda i, c: (i, 0, 0)),
-        ),
-        out_shape=jax.ShapeDtypeStruct((NZ, rows, FS), jnp.bfloat16),
+            out_specs=[pl.BlockSpec((FAR, rows, FS), lambda i, p: (0, 0, 0))] * len(shifts),
+        ),
+        out_shape=[jax.ShapeDtypeStruct((FAR, rows, FS), jnp.bfloat16)] * len(shifts),
         compiler_params=pltpu.CompilerParams(vmem_limit_bytes=VMEM),
         cost_estimate=pl.CostEstimate(
-            flops=2 * rows * FS * D, bytes_accessed=D * (rows + 2 * FS), transcendentals=0
+            flops=len(shifts) * 4 * rows * FS * FAR * FS,
+            bytes_accessed=len(shifts) * 2 * FAR * FS * (rows + 2 * FS),
+            transcendentals=0,
         ),
         name="out_project",
-    )(core, mine, theirs, *[w_mine] * PER, *[w_theirs] * PER)
+    )(place, mine, theirs, *[w_mine] * FAR, *[w_theirs] * FAR)
+
+
+def sum_over_chips(place, context, theirs, w_mine, w_theirs):
+    up, down = out_project(place, context, theirs, w_mine, w_theirs, (1, 2))
+    below = lax.ppermute(up, "tensor", [(t, (t + 2) % NT) for t in range(NT)])
+    above = lax.ppermute(down, "tensor", [(t, (t - 2) % NT) for t in range(NT)])
+    (own,) = out_project(place, context, theirs, w_mine, w_theirs, (0,))
+    three = own.astype(jnp.float32) + below.astype(jnp.float32) + above.astype(jnp.float32)
+    parts = lax.all_to_all(
+        three.astype(jnp.bfloat16), "tensor", split_axis=0, concat_axis=0, tiled=True,
+        axis_index_groups=FAR_GROUPS,
+    )
+    return jnp.sum(parts.astype(jnp.float32), axis=0)
 
 
 def gather_rows(x):
@@ -265,34 +335,26 @@
 def layer(rows, rollout, lengths, packing, norm_gain, query_weight, keyval_weight, out_weight):
     source = lax.axis_index("dp")
     tensor_index = lax.axis_index("tensor")
-    core = (tensor_index % 2).astype(jnp.int32).reshape(1)
+    core = jnp.stack([tensor_index % 2, tensor_index // 2 % 3, tensor_index // 2 % 2, source]).astype(jnp.int32)
     x = rollout[:rows]
 
     mine, tail = gather_rows(x)
+    if tail is not None:
+        mine, tail = lax.optimization_barrier((mine, tail))
     theirs = swap(mine)
     gain = norm_gain.reshape(NT, 1, FS)
     wk = keyval_weight.T
     keyval, inverse = project_kv(core, mine, theirs, tail, gain, wk, swap(wk))
     first = lax.ppermute(keyval, "tensor", kv_pairs(True))
     second = lax.ppermute(keyval, "tensor", kv_pairs(False))
-    q = project_q(core, mine, theirs, tail, gain, query_weight, inverse)
-
+    q, cosine, sine, bias = project_q(core, mine, theirs, tail, gain, query_weight, inverse, lengths)
+    context = attend(core, q, first, second, cosine, sine, bias)
+    summed = sum_over_chips(core, context, swap(context), out_weight, swap(out_weight))
     my_len = lax.dynamic_index_in_dim(lengths, source, 0, keepdims=False)
     earlier = jnp.arange(RPS)[None, :] < jnp.arange(RPS)[:, None]
     start = jnp.sum(jnp.where(earlier, my_len[None, :], 0), axis=1)
     places = jnp.arange(rows, dtype=jnp.int32)
-    doc = jnp.sum((places[:, None] >= (start + my_len)[None, :]).astype(jnp.int32), axis=1)
-    begun = jnp.max(jnp.where(start[None, :] <= places[:, None], start[None, :], 0), axis=1)
-    position = jnp.where(doc < RPS, places - begun, 0)
-    frequency = ROPE_BASE ** (-jnp.arange(HD // 2, dtype=jnp.float32) * 2.0 / HD)
-    angles = position.astype(jnp.float32)[:, None] * jnp.concatenate([frequency, frequency])[None, :]
-    odd = (tensor_index // 2 % 2).astype(jnp.int32).reshape(1)
-    context = attend(odd, q, first, second, jnp.cos(angles), jnp.sin(angles), doc)
-    partial = out_project(core, context, swap(context), out_weight, swap(out_weight))
-    parts = lax.all_to_all(
-        partial, "tensor", split_axis=0, concat_axis=0, tiled=True, axis_index_groups=Z_GROUPS
-    )
-    result = (jnp.sum(parts.astype(jnp.float32), axis=0) + x.astype(jnp.float32)).astype(jnp.bfloat16)
+    result = (summed + x.astype(jnp.float32)).astype(jnp.bfloat16)
 
     pack = packing.reshape(RPS, RPS)
     of_mine = pack // RPS == source

time: 161 us -> 146 us (0.907)
  the two profiles are of different devices: /device:TPU:64 before, /device:TPU:8 now
where the time goes in v3:
time: 146 us; the launch traced here: 145 us
  blocking collectives  39.2 us (27%)
  waiting for transfers between devices  38.3 us (26%)
  starting transfers between devices  34.2 us (23%)
  Pallas kernels  19.2 us (13%)
  other arithmetic  6.03 us (4%)
  local copies, waits for them, and re-layouts  4.38 us (3%)
  between operations  2 us (1%)
  matrix products  1.79 us (1%)
    all_gather x1, blocking collectives, gather_rows(): lax.all_gather(x[:AG_ROWS], 'tensor', axis=0, axis_index_groups=Z_GROUPS)  39.2 us
    all_to_all x1, waiting for transfers between devices, sum_over_chips(): lax.all_to_all(three.astype(jnp.bfloat16), 'tensor', split_axis=0, concat...  18.2 us
    all_to_all x1, starting transfers between devices, body(): lax.all_to_all(outgoing.reshape(RPS, MAXLEN, FS), 'dp', split_axis=0, con...  10.2 us
    ppermute x4, starting transfers between devices, swap(): return lax.ppermute(v, 'tensor', SWAP)  8.28 us
    all_to_all x1, waiting for transfers between devices, body(): lax.all_to_all(outgoing.reshape(RPS, MAXLEN, FS), 'dp', split_axis=0, con...  7.19 us
    pallas_call x2, Pallas kernels, out_project(): pl.pallas_call(out_kernel, grid_spec=pltpu.PrefetchScalarGridSpec(num_sca...  6.74 us
    ppermute x1, waiting for transfers between devices, layer(): second = lax.ppermute(keyval, 'tensor', kv_pairs(False))  5.38 us
    ppermute x1, starting transfers between devices, sum_over_chips(): above = lax.ppermute(down, 'tensor', [(t, (t - 2) % NT) for t in range(NT)])  5.26 us
  transfers between devices with their start and end apart: 10, of which 7 were waited for; matrix products, arithmetic and copies ran while one was open for 3% of the time, Pallas kernels for 11%

profile of v3, /device:TPU:8, one launch (start us, length us, event | category | flops | bytes accessed | tf_op | source)
XLA Modules:
  0.0 145.4 jit_solution(11008890345915942285)
XLA Ops:
  3.4 121.4 %conditional.2 = (bf16[256,256]{1,0:T(8,128)(2,1)}) conditional(s32[]{:T(128)} %clamp.3, (s32[1024]{0:T(1024)}, s32[32,32]{1,0:T(8,128)}, bf16[256,256]{1,0:T(8,128)(2,1)}, f32[6144]{0:T(1024)}, bf16[6144,256]{1,0:T(8,128)(2,1)}, /*index=5*/bf16[6144,64]{0,1:T(8,128)(2,1)}, f32[8,128]{1,0:T(8,128)}, ...), branch_computations={%region_7.13_spmd, %region_13.19_spmd, %region_19.25_spmd, %region... | conditional | flops 2116254464 | bytes 83266320
  3.5 2.1 %collective-permute-start.5 = (bf16[256,6144]{1,0:T(8,128)(2,1)}, bf16[256,6144]{1,0:T(8,128)(2,1)}, u32[]{:S(2)}, u32[]{:S(2)}) collective-permute-start(bf16[256,6144]{1,0:T(8,128)(2,1)} %get-tuple-element.98.rest_0_.rest_1_.rest_2_.rest_3_), channel_id=1, source_target_pairs={{0,1},{1,0},{2,3},{3,2},{4,5},{5,4},{6,7},{7,6},{8,9},{9,8},{10,11... | collective-permute-start | bytes 9437192 | tf_op jit(solution)/shard_map/cond/branch_0_fun/ppermute | solution.py:75
  6.4 39.2 %all-gather = bf16[2016,256]{1,0:T(8,128)(2,1)S(1)} all-gather(bf16[168,256]{1,0:T(8,128)(2,1)S(1)} %slice.22), channel_id=2, replica_groups={{0,2,4,6,8,10,12,14,16,18,20,22},{1,3,5,7,9,11,13,15,17,19,21,23},{24,2..., dimensions={0}, use_global_device_ids=true | all-gather | bytes 1118208 | tf_op jit(solution)/shard_map/cond/branch_0_fun/all_gather | solution.py:332
  45.6 1.9 %collective-permute-start = (bf16[12,168,256]{2,1,0:T(8,128)(2,1)S(1)}, bf16[12,168,256]{2,1,0:T(8,128)(2,1)S(1)}, u32[]{:S(2)}, u32[]{:S(2)}) collective-permute-start(bf16[12,168,256]{2,1,0:T(8,128)(2,1)S(1)} %bitcast.85), channel_id=1, source_target_pairs={{0,1},{1,0},{2,3},{3,2},{4,5},{5,4},{6,7},{7,6},{8,9},{9,8},{10,11... | collective-permute-start | bytes 3096584 | tf_op jit(solution)/shard_map/cond/branch_0_fun/ppermute | solution.py:75
  47.6 2.4 %collective-permute-start.1 = (bf16[64,6144]{1,0:T(8,128)(2,1)}, bf16[64,6144]{1,0:T(8,128)(2,1)S(1)}, u32[]{:S(2)}, u32[]{:S(2)}) collective-permute-start(bf16[64,6144]{1,0:T(8,128)(2,1)} %bitcast.68), channel_id=1, source_target_pairs={{0,1},{1,0},{2,3},{3,2},{4,5},{5,4},{6,7},{7,6},{8,9},{9,8},{10,11... | collective-permute-start | bytes 2359304 | tf_op jit(solution)/shard_map/cond/branch_0_fun/ppermute | solution.py:75
  53.3 4.8 %project_kv.4 = (bf16[168,128]{1,0:T(8,128)(2,1)}, f32[168,128]{1,0:T(8,128)}) custom-call(s32[4]{0:T(128)} %pad_add_fusion.core.place, bf16[12,168,256]{2,1,0:T(8,128)(2,1)} %bitcast.86, bf16[12,168,256]{2,1,0:T(8,128)(2,1)} %copy-done.17, f32[24,1,256]{2,1,0:T(1,128)} %bitcast.88, bf16[64,6144]{1,0:T(8,128)(2,1)} %bitcast.69, bf16[64,6144]{1,0:T(8,128)(2,1)} %copy-done.25), custom_call_target="tpu_custom_call" | custom-call | flops 264241152 | bytes 3637248 | tf_op jit(solution)/shard_map/cond/branch_0_fun/project_kv/pallas_call | solution.py:178
  58.1 1.4 collective-permute-start.2
  59.6 3.2 %collective-permute-start.3 = (bf16[168,128]{1,0:T(8,128)(2,1)}, bf16[168,128]{1,0:T(8,128)(2,1)S(1)}, u32[]{:S(2)}, u32[]{:S(2)}) collective-permute-start(bf16[168,128]{1,0:T(8,128)(2,1)} %get-tuple-element.94), channel_id=1, source_target_pairs={{0,2},{1,3},{2,6},{3,7},{4,10},{5,11},{6,14},{7,15},{8,18},{9,19},... | collective-permute-start | bytes 129032 | tf_op jit(solution)/shard_map/cond/branch_0_fun/ppermute | solution.py:349
  62.8 5.0 %project_q.4 = (bf16[168,256]{1,0:T(8,128)(2,1)}, f32[168,128]{1,0:T(8,128)}, f32[168,128]{1,0:T(8,128)}, f32[168,168]{1,0:T(8,128)}) custom-call(s32[4]{0:T(128)} %pad_add_fusion.core.place, bf16[12,168,256]{2,1,0:T(8,128)(2,1)} %bitcast.87, bf16[12,168,256]{2,1,0:T(8,128)(2,1)} %copy-done.17, f32[24,1,256]{2,1,0:T(1,128)S(1)} %bitcast.89, ...), custom_call_target="tpu_custom_call" | custom-call | flops 528482304 | bytes 5210112 | tf_op jit(solution)/shard_map/cond/branch_0_fun/project_q/pallas_call | solution.py:204
  67.8 5.4 %collective-permute-done.3.second = bf16[168,128]{1,0:T(8,128)(2,1)S(1)} collective-permute-done((bf16[168,128]{1,0:T(8,128)(2,1)}, bf16[168,128]{1,0:T(8,128)(2,1)S(1)}, u32[]{:S(2)}, u32[]{:S(2)}) %collective-permute-start.3) | collective-permute-done | bytes 43040 | tf_op jit(solution)/shard_map/cond/branch_0_fun/ppermute | solution.py:349
  73.8 2.6 %attend.4.mine = bf16[168,256]{1,0:T(8,128)(2,1)} custom-call(s32[4]{0:T(128)} %pad_add_fusion.core.place, bf16[168,256]{1,0:T(8,128)(2,1)} %get-tuple-element.93.q_ref, bf16[168,128]{1,0:T(8,128)(2,1)} %copy-done.53, bf16[168,128]{1,0:T(8,128)(2,1)} %copy-done.54, f32[168,128]{1,0:T(8,128)} %get-tuple-element.95.cos_ref, ...), custom_call_target="tpu_custom_call" | custom-call | flops 28901376 | bytes 172032 | tf_op jit(solution)/shard_map/cond/branch_0_fun/attend/pallas_call | solution.py:261
  76.5 1.9 %collective-permute-start.4 = (bf16[168,256]{1,0:T(8,128)(2,1)}, bf16[168,256]{1,0:T(8,128)(2,1)S(1)}, u32[]{:S(2)}, u32[]{:S(2)}) collective-permute-start(bf16[168,256]{1,0:T(8,128)(2,1)} %attend.4.mine), channel_id=1, source_target_pairs={{0,1},{1,0},{2,3},{3,2},{4,5},{5,4},{6,7},{7,6},{8,9},{9,8},{10,11... | collective-permute-start | bytes 258056 | tf_op jit(solution)/shard_map/cond/branch_0_fun/ppermute | solution.py:75
  78.4 1.5 %collective-permute-done.4.theirs = bf16[168,256]{1,0:T(8,128)(2,1)S(1)} collective-permute-done((bf16[168,256]{1,0:T(8,128)(2,1)}, bf16[168,256]{1,0:T(8,128)(2,1)S(1)}, u32[]{:S(2)}, u32[]{:S(2)}) %collective-permute-start.4) | collective-permute-done | bytes 86048 | tf_op jit(solution)/shard_map/cond/branch_0_fun/ppermute | solution.py:75
  80.5 3.8 %out_project.9 = (bf16[4,168,256]{2,1,0:T(8,128)(2,1)}, bf16[4,168,256]{2,1,0:T(8,128)(2,1)}) custom-call(s32[4]{0:T(128)} %pad_add_fusion.core.place, bf16[168,256]{1,0:T(8,128)(2,1)} %attend.4.mine, bf16[168,256]{1,0:T(8,128)(2,1)} %copy-done.34, bf16[256,6144]{1,0:T(8,128)(2,1)S(1)} %copy-done, bf16[256,6144]{1,0:T(8,128)(2,1)S(1)} %copy-done, ...), custom_call_target="tpu_custom_call" | custom-call | flops 352321536 | bytes 2785280 | tf_op jit(solution)/shard_map/cond/branch_0_fun/out_project/pallas_call | solution.py:294
  84.3 1.9 %collective-permute-start.6 = (bf16[4,168,256]{2,1,0:T(8,128)(2,1)}, bf16[4,168,256]{2,1,0:T(8,128)(2,1)S(1)}, u32[]{:S(2)}, u32[]{:S(2)}) collective-permute-start(bf16[4,168,256]{2,1,0:T(8,128)(2,1)} %get-tuple-element.99), channel_id=1, source_target_pairs={{0,2},{1,3},{2,4},{3,5},{4,6},{5,7},{6,8},{7,9},{8,10},{9,11},{10,... | collective-permute-start | bytes 1032200 | tf_op jit(solution)/shard_map/cond/branch_0_fun/ppermute | solution.py:315
  86.2 5.3 %collective-permute-start.7 = (bf16[4,168,256]{2,1,0:T(8,128)(2,1)}, bf16[4,168,256]{2,1,0:T(8,128)(2,1)S(1)}, u32[]{:S(2)}, u32[]{:S(2)}) collective-permute-start(bf16[4,168,256]{2,1,0:T(8,128)(2,1)} %get-tuple-element.100), channel_id=1, source_target_pairs={{0,22},{1,23},{2,0},{3,1},{4,2},{5,3},{6,4},{7,5},{8,6},{9,7},{10,... | collective-permute-start | bytes 1032200 | tf_op jit(solution)/shard_map/cond/branch_0_fun/ppermute | solution.py:316
  91.5 3.0 %out_project.8 = bf16[4,168,256]{2,1,0:T(8,128)(2,1)} custom-call(s32[4]{0:T(128)} %pad_add_fusion.core.place, bf16[168,256]{1,0:T(8,128)(2,1)} %attend.4.mine, bf16[168,256]{1,0:T(8,128)(2,1)} %copy-done.34, bf16[256,6144]{1,0:T(8,128)(2,1)S(1)} %copy-done, bf16[256,6144]{1,0:T(8,128)(2,1)S(1)} %copy-done, bf16[256,6144]{1,0:T(8,128)(2,1)S(1)} %copy-done, ...), custom_call_target="tpu_custom_call" | custom-call | flops 176160768 | bytes 1392640 | tf_op jit(solution)/shard_map/cond/branch_0_fun/out_project/pallas_call | solution.py:294
  94.4 3.2 %collective-permute-done.6 = bf16[4,168,256]{2,1,0:T(8,128)(2,1)S(1)} collective-permute-done((bf16[4,168,256]{2,1,0:T(8,128)(2,1)}, bf16[4,168,256]{2,1,0:T(8,128)(2,1)S(1)}, u32[]{:S(2)}, u32[]{:S(2)}) %collective-permute-start.6) | collective-permute-done | bytes 344096 | tf_op jit(solution)/shard_map/cond/branch_0_fun/ppermute | solution.py:315
  97.7 1.4 collective-permute-done.7
  99.1 1.9 %add_convert_fusion = bf16[4,168,256]{2,1,0:T(8,128)(2,1)} fusion(bf16[4,168,256]{2,1,0:T(8,128)(2,1)S(1)} %collective-permute-done.7, bf16[4,168,256]{2,1,0:T(8,128)(2,1)S(1)} %collective-permute-done.6, bf16[4,168,256]{2,1,0:T(8,128)(2,1)} %out_project.8), kind=kLoop, calls=%fused_computation.1 | loop fusion | flops 1032192 | bytes 1376256 | tf_op jit(solution)/shard_map/cond/branch_0_fun/convert_element_type | solution.py:320
  101.0 4.0 %all-to-all-start = ((bf16[4,168,256]{2,1,0:T(8,128)(2,1)}), bf16[4,168,256]{2,1,0:T(8,128)(2,1)S(1)}, u32[]{:S(2)}, u32[]{:S(2)}) async-start(bf16[4,168,256]{2,1,0:T(8,128)(2,1)} %add_convert_fusion), calls=%async_computation | async-start | bytes 688128 | tf_op jit(solution)/shard_map/cond/branch_0_fun/all_to_all | solution.py:319
  105.7 18.2 %all-to-all-done = bf16[4,168,256]{2,1,0:T(8,128)(2,1)S(1)} async-done(((bf16[4,168,256]{2,1,0:T(8,128)(2,1)}), bf16[4,168,256]{2,1,0:T(8,128)(2,1)S(1)}, u32[]{:S(2)}, u32[]{:S(2)}) %all-to-all-start) | async-done | bytes 344096 | tf_op jit(solution)/shard_map/cond/branch_0_fun/all_to_all | solution.py:319
  124.8 10.2 %all-to-all-start.7 = ((bf16[32,8,256]{2,1,0:T(8,128)(2,1)}), bf16[32,8,256]{2,1,0:T(8,128)(2,1)S(1)}, u32[]{:S(2)}, u32[]{:S(2)}) async-start(bf16[32,8,256]{2,1,0:T(8,128)(2,1)} %bitcast.58), calls=%async_computation.7 | async-start | bytes 262144 | tf_op jit(solution)/shard_map/all_to_all | solution.py:382
  137.3 7.2 %all-to-all-done.7 = bf16[32,8,256]{2,1,0:T(8,128)(2,1)S(1)} async-done(((bf16[32,8,256]{2,1,0:T(8,128)(2,1)}), bf16[32,8,256]{2,1,0:T(8,128)(2,1)S(1)}, u32[]{:S(2)}, u32[]{:S(2)}) %all-to-all-start.7) | async-done | bytes 131104 | tf_op jit(solution)/shard_map/all_to_all | solution.py:382
  (58 shorter events, 11.8 us)
Async XLA Ops:
  3.4 59.3 %copy-start.19 = (f32[6144]{0:T(1024)S(1)}, f32[6144]{0:T(1024)}, u32[]{:S(2)}) copy-start(f32[6144]{0:T(1024)} %get-tuple-element.87) | copy-start | bytes 73732 | tf_op jit(solution)/shard_map/conditional
  3.4 59.3 %copy-start.27 = (s32[32,32]{1,0:T(8,128)S(1)}, s32[32,32]{1,0:T(8,128)}, u32[]{:S(2)}) copy-start(s32[32,32]{1,0:T(8,128)} %get-tuple-element.85.rest_4_) | copy-start | bytes 12292 | tf_op jit(solution)/shard_map/conditional
  3.5 59.3 %copy-start.39 = (f32[8,128]{1,0:T(8,128)S(1)}, f32[8,128]{1,0:T(8,128)}, u32[]{:S(2)}) copy-start(f32[8,128]{1,0:T(8,128)} %get-tuple-element.91.rest_5_) | copy-start | bytes 12292 | tf_op jit(solution)/shard_map/conditional
  3.5 59.3 %copy-start.43 = (f32[8,128]{1,0:T(8,128)S(1)}, f32[8,128]{1,0:T(8,128)}, u32[]{:S(2)}) copy-start(f32[8,128]{1,0:T(8,128)} %get-tuple-element.92.rest_6_) | copy-start | bytes 12292 | tf_op jit(solution)/shard_map/conditional
  3.5 76.4 %collective-permute-start.5 = (bf16[256,6144]{1,0:T(8,128)(2,1)}, bf16[256,6144]{1,0:T(8,128)(2,1)}, u32[]{:S(2)}, u32[]{:S(2)}) collective-permute-start(bf16[256,6144]{1,0:T(8,128)(2,1)} %get-tuple-element.98.rest_0_.rest_1_.rest_2_.rest_3_), channel_id=1, source_target_pairs={{0,1},{1,0},{2,3},{3,2},{4,5},{5,4},{6,7},{7,6},{8,9},{9,8},{10,11... | collective-permute-start | bytes 9437192 | tf_op jit(solution)/shard_map/cond/branch_0_fun/ppermute | solution.py:75
  45.6 6.4 %copy-start.10 = (bf16[2016,256]{1,0:T(8,128)(2,1)}, bf16[2016,256]{1,0:T(8,128)(2,1)S(1)}, u32[]{:S(2)}) copy-start(bf16[2016,256]{1,0:T(8,128)(2,1)S(1)} %all-gather) | copy-start | bytes 3096580 | tf_op jit(solution)/shard_map/conditional
  45.6 6.4 %collective-permute-start = (bf16[12,168,256]{2,1,0:T(8,128)(2,1)S(1)}, bf16[12,168,256]{2,1,0:T(8,128)(2,1)S(1)}, u32[]{:S(2)}, u32[]{:S(2)}) collective-permute-start(bf16[12,168,256]{2,1,0:T(8,128)(2,1)S(1)} %bitcast.85), channel_id=1, source_target_pairs={{0,1},{1,0},{2,3},{3,2},{4,5},{5,4},{6,7},{7,6},{8,9},{9,8},{10,11... | collective-permute-start | bytes 3096584 | tf_op jit(solution)/shard_map/cond/branch_0_fun/ppermute | solution.py:75
  47.6 4.5 %collective-permute-start.1 = (bf16[64,6144]{1,0:T(8,128)(2,1)}, bf16[64,6144]{1,0:T(8,128)(2,1)S(1)}, u32[]{:S(2)}, u32[]{:S(2)}) collective-permute-start(bf16[64,6144]{1,0:T(8,128)(2,1)} %bitcast.68), channel_id=1, source_target_pairs={{0,1},{1,0},{2,3},{3,2},{4,5},{5,4},{6,7},{7,6},{8,9},{9,8},{10,11... | collective-permute-start | bytes 2359304 | tf_op jit(solution)/shard_map/cond/branch_0_fun/ppermute | solution.py:75
  50.0 12.8 %copy-start.4 = (bf16[6144,256]{1,0:T(8,128)(2,1)S(1)}, bf16[6144,256]{1,0:T(8,128)(2,1)}, u32[]{:S(2)}) copy-start(bf16[6144,256]{1,0:T(8,128)(2,1)} %get-tuple-element.88) | copy-start | bytes 9437188 | tf_op jit(solution)/shard_map/conditional
  52.1 0.9 copy-start.25
  52.1 1.2 copy-start.17
  58.1 9.7 %collective-permute-start.2 = (bf16[168,128]{1,0:T(8,128)(2,1)}, bf16[168,128]{1,0:T(8,128)(2,1)S(1)}, u32[]{:S(2)}, u32[]{:S(2)}) collective-permute-start(bf16[168,128]{1,0:T(8,128)(2,1)} %get-tuple-element.94), channel_id=1, source_target_pairs={{0,0},{1,1},{2,4},{3,5},{4,8},{5,9},{6,12},{7,13},{8,16},{9,17},{1... | collective-permute-start | bytes 129032 | tf_op jit(solution)/shard_map/cond/branch_0_fun/ppermute | solution.py:348
  59.6 13.7 %collective-permute-start.3 = (bf16[168,128]{1,0:T(8,128)(2,1)}, bf16[168,128]{1,0:T(8,128)(2,1)S(1)}, u32[]{:S(2)}, u32[]{:S(2)}) collective-permute-start(bf16[168,128]{1,0:T(8,128)(2,1)} %get-tuple-element.94), channel_id=1, source_target_pairs={{0,2},{1,3},{2,6},{3,7},{4,10},{5,11},{6,14},{7,15},{8,18},{9,19},... | collective-permute-start | bytes 129032 | tf_op jit(solution)/shard_map/cond/branch_0_fun/ppermute | solution.py:349
  62.8 17.7 %copy-start = (bf16[256,6144]{1,0:T(8,128)(2,1)S(1)}, bf16[256,6144]{1,0:T(8,128)(2,1)}, u32[]{:S(2)}) copy-start(bf16[256,6144]{1,0:T(8,128)(2,1)} %get-tuple-element.98.rest_0_.rest_1_.rest_2_.rest_3_) | copy-start | bytes 9437188 | tf_op jit(solution)/shard_map/conditional
  67.8 5.4 %copy-start.53 = (bf16[168,128]{1,0:T(8,128)(2,1)}, bf16[168,128]{1,0:T(8,128)(2,1)S(1)}, u32[]{:S(2)}) copy-start(bf16[168,128]{1,0:T(8,128)(2,1)S(1)} %collective-permute-done.2.first) | copy-start | bytes 129028 | tf_op jit(solution)/shard_map/conditional
  73.2 0.6 copy-start.54
  76.5 3.4 %collective-permute-start.4 = (bf16[168,256]{1,0:T(8,128)(2,1)}, bf16[168,256]{1,0:T(8,128)(2,1)S(1)}, u32[]{:S(2)}, u32[]{:S(2)}) collective-permute-start(bf16[168,256]{1,0:T(8,128)(2,1)} %attend.4.mine), channel_id=1, source_target_pairs={{0,1},{1,0},{2,3},{3,2},{4,5},{5,4},{6,7},{7,6},{8,9},{9,8},{10,11... | collective-permute-start | bytes 258056 | tf_op jit(solution)/shard_map/cond/branch_0_fun/ppermute | solution.py:75
  79.9 0.6 copy-start.34
  84.3 13.4 %collective-permute-start.6 = (bf16[4,168,256]{2,1,0:T(8,128)(2,1)}, bf16[4,168,256]{2,1,0:T(8,128)(2,1)S(1)}, u32[]{:S(2)}, u32[]{:S(2)}) collective-permute-start(bf16[4,168,256]{2,1,0:T(8,128)(2,1)} %get-tuple-element.99), channel_id=1, source_target_pairs={{0,2},{1,3},{2,4},{3,5},{4,6},{5,7},{6,8},{7,9},{8,10},{9,11},{10,... | collective-permute-start | bytes 1032200 | tf_op jit(solution)/shard_map/cond/branch_0_fun/ppermute | solution.py:315
  86.2 18.8 %copy-start.35 = (s32[1024]{0:T(1024)S(1)}, s32[1024]{0:T(1024)}, u32[]{:S(2)}) copy-start(s32[1024]{0:T(1024)} %get-tuple-element.84) | copy-start | bytes 12292 | tf_op jit(solution)/shard_map/conditional
  86.2 37.7 %copy-start.11 = (bf16[256,256]{1,0:T(8,128)(2,1)S(1)}, bf16[256,256]{1,0:T(8,128)(2,1)}, u32[]{:S(2)}) copy-start(bf16[256,256]{1,0:T(8,128)(2,1)} %get-tuple-element.86) | copy-start | bytes 393220 | tf_op jit(solution)/shard_map/conditional
  86.2 12.9 %collective-permute-start.7 = (bf16[4,168,256]{2,1,0:T(8,128)(2,1)}, bf16[4,168,256]{2,1,0:T(8,128)(2,1)S(1)}, u32[]{:S(2)}, u32[]{:S(2)}) collective-permute-start(bf16[4,168,256]{2,1,0:T(8,128)(2,1)} %get-tuple-element.100), channel_id=1, source_target_pairs={{0,22},{1,23},{2,0},{3,1},{4,2},{5,3},{6,4},{7,5},{8,6},{9,7},{10,... | collective-permute-start | bytes 1032200 | tf_op jit(solution)/shard_map/cond/branch_0_fun/ppermute | solution.py:316
  101.0 22.9 %all-to-all-start = ((bf16[4,168,256]{2,1,0:T(8,128)(2,1)}), bf16[4,168,256]{2,1,0:T(8,128)(2,1)S(1)}, u32[]{:S(2)}, u32[]{:S(2)}) async-start(bf16[4,168,256]{2,1,0:T(8,128)(2,1)} %add_convert_fusion), calls=%async_computation | async-start | bytes 688128 | tf_op jit(solution)/shard_map/cond/branch_0_fun/all_to_all | solution.py:319
  124.8 19.7 %all-to-all-start.7 = ((bf16[32,8,256]{2,1,0:T(8,128)(2,1)}), bf16[32,8,256]{2,1,0:T(8,128)(2,1)S(1)}, u32[]{:S(2)}, u32[]{:S(2)}) async-start(bf16[32,8,256]{2,1,0:T(8,128)(2,1)} %bitcast.58), calls=%async_computation.7 | async-start | bytes 262144 | tf_op jit(solution)/shard_map/all_to_all | solution.py:382

commit v4 on v3

--- a/solution.py
+++ b/solution.py
@@ -20,7 +20,7 @@
 EPS = 1e-05
 ROPE_BASE = 500000.0
 AG_ROWS = 168
-VMEM = 56 * 1024 * 1024
+VMEM = 24 * 1024 * 1024
 
 Z_GROUPS = [[z * 2 + c for z in range(NZ)] for c in range(2)]
 FAR = 4
@@ -83,12 +83,12 @@
     return x
 
 
-def kv_kernel(has_tail, core, mine, theirs, *rest):
+def kv_kernel(has_tail, core, mine, *rest):
     if has_tail:
         tail, *rest = rest
     else:
         tail = None
-    gain, wk_m, wk_t, kv_out, inv_out, kv_acc, sq_acc = rest
+    gain, wk_m, wk_t, out, kv_acc, sq_acc = rest
     step = pl.program_id(0)
     c = core[0]
 
@@ -99,26 +99,28 @@
 
     total, squares = kv_acc[...], sq_acc[...]
     for j in range(PER):
-        for x_ref, side in ((mine, c), (theirs, 1 - c)):
-            x = rows_of((x_ref, tail), j, side)
-            square = x * x
-            squares += square[:, :128] + square[:, 128:]
-            scaled = (x * gain[2 * j + side]).astype(jnp.bfloat16)
-            at = pl.ds(pl.multiple_of((2 * j + side) * FS, FS), FS)
-            w = jnp.concatenate([wk_m[:, at], wk_t[:, at]], axis=0)
-            total += lax.dot_general(
-                scaled, w, (((1,), (1,)), ((), ())), preferred_element_type=jnp.float32
-            )
+        x = rows_of((mine, tail), j, c)
+        square = x * x
+        squares += square[:, :128] + square[:, 128:]
+        scaled = (x * gain[2 * j + c]).astype(jnp.bfloat16)
+        at = pl.ds(pl.multiple_of((2 * j + c) * FS, FS), FS)
+        w = jnp.concatenate([wk_m[:, at], wk_t[:, at]], axis=0)
+        total += lax.dot_general(scaled, w, (((1,), (1,)), ((), ())), preferred_element_type=jnp.float32)
     kv_acc[...] = total
     sq_acc[...] = squares
 
     @pl.when(step == STEPS - 1)
     def _():
-        inverse = lax.rsqrt(jnp.sum(squares, axis=1, keepdims=True) / D + EPS)
-        out = total * inverse
-        turned = jnp.concatenate([out[:, KVS:], out[:, :KVS]], axis=1)
-        kv_out[...] = jnp.where(c == 0, out, turned).astype(jnp.bfloat16)
-        inv_out[...] = jnp.broadcast_to(inverse, inv_out.shape)
+        turned = jnp.concatenate([total[:, KVS:], total[:, :KVS]], axis=1)
+        out[:, :HD] = jnp.where(c == 0, total, turned)
+        out[:, HD:] = squares
+
+
+def join_kernel(mine, theirs, kv_out, inv_out):
+    total = mine[...] + theirs[...]
+    inverse = lax.rsqrt(jnp.sum(total[:, HD:], axis=1, keepdims=True) / D + EPS)
+    kv_out[...] = (total[:, :HD] * inverse).astype(jnp.bfloat16)
+    inv_out[...] = jnp.broadcast_to(inverse, inv_out.shape)
 
 
 def q_kernel(has_tail, core, mine, theirs, *rest):
@@ -163,37 +165,45 @@
             q_out[:, h * HD : (h + 1) * HD] = turn(head, cos_out[...], sin_out[...])
 
 
-def x_specs(mine, tail):
-    specs = [pl.BlockSpec((PER, mine.shape[1], FS), lambda i, c: (i, 0, 0))] * 2
+def x_specs(xs, tail):
+    specs = [pl.BlockSpec((PER, x.shape[1], FS), lambda i, c: (i, 0, 0)) for x in xs]
     if tail is not None:
         specs.append(pl.BlockSpec((2 * PER, tail.shape[1], FS), lambda i, c: (i, 0, 0)))
     specs.append(pl.BlockSpec((2 * PER, 1, FS), lambda i, c: (i, 0, 0)))
     return specs
 
 
-def project_kv(core, mine, theirs, tail, gain, wk_m, wk_t):
+def project_kv(core, mine, tail, gain, wk_m, wk_t):
     rows = mine.shape[1] + (0 if tail is None else tail.shape[1])
-    whole = pl.BlockSpec((rows, HD), lambda i, c: (0, 0))
     wk_spec = pl.BlockSpec((KVS, 2 * PER * FS), lambda i, c: (0, i))
-    return pl.pallas_call(
+    part = pl.pallas_call(
         functools.partial(kv_kernel, tail is not None),
         grid_spec=pltpu.PrefetchScalarGridSpec(
             num_scalar_prefetch=1,
             grid=(STEPS,),
-            in_specs=x_specs(mine, tail) + [wk_spec, wk_spec],
-            out_specs=[whole, whole],
+            in_specs=x_specs([mine], tail) + [wk_spec, wk_spec],
+            out_specs=pl.BlockSpec((rows, 2 * HD), lambda i, c: (0, 0)),
             scratch_shapes=[pltpu.VMEM((rows, HD), jnp.float32), pltpu.VMEM((rows, HD), jnp.float32)],
         ),
+        out_shape=jax.ShapeDtypeStruct((rows, 2 * HD), jnp.float32),
+        compiler_params=pltpu.CompilerParams(vmem_limit_bytes=VMEM),
+        cost_estimate=pl.CostEstimate(
+            flops=rows * D * HD, bytes_accessed=D * (rows + 2 * HD), transcendentals=0
+        ),
+        name="project_kv",
+    )(core, mine, *([] if tail is None else [tail]), gain, wk_m, wk_t)
+    vm = pl.BlockSpec(memory_space=pltpu.VMEM)
+    return pl.pallas_call(
+        join_kernel,
+        in_specs=[vm, vm],
+        out_specs=[vm, vm],
         out_shape=[
             jax.ShapeDtypeStruct((rows, HD), jnp.bfloat16),
             jax.ShapeDtypeStruct((rows, HD), jnp.float32),
         ],
         compiler_params=pltpu.CompilerParams(vmem_limit_bytes=VMEM),
-        cost_estimate=pl.CostEstimate(
-            flops=2 * rows * D * HD, bytes_accessed=2 * D * (rows + HD), transcendentals=rows
-        ),
-        name="project_kv",
-    )(core, mine, theirs, *([] if tail is None else [tail]), gain, wk_m, wk_t)
+        name="join_kv",
+    )(part, swap(part))
 
 
 def project_q(core, mine, theirs, tail, gain, wq, inverse, lengths):
@@ -206,7 +216,7 @@
         grid_spec=pltpu.PrefetchScalarGridSpec(
             num_scalar_prefetch=1,
             grid=(STEPS,),
-            in_specs=x_specs(mine, tail)
+            in_specs=x_specs([mine, theirs], tail)
             + [
                 pl.BlockSpec((PER, 1, FS, FS), lambda i, c: (i, c[0], 0, 0)),
                 pl.BlockSpec((PER, 1, FS, FS), lambda i, c: (i, 1 - c[0], 0, 0)),
@@ -339,12 +349,11 @@
     x = rollout[:rows]
 
     mine, tail = gather_rows(x)
-    if tail is not None:
-        mine, tail = lax.optimization_barrier((mine, tail))
-    theirs = swap(mine)
     gain = norm_gain.reshape(NT, 1, FS)
     wk = keyval_weight.T
-    keyval, inverse = project_kv(core, mine, theirs, tail, gain, wk, swap(wk))
+    mine, tail, wk_theirs = lax.optimization_barrier((mine, tail, swap(wk)))
+    theirs = swap(mine)
+    keyval, inverse = project_kv(core, mine, tail, gain, wk, wk_theirs)
     first = lax.ppermute(keyval, "tensor", kv_pairs(True))
     second = lax.ppermute(keyval, "tensor", kv_pairs(False))
     q, cosine, sine, bias = project_q(core, mine, theirs, tail, gain, query_weight, inverse, lengths)

time: 146 us -> 143 us (0.979)
  Pallas kernels: 19.2 us -> 12.3 us
  starting transfers between devices: 34.2 us -> 37.4 us
  other arithmetic: 6.03 us -> 4.5 us
    pallas_call x2, Pallas kernels: 6.74 us -> 2.95 us  [out_project(): pl.pallas_call(out_kernel, grid_spec=pltpu.PrefetchScalarGridSpec(num_sca...]
    ppermute x4 -> x5, starting transfers between devices: 8.28 us -> 10.7 us  [swap(): return lax.ppermute(v, 'tensor', SWAP)]
    ppermute x1, waiting for transfers between devices: 3.23 us -> 5.08 us  [sum_over_chips(): below = lax.ppermute(up, 'tensor', [(t, (t + 2) % NT) for t in range(NT)])]
  transfers between devices with their start and end apart: 10 -> 11, of which waited for: 7 -> 7; matrix products, arithmetic and copies ran while one was open for 3% -> 3% of each run, Pallas kernels for 11% -> 7%
where the time goes in v4:
time: 143 us; the launch traced here: 142 us
  blocking collectives  40.5 us (28%)
  waiting for transfers between devices  39.6 us (28%)
  starting transfers between devices  37.4 us (26%)
  Pallas kernels  12.3 us (9%)
  other arithmetic  4.5 us (3%)
  local copies, waits for them, and re-layouts  3.91 us (3%)
  between operations  2 us (1%)
  matrix products  1.78 us (1%)
    all_gather x1, blocking collectives, gather_rows(): lax.all_gather(x[:AG_ROWS], 'tensor', axis=0, axis_index_groups=Z_GROUPS)  40.5 us
    all_to_all x1, waiting for transfers between devices, sum_over_chips(): lax.all_to_all(three.astype(jnp.bfloat16), 'tensor', split_axis=0, concat...  18.2 us
    ppermute x5, starting transfers between devices, swap(): return lax.ppermute(v, 'tensor', SWAP)  10.7 us
    all_to_all x1, starting transfers between devices, body(): lax.all_to_all(outgoing.reshape(RPS, MAXLEN, FS), 'dp', split_axis=0, con...  10.2 us
    all_to_all x1, waiting for transfers between devices, body(): lax.all_to_all(outgoing.reshape(RPS, MAXLEN, FS), 'dp', split_axis=0, con...  7.19 us
    ppermute x1, waiting for transfers between devices, layer(): second = lax.ppermute(keyval, 'tensor', kv_pairs(False))  5.48 us
    ppermute x1, starting transfers between devices, sum_over_chips(): above = lax.ppermute(down, 'tensor', [(t, (t - 2) % NT) for t in range(NT)])  5.26 us
    ppermute x1, waiting for transfers between devices, sum_over_chips(): below = lax.ppermute(up, 'tensor', [(t, (t + 2) % NT) for t in range(NT)])  5.08 us
  transfers between devices with their start and end apart: 11, of which 7 were waited for; matrix products, arithmetic and copies ran while one was open for 3% of the time, Pallas kernels for 7%

profile of v4, /device:TPU:8, one launch (start us, length us, event | category | flops | bytes accessed | tf_op | source)
XLA Modules:
  0.0 142.3 jit_solution(4299120208483072916)
XLA Ops:
  3.4 118.2 %conditional.2 = (bf16[256,256]{1,0:T(8,128)(2,1)}) conditional(s32[]{:T(128)} %clamp.3, (s32[1024]{0:T(1024)}, s32[32,32]{1,0:T(8,128)}, bf16[256,256]{1,0:T(8,128)(2,1)}, bf16[6144,64]{0,1:T(8,128)(2,1)}, f32[6144]{0:T(1024)}, /*index=5*/bf16[6144,256]{1,0:T(8,128)(2,1)}, f32[8,128]{1,0:T(8,128)}, ...), branch_computations={%region_7.13_spmd, %region_13.19_spmd, %region_19.25_spmd, %region... | conditional | flops 1914927872 | bytes 91720408
  3.5 2.1 %collective-permute-start.6 = (bf16[256,6144]{1,0:T(8,128)(2,1)}, bf16[256,6144]{1,0:T(8,128)(2,1)S(1)}, u32[]{:S(2)}, u32[]{:S(2)}) collective-permute-start(bf16[256,6144]{1,0:T(8,128)(2,1)} %get-tuple-element.100.rest_0_.rest_1_.rest_2_.rest_3_), channel_id=1, source_target_pairs={{0,1},{1,0},{2,3},{3,2},{4,5},{5,4},{6,7},{7,6},{8,9},{9,8},{10,11... | collective-permute-start | bytes 9437192 | tf_op jit(solution)/shard_map/cond/branch_0_fun/ppermute | solution.py:75
  5.5 2.4 %collective-permute-start = (bf16[64,6144]{1,0:T(8,128)(2,1)}, bf16[64,6144]{1,0:T(8,128)(2,1)S(1)}, u32[]{:S(2)}, u32[]{:S(2)}) collective-permute-start(bf16[64,6144]{1,0:T(8,128)(2,1)} %bitcast.77), channel_id=1, source_target_pairs={{0,1},{1,0},{2,3},{3,2},{4,5},{5,4},{6,7},{7,6},{8,9},{9,8},{10,11... | collective-permute-start | bytes 2359304 | tf_op jit(solution)/shard_map/cond/branch_0_fun/ppermute | solution.py:75
  8.9 40.5 %all-gather = bf16[2016,256]{1,0:T(8,128)(2,1)} all-gather(bf16[168,256]{1,0:T(8,128)(2,1)S(1)} %slice.22), channel_id=2, replica_groups={{0,2,4,6,8,10,12,14,16,18,20,22},{1,3,5,7,9,11,13,15,17,19,21,23},{24,2..., dimensions={0}, use_global_device_ids=true | all-gather | bytes 1118208 | tf_op jit(solution)/shard_map/cond/branch_0_fun/all_gather | solution.py:342
  50.2 1.9 %collective-permute-start.1 = (bf16[12,168,256]{2,1,0:T(8,128)(2,1)}, bf16[12,168,256]{2,1,0:T(8,128)(2,1)}, u32[]{:S(2)}, u32[]{:S(2)}) collective-permute-start(bf16[12,168,256]{2,1,0:T(8,128)(2,1)} %bitcast.5.mine), channel_id=1, source_target_pairs={{0,1},{1,0},{2,3},{3,2},{4,5},{5,4},{6,7},{7,6},{8,9},{9,8},{10,11... | collective-permute-start | bytes 3096584 | tf_op jit(solution)/shard_map/cond/branch_0_fun/ppermute | solution.py:75
  52.3 1.1 copy-done.9
  53.4 3.6 %project_kv.4.mine = f32[168,256]{1,0:T(8,128)S(1)} custom-call(s32[4]{0:T(128)S(1)} %pad_add_fusion.core.place, bf16[12,168,256]{2,1,0:T(8,128)(2,1)} %bitcast.5.mine, f32[24,1,256]{2,1,0:T(1,128)} %bitcast.85, bf16[64,6144]{1,0:T(8,128)(2,1)} %bitcast.78, bf16[64,6144]{1,0:T(8,128)(2,1)S(1)} %copy-done.9), custom_call_target="tpu_custom_call" | custom-call | flops 132120576 | bytes 2605056 | tf_op jit(solution)/shard_map/cond/branch_0_fun/project_kv/pallas_call | solution.py:179
  57.1 2.4 %collective-permute-start.2 = (f32[168,256]{1,0:T(8,128)S(1)}, f32[168,256]{1,0:T(8,128)S(1)}, u32[]{:S(2)}, u32[]{:S(2)}) collective-permute-start(f32[168,256]{1,0:T(8,128)S(1)} %project_kv.4.mine), channel_id=1, source_target_pairs={{0,1},{1,0},{2,3},{3,2},{4,5},{5,4},{6,7},{7,6},{8,9},{9,8},{10,11... | collective-permute-start | bytes 516104 | tf_op jit(solution)/shard_map/cond/branch_0_fun/ppermute | solution.py:75
  59.5 1.0 collective-permute-done.2.theirs
  61.3 4.0 %collective-permute-start.4 = (bf16[168,128]{1,0:T(8,128)(2,1)S(1)}, bf16[168,128]{1,0:T(8,128)(2,1)S(1)}, u32[]{:S(2)}, u32[]{:S(2)}) collective-permute-start(bf16[168,128]{1,0:T(8,128)(2,1)S(1)} %get-tuple-element.96), channel_id=1, source_target_pairs={{0,2},{1,3},{2,6},{3,7},{4,10},{5,11},{6,14},{7,15},{8,18},{9,19},... | collective-permute-start | bytes 129032 | tf_op jit(solution)/shard_map/cond/branch_0_fun/ppermute | solution.py:358
  65.4 4.1 %project_q.4 = (bf16[168,256]{1,0:T(8,128)(2,1)S(1)}, f32[168,128]{1,0:T(8,128)S(1)}, f32[168,128]{1,0:T(8,128)S(1)}, f32[168,168]{1,0:T(8,128)S(1)}) custom-call(s32[4]{0:T(128)S(1)} %pad_add_fusion.core.place, bf16[12,168,256]{2,1,0:T(8,128)(2,1)} %bitcast.5.mine, bf16[12,168,256]{2,1,0:T(8,128)(2,1)} %collective-permute-done.1.theirs, ...), custom_call_target="tpu_custom_call" | custom-call | flops 528482304 | bytes 5210112 | tf_op jit(solution)/shard_map/cond/branch_0_fun/project_q/pallas_call | solution.py:214
  69.5 5.5 %collective-permute-done.4.second = bf16[168,128]{1,0:T(8,128)(2,1)S(1)} collective-permute-done((bf16[168,128]{1,0:T(8,128)(2,1)S(1)}, bf16[168,128]{1,0:T(8,128)(2,1)S(1)}, u32[]{:S(2)}, u32[]{:S(2)}) %collective-permute-start.4) | collective-permute-done | bytes 43040 | tf_op jit(solution)/shard_map/cond/branch_0_fun/ppermute | solution.py:358
  75.0 1.4 %attend.4.mine = bf16[168,256]{1,0:T(8,128)(2,1)S(1)} custom-call(s32[4]{0:T(128)S(1)} %pad_add_fusion.core.place, bf16[168,256]{1,0:T(8,128)(2,1)S(1)} %get-tuple-element.95.q_ref, bf16[168,128]{1,0:T(8,128)(2,1)S(1)} %collective-permute-done.3.first, bf16[168,128]{1,0:T(8,128)(2,1)S(1)} %collective-permute-done.4.second, ...), custom_call_target="tpu_custom_call" | custom-call | flops 28901376 | bytes 172032 | tf_op jit(solution)/shard_map/cond/branch_0_fun/attend/pallas_call | solution.py:271
  76.5 1.9 %collective-permute-start.5 = (bf16[168,256]{1,0:T(8,128)(2,1)S(1)}, bf16[168,256]{1,0:T(8,128)(2,1)S(1)}, u32[]{:S(2)}, u32[]{:S(2)}) collective-permute-start(bf16[168,256]{1,0:T(8,128)(2,1)S(1)} %attend.4.mine), channel_id=1, source_target_pairs={{0,1},{1,0},{2,3},{3,2},{4,5},{5,4},{6,7},{7,6},{8,9},{9,8},{10,11... | collective-permute-start | bytes 258056 | tf_op jit(solution)/shard_map/cond/branch_0_fun/ppermute | solution.py:75
  78.4 1.2 collective-permute-done.5.theirs
  79.6 2.0 %out_project.9 = (bf16[4,168,256]{2,1,0:T(8,128)(2,1)S(1)}, bf16[4,168,256]{2,1,0:T(8,128)(2,1)S(1)}) custom-call(s32[4]{0:T(128)S(1)} %pad_add_fusion.core.place, bf16[168,256]{1,0:T(8,128)(2,1)S(1)} %attend.4.mine, bf16[168,256]{1,0:T(8,128)(2,1)S(1)} %collective-permute-done.5.theirs, bf16[256,6144]{1,0:T(8,128)(2,1)S(1)} %copy-done.12, ...), custom_call_target="tpu_custom_call" | custom-call | flops 352321536 | bytes 2785280 | tf_op jit(solution)/shard_map/cond/branch_0_fun/out_project/pallas_call | solution.py:304
  81.7 1.9 %collective-permute-start.7 = (bf16[4,168,256]{2,1,0:T(8,128)(2,1)S(1)}, bf16[4,168,256]{2,1,0:T(8,128)(2,1)S(1)}, u32[]{:S(2)}, u32[]{:S(2)}) collective-permute-start(bf16[4,168,256]{2,1,0:T(8,128)(2,1)S(1)} %get-tuple-element.101), channel_id=1, source_target_pairs={{0,2},{1,3},{2,4},{3,5},{4,6},{5,7},{6,8},{7,9},{8,10},{9,11},{10,... | collective-permute-start | bytes 1032200 | tf_op jit(solution)/shard_map/cond/branch_0_fun/ppermute | solution.py:325
  83.6 5.3 %collective-permute-start.8 = (bf16[4,168,256]{2,1,0:T(8,128)(2,1)S(1)}, bf16[4,168,256]{2,1,0:T(8,128)(2,1)S(1)}, u32[]{:S(2)}, u32[]{:S(2)}) collective-permute-start(bf16[4,168,256]{2,1,0:T(8,128)(2,1)S(1)} %get-tuple-element.102), channel_id=1, source_target_pairs={{0,22},{1,23},{2,0},{3,1},{4,2},{5,3},{6,4},{7,5},{8,6},{9,7},{10,... | collective-permute-start | bytes 1032200 | tf_op jit(solution)/shard_map/cond/branch_0_fun/ppermute | solution.py:326
  89.8 5.1 %collective-permute-done.7 = bf16[4,168,256]{2,1,0:T(8,128)(2,1)S(1)} collective-permute-done((bf16[4,168,256]{2,1,0:T(8,128)(2,1)S(1)}, bf16[4,168,256]{2,1,0:T(8,128)(2,1)S(1)}, u32[]{:S(2)}, u32[]{:S(2)}) %collective-permute-start.7) | collective-permute-done | bytes 344096 | tf_op jit(solution)/shard_map/cond/branch_0_fun/ppermute | solution.py:325
  94.9 1.3 collective-permute-done.8
  97.1 4.7 %all-to-all-start = ((bf16[4,168,256]{2,1,0:T(8,128)(2,1)}), bf16[4,168,256]{2,1,0:T(8,128)(2,1)S(1)}, u32[]{:S(2)}, u32[]{:S(2)}) async-start(bf16[4,168,256]{2,1,0:T(8,128)(2,1)} %add_convert_fusion), calls=%async_computation | async-start | bytes 688128 | tf_op jit(solution)/shard_map/cond/branch_0_fun/all_to_all | solution.py:329
  102.5 18.2 %all-to-all-done = bf16[4,168,256]{2,1,0:T(8,128)(2,1)S(1)} async-done(((bf16[4,168,256]{2,1,0:T(8,128)(2,1)}), bf16[4,168,256]{2,1,0:T(8,128)(2,1)S(1)}, u32[]{:S(2)}, u32[]{:S(2)}) %all-to-all-start) | async-done | bytes 344096 | tf_op jit(solution)/shard_map/cond/branch_0_fun/all_to_all | solution.py:329
  121.7 10.2 %all-to-all-start.7 = ((bf16[32,8,256]{2,1,0:T(8,128)(2,1)}), bf16[32,8,256]{2,1,0:T(8,128)(2,1)S(1)}, u32[]{:S(2)}, u32[]{:S(2)}) async-start(bf16[32,8,256]{2,1,0:T(8,128)(2,1)} %bitcast.58), calls=%async_computation.7 | async-start | bytes 262144 | tf_op jit(solution)/shard_map/all_to_all | solution.py:391
  134.2 7.2 %all-to-all-done.7 = bf16[32,8,256]{2,1,0:T(8,128)(2,1)S(1)} async-done(((bf16[32,8,256]{2,1,0:T(8,128)(2,1)}), bf16[32,8,256]{2,1,0:T(8,128)(2,1)S(1)}, u32[]{:S(2)}, u32[]{:S(2)}) %all-to-all-start.7) | async-done | bytes 131104 | tf_op jit(solution)/shard_map/all_to_all | solution.py:391
  (53 shorter events, 10.8 us)
Async XLA Ops:
  3.4 61.9 %copy-start.22 = (f32[6144]{0:T(1024)S(1)}, f32[6144]{0:T(1024)}, u32[]{:S(2)}) copy-start(f32[6144]{0:T(1024)} %get-tuple-element.89) | copy-start | bytes 73732 | tf_op jit(solution)/shard_map/conditional
  3.4 61.9 %copy-start.26 = (s32[32,32]{1,0:T(8,128)S(1)}, s32[32,32]{1,0:T(8,128)}, u32[]{:S(2)}) copy-start(s32[32,32]{1,0:T(8,128)} %get-tuple-element.85.rest_4_) | copy-start | bytes 12292 | tf_op jit(solution)/shard_map/conditional
  3.5 61.9 %copy-start.34 = (f32[8,128]{1,0:T(8,128)S(1)}, f32[8,128]{1,0:T(8,128)}, u32[]{:S(2)}) copy-start(f32[8,128]{1,0:T(8,128)} %get-tuple-element.93.rest_5_) | copy-start | bytes 12292 | tf_op jit(solution)/shard_map/conditional
  3.5 61.9 %copy-start.38 = (f32[8,128]{1,0:T(8,128)S(1)}, f32[8,128]{1,0:T(8,128)}, u32[]{:S(2)}) copy-start(f32[8,128]{1,0:T(8,128)} %get-tuple-element.94.rest_6_) | copy-start | bytes 12292 | tf_op jit(solution)/shard_map/conditional
  3.5 76.1 %collective-permute-start.6 = (bf16[256,6144]{1,0:T(8,128)(2,1)}, bf16[256,6144]{1,0:T(8,128)(2,1)S(1)}, u32[]{:S(2)}, u32[]{:S(2)}) collective-permute-start(bf16[256,6144]{1,0:T(8,128)(2,1)} %get-tuple-element.100.rest_0_.rest_1_.rest_2_.rest_3_), channel_id=1, source_target_pairs={{0,1},{1,0},{2,3},{3,2},{4,5},{5,4},{6,7},{7,6},{8,9},{9,8},{10,11... | collective-permute-start | bytes 9437192 | tf_op jit(solution)/shard_map/cond/branch_0_fun/ppermute | solution.py:75
  5.5 43.8 %collective-permute-start = (bf16[64,6144]{1,0:T(8,128)(2,1)}, bf16[64,6144]{1,0:T(8,128)(2,1)S(1)}, u32[]{:S(2)}, u32[]{:S(2)}) collective-permute-start(bf16[64,6144]{1,0:T(8,128)(2,1)} %bitcast.77), channel_id=1, source_target_pairs={{0,1},{1,0},{2,3},{3,2},{4,5},{5,4},{6,7},{7,6},{8,9},{9,8},{10,11... | collective-permute-start | bytes 2359304 | tf_op jit(solution)/shard_map/cond/branch_0_fun/ppermute | solution.py:75
  49.4 0.9 copy-start.8
  50.2 15.0 %collective-permute-start.1 = (bf16[12,168,256]{2,1,0:T(8,128)(2,1)}, bf16[12,168,256]{2,1,0:T(8,128)(2,1)}, u32[]{:S(2)}, u32[]{:S(2)}) collective-permute-start(bf16[12,168,256]{2,1,0:T(8,128)(2,1)} %bitcast.5.mine), channel_id=1, source_target_pairs={{0,1},{1,0},{2,3},{3,2},{4,5},{5,4},{6,7},{7,6},{8,9},{9,8},{10,11... | collective-permute-start | bytes 3096584 | tf_op jit(solution)/shard_map/cond/branch_0_fun/ppermute | solution.py:75
  52.3 1.1 copy-start.9
  53.4 11.9 %copy-start.16 = (bf16[6144,256]{1,0:T(8,128)(2,1)S(1)}, bf16[6144,256]{1,0:T(8,128)(2,1)}, u32[]{:S(2)}) copy-start(bf16[6144,256]{1,0:T(8,128)(2,1)} %get-tuple-element.90) | copy-start | bytes 9437188 | tf_op jit(solution)/shard_map/conditional
  57.1 3.4 %collective-permute-start.2 = (f32[168,256]{1,0:T(8,128)S(1)}, f32[168,256]{1,0:T(8,128)S(1)}, u32[]{:S(2)}, u32[]{:S(2)}) collective-permute-start(f32[168,256]{1,0:T(8,128)S(1)} %project_kv.4.mine), channel_id=1, source_target_pairs={{0,1},{1,0},{2,3},{3,2},{4,5},{5,4},{6,7},{7,6},{8,9},{9,8},{10,11... | collective-permute-start | bytes 516104 | tf_op jit(solution)/shard_map/cond/branch_0_fun/ppermute | solution.py:75
  60.6 8.9 %collective-permute-start.3 = (bf16[168,128]{1,0:T(8,128)(2,1)S(1)}, bf16[168,128]{1,0:T(8,128)(2,1)S(1)}, u32[]{:S(2)}, u32[]{:S(2)}) collective-permute-start(bf16[168,128]{1,0:T(8,128)(2,1)S(1)} %get-tuple-element.96), channel_id=1, source_target_pairs={{0,0},{1,1},{2,4},{3,5},{4,8},{5,9},{6,12},{7,13},{8,16},{9,17},{1... | collective-permute-start | bytes 129032 | tf_op jit(solution)/shard_map/cond/branch_0_fun/ppermute | solution.py:357
  61.3 13.7 %collective-permute-start.4 = (bf16[168,128]{1,0:T(8,128)(2,1)S(1)}, bf16[168,128]{1,0:T(8,128)(2,1)S(1)}, u32[]{:S(2)}, u32[]{:S(2)}) collective-permute-start(bf16[168,128]{1,0:T(8,128)(2,1)S(1)} %get-tuple-element.96), channel_id=1, source_target_pairs={{0,2},{1,3},{2,6},{3,7},{4,10},{5,11},{6,14},{7,15},{8,18},{9,19},... | collective-permute-start | bytes 129032 | tf_op jit(solution)/shard_map/cond/branch_0_fun/ppermute | solution.py:358
  65.3 14.3 %copy-start.12 = (bf16[256,6144]{1,0:T(8,128)(2,1)S(1)}, bf16[256,6144]{1,0:T(8,128)(2,1)}, u32[]{:S(2)}) copy-start(bf16[256,6144]{1,0:T(8,128)(2,1)} %get-tuple-element.100.rest_0_.rest_1_.rest_2_.rest_3_) | copy-start | bytes 9437188 | tf_op jit(solution)/shard_map/conditional
  76.5 3.2 %collective-permute-start.5 = (bf16[168,256]{1,0:T(8,128)(2,1)S(1)}, bf16[168,256]{1,0:T(8,128)(2,1)S(1)}, u32[]{:S(2)}, u32[]{:S(2)}) collective-permute-start(bf16[168,256]{1,0:T(8,128)(2,1)S(1)} %attend.4.mine), channel_id=1, source_target_pairs={{0,1},{1,0},{2,3},{3,2},{4,5},{5,4},{6,7},{7,6},{8,9},{9,8},{10,11... | collective-permute-start | bytes 258056 | tf_op jit(solution)/shard_map/cond/branch_0_fun/ppermute | solution.py:75
  81.7 13.2 %collective-permute-start.7 = (bf16[4,168,256]{2,1,0:T(8,128)(2,1)S(1)}, bf16[4,168,256]{2,1,0:T(8,128)(2,1)S(1)}, u32[]{:S(2)}, u32[]{:S(2)}) collective-permute-start(bf16[4,168,256]{2,1,0:T(8,128)(2,1)S(1)} %get-tuple-element.101), channel_id=1, source_target_pairs={{0,2},{1,3},{2,4},{3,5},{4,6},{5,7},{6,8},{7,9},{8,10},{9,11},{10,... | collective-permute-start | bytes 1032200 | tf_op jit(solution)/shard_map/cond/branch_0_fun/ppermute | solution.py:325
  83.6 18.2 %copy-start.30 = (s32[1024]{0:T(1024)S(1)}, s32[1024]{0:T(1024)}, u32[]{:S(2)}) copy-start(s32[1024]{0:T(1024)} %get-tuple-element.84) | copy-start | bytes 12292 | tf_op jit(solution)/shard_map/conditional
  83.6 37.1 %copy-start.18 = (bf16[256,256]{1,0:T(8,128)(2,1)S(1)}, bf16[256,256]{1,0:T(8,128)(2,1)}, u32[]{:S(2)}) copy-start(bf16[256,256]{1,0:T(8,128)(2,1)} %get-tuple-element.86) | copy-start | bytes 393220 | tf_op jit(solution)/shard_map/conditional
  83.6 12.6 %collective-permute-start.8 = (bf16[4,168,256]{2,1,0:T(8,128)(2,1)S(1)}, bf16[4,168,256]{2,1,0:T(8,128)(2,1)S(1)}, u32[]{:S(2)}, u32[]{:S(2)}) collective-permute-start(bf16[4,168,256]{2,1,0:T(8,128)(2,1)S(1)} %get-tuple-element.102), channel_id=1, source_target_pairs={{0,22},{1,23},{2,0},{3,1},{4,2},{5,3},{6,4},{7,5},{8,6},{9,7},{10,... | collective-permute-start | bytes 1032200 | tf_op jit(solution)/shard_map/cond/branch_0_fun/ppermute | solution.py:326
  97.1 23.6 %all-to-all-start = ((bf16[4,168,256]{2,1,0:T(8,128)(2,1)}), bf16[4,168,256]{2,1,0:T(8,128)(2,1)S(1)}, u32[]{:S(2)}, u32[]{:S(2)}) async-start(bf16[4,168,256]{2,1,0:T(8,128)(2,1)} %add_convert_fusion), calls=%async_computation | async-start | bytes 688128 | tf_op jit(solution)/shard_map/cond/branch_0_fun/all_to_all | solution.py:329
  121.7 19.7 %all-to-all-start.7 = ((bf16[32,8,256]{2,1,0:T(8,128)(2,1)}), bf16[32,8,256]{2,1,0:T(8,128)(2,1)S(1)}, u32[]{:S(2)}, u32[]{:S(2)}) async-start(bf16[32,8,256]{2,1,0:T(8,128)(2,1)} %bitcast.58), calls=%async_computation.7 | async-start | bytes 262144 | tf_op jit(solution)/shard_map/all_to_all | solution.py:391

commit v5 on v4

--- a/solution.py
+++ b/solution.py
@@ -320,26 +320,108 @@
     )(place, mine, theirs, *[w_mine] * FAR, *[w_theirs] * FAR)
 
 
-def sum_over_chips(place, context, theirs, w_mine, w_theirs):
+def sum_over_chips(place, context, theirs, w_mine, w_theirs, lengths, packing):
     up, down = out_project(place, context, theirs, w_mine, w_theirs, (1, 2))
+    up, lengths, packing = lax.optimization_barrier((up, lengths, packing))
+    picks = make_picks(place, lengths, packing, context.shape[0])
     below = lax.ppermute(up, "tensor", [(t, (t + 2) % NT) for t in range(NT)])
     above = lax.ppermute(down, "tensor", [(t, (t - 2) % NT) for t in range(NT)])
     (own,) = out_project(place, context, theirs, w_mine, w_theirs, (0,))
     three = own.astype(jnp.float32) + below.astype(jnp.float32) + above.astype(jnp.float32)
+    three, *picks = lax.optimization_barrier((three.astype(jnp.bfloat16), *picks))
     parts = lax.all_to_all(
-        three.astype(jnp.bfloat16), "tensor", split_axis=0, concat_axis=0, tiled=True,
+        three, "tensor", split_axis=0, concat_axis=0, tiled=True,
         axis_index_groups=FAR_GROUPS,
     )
-    return jnp.sum(parts.astype(jnp.float32), axis=0)
-
-
-def gather_rows(x):
-    rows = x.shape[0]
-    tail = None
-    if rows > AG_ROWS:
-        last = jnp.broadcast_to(x[AG_ROWS:][None], (NT, rows - AG_ROWS, FS))
+    return jnp.sum(parts.astype(jnp.float32), axis=0), *picks
+
+
+def split_kernel(x_ref, head, tail):
+    head[...] = x_ref[:AG_ROWS]
+    last = x_ref[AG_ROWS : AG_ROWS + tail.shape[1]]
+    for t in range(NT):
+        tail[t] = last
+
+
+def gather_rows(rollout, rows):
+    if rows == AG_ROWS:
+        head, tail = rollout[:rows], None
+    else:
+        vm = pl.BlockSpec(memory_space=pltpu.VMEM)
+        head, last = pl.pallas_call(
+            split_kernel,
+            in_specs=[vm],
+            out_specs=[vm, vm],
+            out_shape=[
+                jax.ShapeDtypeStruct((AG_ROWS, FS), jnp.bfloat16),
+                jax.ShapeDtypeStruct((NT, rows - AG_ROWS, FS), jnp.bfloat16),
+            ],
+            compiler_params=pltpu.CompilerParams(vmem_limit_bytes=VMEM),
+            name="split_rows",
+        )(rollout)
         tail = lax.all_to_all(last, "tensor", split_axis=0, concat_axis=0, tiled=True)
-    return lax.all_gather(x[:AG_ROWS], "tensor", axis=0, axis_index_groups=Z_GROUPS), tail
+    return lax.all_gather(head, "tensor", axis=0, axis_index_groups=Z_GROUPS), tail
+
+
+def along_lanes(row):
+    first = lax.broadcasted_iota(jnp.int32, (RPS, RPS), 0)
+    second = lax.broadcasted_iota(jnp.int32, (RPS, RPS), 1)
+    column = jnp.sum(jnp.where(first == second, row, 0.0), axis=1, keepdims=True)
+    return jnp.sum(jnp.where(first <= second, column, 0.0), axis=0, keepdims=True)
+
+
+def picks_kernel(core, lengths, pack, out_pick, in_pick):
+    here = core[3]
+    slots = RPS * MAXLEN
+    lane = lax.broadcasted_iota(jnp.int32, (RPS, RPS), 1)
+    sub = lax.broadcasted_iota(jnp.int32, (RPS, RPS), 0)
+    own = lengths[pl.ds(here, 1), :].astype(jnp.float32)
+    start = along_lanes(own) - own
+    packed = pack[...]
+    which = jnp.sum(jnp.where(packed // RPS == here, (packed % RPS).astype(jnp.float32), 0.0), axis=1, keepdims=True)
+    chosen = which == lane.astype(jnp.float32)
+    o_start = jnp.sum(jnp.where(chosen, start, 0.0), axis=1, keepdims=True)
+    o_len = jnp.sum(jnp.where(chosen, own, 0.0), axis=1, keepdims=True)
+    wide = lax.broadcasted_iota(jnp.int32, (RPS, 128), 1)
+    both = jnp.where(wide == 0, o_start, jnp.where(wide == 1, o_len, 0.0)).astype(jnp.bfloat16)
+    owner_of = lax.broadcasted_iota(jnp.int32, (slots, RPS), 0) // MAXLEN
+    spread = jnp.where(owner_of == lax.broadcasted_iota(jnp.int32, (slots, RPS), 1), 1.0, 0.0).astype(jnp.bfloat16)
+    both = jnp.dot(spread, both, preferred_element_type=jnp.float32)
+    slot = (lax.broadcasted_iota(jnp.int32, (slots, 1), 0) % MAXLEN).astype(jnp.float32)
+    row = jnp.where(slot < both[:, 1:2], both[:, 0:1] + slot, -1.0)
+    places = lax.broadcasted_iota(jnp.int32, out_pick.shape, 1).astype(jnp.float32)
+    out_pick[...] = jnp.where(places == row, 1.0, 0.0).astype(jnp.bfloat16)
+    mine = pack[pl.ds(here, 1), :]
+    from_source = mine // RPS
+    is_source = jnp.where(sub == from_source, 1.0, 0.0).astype(jnp.bfloat16)
+    by_k = lax.dot_general(
+        lengths[...].astype(jnp.float32).astype(jnp.bfloat16), is_source, (((0,), (0,)), ((), ())),
+        preferred_element_type=jnp.float32,
+    )
+    length = jnp.sum(jnp.where(sub == mine % RPS, by_k, 0.0), axis=0, keepdims=True)
+    end = along_lanes(length)
+    begin = end - length
+    place = lax.broadcasted_iota(jnp.int32, (slots, RPS), 0).astype(jnp.float32)
+    inside = (place >= begin) & (place < end)
+    at = jnp.where(inside, from_source.astype(jnp.float32) * MAXLEN + place - begin + 1.0, 0.0)
+    at = jnp.sum(at, axis=1, keepdims=True) - 1.0
+    arrived = lax.broadcasted_iota(jnp.int32, in_pick.shape, 1).astype(jnp.float32)
+    in_pick[...] = jnp.where(arrived == at, 1.0, 0.0).astype(jnp.bfloat16)
+
+
+def make_picks(core, lengths, packing, rows):
+    vm = pl.BlockSpec(memory_space=pltpu.VMEM)
+    return pl.pallas_call(
+        picks_kernel,
+        in_specs=[pl.BlockSpec(memory_space=pltpu.SMEM), vm, vm],
+        out_specs=[vm, vm],
+        out_shape=[
+            jax.ShapeDtypeStruct((RPS * MAXLEN, rows), jnp.bfloat16),
+            jax.ShapeDtypeStruct((RPS * MAXLEN, RPS * MAXLEN), jnp.bfloat16),
+        ],
+        compiler_params=pltpu.CompilerParams(vmem_limit_bytes=VMEM),
+        name="make_picks",
+    )(core, lengths, packing.reshape(RPS, RPS))
 
 
 def layer(rows, rollout, lengths, packing, norm_gain, query_weight, keyval_weight, out_weight):
@@ -348,7 +430,7 @@
     core = jnp.stack([tensor_index % 2, tensor_index // 2 % 3, tensor_index // 2 % 2, source]).astype(jnp.int32)
     x = rollout[:rows]
 
-    mine, tail = gather_rows(x)
+    mine, tail = gather_rows(rollout, rows)
     gain = norm_gain.reshape(NT, 1, FS)
     wk = keyval_weight.T
     mine, tail, wk_theirs = lax.optimization_barrier((mine, tail, swap(wk)))
@@ -358,55 +440,25 @@
     second = lax.ppermute(keyval, "tensor", kv_pairs(False))
     q, cosine, sine, bias = project_q(core, mine, theirs, tail, gain, query_weight, inverse, lengths)
     context = attend(core, q, first, second, cosine, sine, bias)
-    summed = sum_over_chips(core, context, swap(context), out_weight, swap(out_weight))
-    my_len = lax.dynamic_index_in_dim(lengths, source, 0, keepdims=False)
-    earlier = jnp.arange(RPS)[None, :] < jnp.arange(RPS)[:, None]
-    start = jnp.sum(jnp.where(earlier, my_len[None, :], 0), axis=1)
-    places = jnp.arange(rows, dtype=jnp.int32)
+    summed, out_pick, in_pick = sum_over_chips(
+        core, context, swap(context), out_weight, swap(out_weight), lengths, packing
+    )
     result = (summed + x.astype(jnp.float32)).astype(jnp.bfloat16)
-
-    pack = packing.reshape(RPS, RPS)
-    of_mine = pack // RPS == source
-    which = jnp.sum(jnp.where(of_mine, pack % RPS, 0), axis=1)
-    chosen = which[:, None] == jnp.arange(RPS)[None, :]
-    o_start = jnp.sum(jnp.where(chosen, start[None, :], 0), axis=1)
-    o_len = jnp.sum(jnp.where(chosen, my_len[None, :], 0), axis=1)
-    slot = jnp.arange(MAXLEN, dtype=jnp.int32)
-    row_of = jnp.where(slot[None, :] < o_len[:, None], o_start[:, None] + slot[None, :], -1).reshape(-1)
-    pick = (row_of[:, None] == places[None, :]).astype(jnp.bfloat16)
-    outgoing = jnp.dot(pick, result, preferred_element_type=jnp.float32).astype(jnp.bfloat16)
-    return outgoing
+    outgoing = jnp.dot(out_pick, result, preferred_element_type=jnp.float32).astype(jnp.bfloat16)
+    incoming = lax.all_to_all(
+        outgoing.reshape(RPS, MAXLEN, FS), "dp", split_axis=0, concat_axis=0, tiled=True
+    ).reshape(RPS * MAXLEN, FS)
+    return jnp.dot(in_pick, incoming, preferred_element_type=jnp.float32).astype(jnp.bfloat16)
 
 
 def body(rollout, lengths, packing, norm_gain, query_weight, keyval_weight, out_weight):
-    owner = lax.axis_index("dp")
-    total = rollout.shape[0]
     longest = jnp.max(jnp.sum(lengths, axis=1))
     size = sum((longest > cap).astype(jnp.int32) for cap in CAPS[:-1])
-    outgoing = lax.switch(
+    return lax.switch(
         size,
         [functools.partial(layer, cap) for cap in CAPS],
         rollout, lengths, packing, norm_gain, query_weight, keyval_weight, out_weight,
     )
-    incoming = lax.all_to_all(
-        outgoing.reshape(RPS, MAXLEN, FS), "dp", split_axis=0, concat_axis=0, tiled=True
-    ).reshape(RPS * MAXLEN, FS)
-
-    chosen = lax.dynamic_index_in_dim(packing.reshape(RPS, RPS), owner, 0, keepdims=False)
-    from_source = chosen // RPS
-    is_source = from_source[:, None] == jnp.arange(RPS)[None, :]
-    of_source = jnp.sum(jnp.where(is_source[:, :, None], lengths[None], 0), axis=1)
-    is_k = (chosen % RPS)[:, None] == jnp.arange(RPS)[None, :]
-    length = jnp.sum(jnp.where(is_k, of_source, 0), axis=1)
-    earlier = jnp.arange(RPS)[None, :] < jnp.arange(RPS)[:, None]
-    start = jnp.sum(jnp.where(earlier, length[None, :], 0), axis=1)
-    places = jnp.arange(total, dtype=jnp.int32)
-    inside = (places[:, None] >= start[None, :]) & (places[:, None] < (start + length)[None, :])
-    valid = jnp.any(inside, axis=1)
-    at = jnp.sum(jnp.where(inside, from_source[None, :] * MAXLEN + places[:, None] - start[None, :], 0), axis=1)
-    at = jnp.where(valid, at, -1)
-    pick = (at[:, None] == jnp.arange(RPS * MAXLEN)[None, :]).astype(jnp.bfloat16)
-    return jnp.dot(pick, incoming, preferred_element_type=jnp.float32).astype(jnp.bfloat16)
 
 
 def solution(mesh):

time: 143 us -> 153 us (1.070)
  the two profiles are of different devices: /device:TPU:8 before, /device:TPU:64 now
where the time goes in v5:
time: 153 us
  blocking collectives  76.4 us (50%)
  starting transfers between devices  40.6 us (27%)
  Pallas kernels  17.1 us (11%)
  waiting for transfers between devices  10.8 us (7%)
  other arithmetic  2.81 us (2%)
  local copies, waits for them, and re-layouts  1.99 us (1%)
  between operations  1.97 us (1%)
    all_gather x1, blocking collectives, gather_rows(): lax.all_gather(head, 'tensor', axis=0, axis_index_groups=Z_GROUPS)  31.1 us
    all_to_all x1, blocking collectives, sum_over_chips(): lax.all_to_all(three, 'tensor', split_axis=0, concat_axis=0, tiled=True,...  25 us
    all_to_all x1, blocking collectives, layer(): lax.all_to_all(outgoing.reshape(RPS, MAXLEN, FS), 'dp', split_axis=0, con...  20.4 us
    all_to_all x1, starting transfers between devices, gather_rows(): lax.all_to_all(last, 'tensor', split_axis=0, concat_axis=0, tiled=True)  14.8 us
    ppermute x5, starting transfers between devices, swap(): return lax.ppermute(v, 'tensor', SWAP)  10.7 us
    ppermute x1, starting transfers between devices, sum_over_chips(): below = lax.ppermute(up, 'tensor', [(t, (t + 2) % NT) for t in range(NT)])  5.25 us
    ppermute x1, starting transfers between devices, layer(): first = lax.ppermute(keyval, 'tensor', kv_pairs(True))  5.07 us
    pallas_call x2, Pallas kernels, out_project(): pl.pallas_call(out_kernel, grid_spec=pltpu.PrefetchScalarGridSpec(num_sca...  4.89 us
  transfers between devices with their start and end apart: 10, of which 5 were waited for; matrix products, arithmetic and copies ran while one was open for 0% of the time, Pallas kernels for 9%

profile of v5, /device:TPU:64, one launch (start us, length us, event | category | flops | bytes accessed | tf_op | source)
XLA Modules:
  0.0 152.6 jit_solution(551695471734870383)
XLA Ops:
  3.4 148.5 %conditional.2 = (bf16[256,256]{1,0:T(8,128)(2,1)S(1)}) conditional(s32[]{:T(128)} %clamp.3, (bf16[256,256]{1,0:T(8,128)(2,1)}, bf16[6144,64]{0,1:T(8,128)(2,1)}, f32[6144]{0:T(1024)}, bf16[6144,256]{1,0:T(8,128)(2,1)}, s32[32,32]{1,0:T(8,128)}, /*index=5*/f32[8,128]{1,0:T(8,128)}, f32[8,128]{1,0:T(8,128)}, ...), branch_computations={%region_2.4_spmd, %region_4.6_spmd, %region_6.8_spmd, %region_8.10... | conditional | flops 1948450816 | bytes 90584208
  3.5 2.1 %collective-permute-start.15 = (bf16[256,6144]{1,0:T(8,128)(2,1)}, bf16[256,6144]{1,0:T(8,128)(2,1)S(1)}, u32[]{:S(2)}, u32[]{:S(2)}) collective-permute-start(bf16[256,6144]{1,0:T(8,128)(2,1)} %get-tuple-element.129.rest_0_.rest_1_.rest_2_.rest_3_), channel_id=1, source_target_pairs={{0,1},{1,0},{2,3},{3,2},{4,5},{5,4},{6,7},{7,6},{8,9},{9,8},{10,11... | collective-permute-start | bytes 9437192 | tf_op jit(solution)/shard_map/cond/branch_1_fun/ppermute | solution.py:75
  5.6 2.4 %collective-permute-start.9 = (bf16[64,6144]{1,0:T(8,128)(2,1)}, bf16[64,6144]{1,0:T(8,128)(2,1)}, u32[]{:S(2)}, u32[]{:S(2)}) collective-permute-start(bf16[64,6144]{1,0:T(8,128)(2,1)} %bitcast.79), channel_id=1, source_target_pairs={{0,1},{1,0},{2,3},{3,2},{4,5},{5,4},{6,7},{7,6},{8,9},{9,8},{10,11... | collective-permute-start | bytes 2359304 | tf_op jit(solution)/shard_map/cond/branch_1_fun/ppermute | solution.py:75
  8.0 1.6 %split_rows.3 = (bf16[168,256]{1,0:T(8,128)(2,1)S(1)}, bf16[24,8,256]{2,1,0:T(8,128)(2,1)}) custom-call(bf16[256,256]{1,0:T(8,128)(2,1)} %get-tuple-element.111.x_ref), custom_call_target="tpu_custom_call" | custom-call | tf_op jit(solution)/shard_map/cond/branch_1_fun/split_rows/pallas_call | solution.py:351
  9.5 14.8 %all-to-all-start.2 = ((bf16[24,8,256]{2,1,0:T(8,128)(2,1)}), bf16[24,8,256]{2,1,0:T(8,128)(2,1)S(1)}, u32[]{:S(2)}, u32[]{:S(2)}) async-start(bf16[24,8,256]{2,1,0:T(8,128)(2,1)} %get-tuple-element.113), calls=%async_computation.2 | async-start | bytes 196608 | tf_op jit(solution)/shard_map/cond/branch_1_fun/all_to_all | solution.py:362
  24.4 31.1 %all-gather.1 = bf16[2016,256]{1,0:T(8,128)(2,1)} all-gather(bf16[168,256]{1,0:T(8,128)(2,1)S(1)} %get-tuple-element.112), channel_id=3, replica_groups={{0,2,4,6,8,10,12,14,16,18,20,22},{1,3,5,7,9,11,13,15,17,19,21,23},{24,2..., dimensions={0}, use_global_device_ids=true | all-gather | bytes 1118208 | tf_op jit(solution)/shard_map/cond/branch_1_fun/all_gather | solution.py:363
  55.5 1.9 %collective-permute-start.10 = (bf16[12,168,256]{2,1,0:T(8,128)(2,1)}, bf16[12,168,256]{2,1,0:T(8,128)(2,1)}, u32[]{:S(2)}, u32[]{:S(2)}) collective-permute-start(bf16[12,168,256]{2,1,0:T(8,128)(2,1)} %bitcast.60), channel_id=1, source_target_pairs={{0,1},{1,0},{2,3},{3,2},{4,5},{5,4},{6,7},{7,6},{8,9},{9,8},{10,11... | collective-permute-start | bytes 3096584 | tf_op jit(solution)/shard_map/cond/branch_1_fun/ppermute | solution.py:75
  58.8 3.3 %project_kv.5.mine = f32[176,256]{1,0:T(8,128)S(1)} custom-call(s32[4]{0:T(128)S(1)} %pad_add_fusion.1.core.place, bf16[12,168,256]{2,1,0:T(8,128)(2,1)S(1)} %bitcast.61, bf16[24,8,256]{2,1,0:T(8,128)(2,1)S(1)} %all-to-all-done.2.rest_0_, f32[24,1,256]{2,1,0:T(1,128)} %bitcast.87, bf16[64,6144]{1,0:T(8,128)(2,1)} %bitcast.80, ...), custom_call_target="tpu_custom_call" | custom-call | flops 138412032 | bytes 2654208 | tf_op jit(solution)/shard_map/cond/branch_1_fun/project_kv/pallas_call | solution.py:179
  62.1 2.4 %collective-permute-start.11 = (f32[176,256]{1,0:T(8,128)S(1)}, f32[176,256]{1,0:T(8,128)S(1)}, u32[]{:S(2)}, u32[]{:S(2)}) collective-permute-start(f32[176,256]{1,0:T(8,128)S(1)} %project_kv.5.mine), channel_id=1, source_target_pairs={{0,1},{1,0},{2,3},{3,2},{4,5},{5,4},{6,7},{7,6},{8,9},{9,8},{10,11... | collective-permute-start | bytes 540680 | tf_op jit(solution)/shard_map/cond/branch_1_fun/ppermute | solution.py:75
  65.6 2.8 %collective-permute-start.13 = (bf16[176,128]{1,0:T(8,128)(2,1)S(1)}, bf16[176,128]{1,0:T(8,128)(2,1)S(1)}, u32[]{:S(2)}, u32[]{:S(2)}) collective-permute-start(bf16[176,128]{1,0:T(8,128)(2,1)S(1)} %get-tuple-element.125), channel_id=1, source_target_pairs={{0,2},{1,3},{2,6},{3,7},{4,10},{5,11},{6,14},{7,15},{8,18},{9,19},... | collective-permute-start | bytes 135176 | tf_op jit(solution)/shard_map/cond/branch_1_fun/ppermute | solution.py:440
  68.5 5.1 %collective-permute-start.12 = (bf16[176,128]{1,0:T(8,128)(2,1)S(1)}, bf16[176,128]{1,0:T(8,128)(2,1)S(1)}, u32[]{:S(2)}, u32[]{:S(2)}) collective-permute-start(bf16[176,128]{1,0:T(8,128)(2,1)S(1)} %get-tuple-element.125), channel_id=1, source_target_pairs={{0,0},{1,1},{2,4},{3,5},{4,8},{5,9},{6,12},{7,13},{8,16},{9,17},{1... | collective-permute-start | bytes 135176 | tf_op jit(solution)/shard_map/cond/branch_1_fun/ppermute | solution.py:439
  73.6 4.6 %project_q.5 = (bf16[176,256]{1,0:T(8,128)(2,1)S(1)}, f32[176,128]{1,0:T(8,128)S(1)}, f32[176,128]{1,0:T(8,128)S(1)}, f32[176,176]{1,0:T(8,128)S(1)}) custom-call(s32[4]{0:T(128)S(1)} %pad_add_fusion.1.core.place, bf16[12,168,256]{2,1,0:T(8,128)(2,1)S(1)} %bitcast.62, bf16[12,168,256]{2,1,0:T(8,128)(2,1)} %collective-permute-done.10.theirs, ...), custom_call_target="tpu_custom_call" | custom-call | flops 553648128 | bytes 5308416 | tf_op jit(solution)/shard_map/cond/branch_1_fun/project_q/pallas_call | solution.py:214
  78.3 1.3 collective-permute-done.12.first
  79.5 1.4 attend.5.mine
  81.0 1.9 %collective-permute-start.14 = (bf16[176,256]{1,0:T(8,128)(2,1)S(1)}, bf16[176,256]{1,0:T(8,128)(2,1)S(1)}, u32[]{:S(2)}, u32[]{:S(2)}) collective-permute-start(bf16[176,256]{1,0:T(8,128)(2,1)S(1)} %attend.5.mine), channel_id=1, source_target_pairs={{0,1},{1,0},{2,3},{3,2},{4,5},{5,4},{6,7},{7,6},{8,9},{9,8},{10,11... | collective-permute-start | bytes 270344 | tf_op jit(solution)/shard_map/cond/branch_1_fun/ppermute | solution.py:75
  82.9 1.3 collective-permute-done.14.theirs
  84.2 2.9 %out_project.11 = (bf16[4,176,256]{2,1,0:T(8,128)(2,1)}, bf16[4,176,256]{2,1,0:T(8,128)(2,1)}) custom-call(s32[4]{0:T(128)S(1)} %pad_add_fusion.1.core.place, bf16[176,256]{1,0:T(8,128)(2,1)S(1)} %attend.5.mine, bf16[176,256]{1,0:T(8,128)(2,1)S(1)} %collective-permute-done.14.theirs, bf16[256,6144]{1,0:T(8,128)(2,1)S(1)} %copy-done.14, ...), custom_call_target="tpu_custom_call" | custom-call | flops 369098752 | bytes 2818048 | tf_op jit(solution)/shard_map/cond/branch_1_fun/out_project/pallas_call | solution.py:304
  87.1 5.3 %collective-permute-start.16 = (bf16[4,176,256]{2,1,0:T(8,128)(2,1)}, bf16[4,176,256]{2,1,0:T(8,128)(2,1)}, u32[]{:S(2)}, u32[]{:S(2)}) collective-permute-start(bf16[4,176,256]{2,1,0:T(8,128)(2,1)} %get-tuple-element.132), channel_id=1, source_target_pairs={{0,2},{1,3},{2,4},{3,5},{4,6},{5,7},{6,8},{7,9},{8,10},{9,11},{10,... | collective-permute-start | bytes 1081352 | tf_op jit(solution)/shard_map/cond/branch_1_fun/ppermute | solution.py:327
  92.3 1.9 %collective-permute-start.17 = (bf16[4,176,256]{2,1,0:T(8,128)(2,1)}, bf16[4,176,256]{2,1,0:T(8,128)(2,1)}, u32[]{:S(2)}, u32[]{:S(2)}) collective-permute-start(bf16[4,176,256]{2,1,0:T(8,128)(2,1)} %get-tuple-element.133), channel_id=1, source_target_pairs={{0,22},{1,23},{2,0},{3,1},{4,2},{5,3},{6,4},{7,5},{8,6},{9,7},{10,... | collective-permute-start | bytes 1081352 | tf_op jit(solution)/shard_map/cond/branch_1_fun/ppermute | solution.py:328
  95.5 2.0 %out_project.10 = bf16[4,176,256]{2,1,0:T(8,128)(2,1)S(1)} custom-call(s32[4]{0:T(128)S(1)} %pad_add_fusion.1.core.place, bf16[176,256]{1,0:T(8,128)(2,1)S(1)} %attend.5.mine, bf16[176,256]{1,0:T(8,128)(2,1)S(1)} %collective-permute-done.14.theirs, bf16[256,6144]{1,0:T(8,128)(2,1)} %get-tuple-element.129.rest_0_.rest_1_.rest_2_.rest_3_, ...), custom_call_target="tpu_custom_call" | custom-call | flops 184549376 | bytes 1409024 | tf_op jit(solution)/shard_map/cond/branch_1_fun/out_project/pallas_call | solution.py:304
  97.5 3.1 %collective-permute-done.16 = bf16[4,176,256]{2,1,0:T(8,128)(2,1)} collective-permute-done((bf16[4,176,256]{2,1,0:T(8,128)(2,1)}, bf16[4,176,256]{2,1,0:T(8,128)(2,1)}, u32[]{:S(2)}, u32[]{:S(2)}) %collective-permute-start.16) | collective-permute-done | bytes 360480 | tf_op jit(solution)/shard_map/cond/branch_1_fun/ppermute | solution.py:327
  100.6 4.1 %collective-permute-done.17 = bf16[4,176,256]{2,1,0:T(8,128)(2,1)} collective-permute-done((bf16[4,176,256]{2,1,0:T(8,128)(2,1)}, bf16[4,176,256]{2,1,0:T(8,128)(2,1)}, u32[]{:S(2)}, u32[]{:S(2)}) %collective-permute-start.17) | collective-permute-done | bytes 360480 | tf_op jit(solution)/shard_map/cond/branch_1_fun/ppermute | solution.py:328
  105.9 25.0 %all_to_all.46 = bf16[4,176,256]{2,1,0:T(8,128)(2,1)S(1)} all-to-all(bf16[4,176,256]{2,1,0:T(8,128)(2,1)S(1)} %add_convert_fusion.3), channel_id=1, replica_groups={{0,6,12,18},{1,7,13,19},{2,8,14,20},{3,9,15,21},{4,10,16,22},{5,11,17,2..., dimensions={0} | all-to-all | bytes 720896 | tf_op jit(solution)/shard_map/cond/branch_1_fun/all_to_all | solution.py:332
  131.2 20.4 %all_to_all.47 = bf16[32,8,256]{2,1,0:T(8,128)(2,1)S(1)} all-to-all(bf16[32,8,256]{2,1,0:T(8,128)(2,1)S(1)} %fusion.4), channel_id=1, replica_groups=mesh['dp'=32,'tensor'=24] {'dp'}, dimensions={0} | all-to-all | bytes 262144 | tf_op jit(solution)/shard_map/cond/branch_1_fun/all_to_all | solution.py:448
  (36 shorter events, 7.4 us)
Async XLA Ops:
  3.4 70.1 %copy-start.24 = (f32[6144]{0:T(1024)S(1)}, f32[6144]{0:T(1024)}, u32[]{:S(2)}) copy-start(f32[6144]{0:T(1024)} %get-tuple-element.117) | copy-start | bytes 73732 | tf_op jit(solution)/shard_map/conditional
  3.5 70.1 %copy-start.28 = (s32[32,32]{1,0:T(8,128)S(1)}, s32[32,32]{1,0:T(8,128)}, u32[]{:S(2)}) copy-start(s32[32,32]{1,0:T(8,128)} %get-tuple-element.134.rest_5_.lengths) | copy-start | bytes 12292 | tf_op jit(solution)/shard_map/conditional
  3.5 70.1 %copy-start.33 = (f32[8,128]{1,0:T(8,128)S(1)}, f32[8,128]{1,0:T(8,128)}, u32[]{:S(2)}) copy-start(f32[8,128]{1,0:T(8,128)} %get-tuple-element.123.rest_7_) | copy-start | bytes 12292 | tf_op jit(solution)/shard_map/conditional
  3.5 70.1 %copy-start.37 = (f32[8,128]{1,0:T(8,128)S(1)}, f32[8,128]{1,0:T(8,128)}, u32[]{:S(2)}) copy-start(f32[8,128]{1,0:T(8,128)} %get-tuple-element.122.rest_6_) | copy-start | bytes 12292 | tf_op jit(solution)/shard_map/conditional
  3.5 80.7 %collective-permute-start.15 = (bf16[256,6144]{1,0:T(8,128)(2,1)}, bf16[256,6144]{1,0:T(8,128)(2,1)S(1)}, u32[]{:S(2)}, u32[]{:S(2)}) collective-permute-start(bf16[256,6144]{1,0:T(8,128)(2,1)} %get-tuple-element.129.rest_0_.rest_1_.rest_2_.rest_3_), channel_id=1, source_target_pairs={{0,1},{1,0},{2,3},{3,2},{4,5},{5,4},{6,7},{7,6},{8,9},{9,8},{10,11... | collective-permute-start | bytes 9437192 | tf_op jit(solution)/shard_map/cond/branch_1_fun/ppermute | solution.py:75
  5.6 49.9 %collective-permute-start.9 = (bf16[64,6144]{1,0:T(8,128)(2,1)}, bf16[64,6144]{1,0:T(8,128)(2,1)}, u32[]{:S(2)}, u32[]{:S(2)}) collective-permute-start(bf16[64,6144]{1,0:T(8,128)(2,1)} %bitcast.79), channel_id=1, source_target_pairs={{0,1},{1,0},{2,3},{3,2},{4,5},{5,4},{6,7},{7,6},{8,9},{9,8},{10,11... | collective-permute-start | bytes 2359304 | tf_op jit(solution)/shard_map/cond/branch_1_fun/ppermute | solution.py:75
  9.5 45.9 %all-to-all-start.2 = ((bf16[24,8,256]{2,1,0:T(8,128)(2,1)}), bf16[24,8,256]{2,1,0:T(8,128)(2,1)S(1)}, u32[]{:S(2)}, u32[]{:S(2)}) async-start(bf16[24,8,256]{2,1,0:T(8,128)(2,1)} %get-tuple-element.113), calls=%async_computation.2 | async-start | bytes 196608 | tf_op jit(solution)/shard_map/cond/branch_1_fun/all_to_all | solution.py:362
  55.5 18.1 %collective-permute-start.10 = (bf16[12,168,256]{2,1,0:T(8,128)(2,1)}, bf16[12,168,256]{2,1,0:T(8,128)(2,1)}, u32[]{:S(2)}, u32[]{:S(2)}) collective-permute-start(bf16[12,168,256]{2,1,0:T(8,128)(2,1)} %bitcast.60), channel_id=1, source_target_pairs={{0,1},{1,0},{2,3},{3,2},{4,5},{5,4},{6,7},{7,6},{8,9},{9,8},{10,11... | collective-permute-start | bytes 3096584 | tf_op jit(solution)/shard_map/cond/branch_1_fun/ppermute | solution.py:75
  57.5 1.2 copy-start
  58.7 14.9 %copy-start.1 = (bf16[2016,256]{1,0:T(8,128)(2,1)S(1)}, bf16[2016,256]{1,0:T(8,128)(2,1)}, u32[]{:S(2)}) copy-start(bf16[2016,256]{1,0:T(8,128)(2,1)} %all-gather.1) | copy-start | bytes 3096580 | tf_op jit(solution)/shard_map/conditional
  62.1 3.5 %collective-permute-start.11 = (f32[176,256]{1,0:T(8,128)S(1)}, f32[176,256]{1,0:T(8,128)S(1)}, u32[]{:S(2)}, u32[]{:S(2)}) collective-permute-start(f32[176,256]{1,0:T(8,128)S(1)} %project_kv.5.mine), channel_id=1, source_target_pairs={{0,1},{1,0},{2,3},{3,2},{4,5},{5,4},{6,7},{7,6},{8,9},{9,8},{10,11... | collective-permute-start | bytes 540680 | tf_op jit(solution)/shard_map/cond/branch_1_fun/ppermute | solution.py:75
  65.6 12.6 %collective-permute-start.13 = (bf16[176,128]{1,0:T(8,128)(2,1)S(1)}, bf16[176,128]{1,0:T(8,128)(2,1)S(1)}, u32[]{:S(2)}, u32[]{:S(2)}) collective-permute-start(bf16[176,128]{1,0:T(8,128)(2,1)S(1)} %get-tuple-element.125), channel_id=1, source_target_pairs={{0,2},{1,3},{2,6},{3,7},{4,10},{5,11},{6,14},{7,15},{8,18},{9,19},... | collective-permute-start | bytes 135176 | tf_op jit(solution)/shard_map/cond/branch_1_fun/ppermute | solution.py:440
  68.5 11.1 %collective-permute-start.12 = (bf16[176,128]{1,0:T(8,128)(2,1)S(1)}, bf16[176,128]{1,0:T(8,128)(2,1)S(1)}, u32[]{:S(2)}, u32[]{:S(2)}) collective-permute-start(bf16[176,128]{1,0:T(8,128)(2,1)S(1)} %get-tuple-element.125), channel_id=1, source_target_pairs={{0,0},{1,1},{2,4},{3,5},{4,8},{5,9},{6,12},{7,13},{8,16},{9,17},{1... | collective-permute-start | bytes 135176 | tf_op jit(solution)/shard_map/cond/branch_1_fun/ppermute | solution.py:439
  73.6 10.6 %copy-start.14 = (bf16[256,6144]{1,0:T(8,128)(2,1)S(1)}, bf16[256,6144]{1,0:T(8,128)(2,1)}, u32[]{:S(2)}) copy-start(bf16[256,6144]{1,0:T(8,128)(2,1)} %get-tuple-element.129.rest_0_.rest_1_.rest_2_.rest_3_) | copy-start | bytes 9437188 | tf_op jit(solution)/shard_map/conditional
  81.0 13.3 %copy-start.41 = (s32[1024]{0:T(1024)S(1)}, s32[1024]{0:T(1024)}, u32[]{:S(2)}) copy-start(s32[1024]{0:T(1024)} %get-tuple-element.135) | copy-start | bytes 12292 | tf_op jit(solution)/shard_map/conditional
  81.0 3.2 %collective-permute-start.14 = (bf16[176,256]{1,0:T(8,128)(2,1)S(1)}, bf16[176,256]{1,0:T(8,128)(2,1)S(1)}, u32[]{:S(2)}, u32[]{:S(2)}) collective-permute-start(bf16[176,256]{1,0:T(8,128)(2,1)S(1)} %attend.5.mine), channel_id=1, source_target_pairs={{0,1},{1,0},{2,3},{3,2},{4,5},{5,4},{6,7},{7,6},{8,9},{9,8},{10,11... | collective-permute-start | bytes 270344 | tf_op jit(solution)/shard_map/cond/branch_1_fun/ppermute | solution.py:75
  87.1 13.5 %collective-permute-start.16 = (bf16[4,176,256]{2,1,0:T(8,128)(2,1)}, bf16[4,176,256]{2,1,0:T(8,128)(2,1)}, u32[]{:S(2)}, u32[]{:S(2)}) collective-permute-start(bf16[4,176,256]{2,1,0:T(8,128)(2,1)} %get-tuple-element.132), channel_id=1, source_target_pairs={{0,2},{1,3},{2,4},{3,5},{4,6},{5,7},{6,8},{7,9},{8,10},{9,11},{10,... | collective-permute-start | bytes 1081352 | tf_op jit(solution)/shard_map/cond/branch_1_fun/ppermute | solution.py:327
  92.3 12.4 %collective-permute-start.17 = (bf16[4,176,256]{2,1,0:T(8,128)(2,1)}, bf16[4,176,256]{2,1,0:T(8,128)(2,1)}, u32[]{:S(2)}, u32[]{:S(2)}) collective-permute-start(bf16[4,176,256]{2,1,0:T(8,128)(2,1)} %get-tuple-element.133), channel_id=1, source_target_pairs={{0,22},{1,23},{2,0},{3,1},{4,2},{5,3},{6,4},{7,5},{8,6},{9,7},{10,... | collective-permute-start | bytes 1081352 | tf_op jit(solution)/shard_map/cond/branch_1_fun/ppermute | solution.py:328
  95.4 35.5 %copy-start.20 = (bf16[256,256]{1,0:T(8,128)(2,1)S(1)}, bf16[256,256]{1,0:T(8,128)(2,1)}, u32[]{:S(2)}) copy-start(bf16[256,256]{1,0:T(8,128)(2,1)} %get-tuple-element.111.x_ref) | copy-start | bytes 393220 | tf_op jit(solution)/shard_map/conditional
  152.0 0.7 copy-start.31

commit v6 on v5

--- a/solution.py
+++ b/solution.py
@@ -20,7 +20,7 @@
 EPS = 1e-05
 ROPE_BASE = 500000.0
 AG_ROWS = 168
-VMEM = 24 * 1024 * 1024
+VMEM = 12 * 1024 * 1024
 
 Z_GROUPS = [[z * 2 + c for z in range(NZ)] for c in range(2)]
 FAR = 4
@@ -83,12 +83,12 @@
     return x
 
 
-def kv_kernel(has_tail, core, mine, *rest):
+def kv_kernel(has_tail, core, mine, theirs, *rest):
     if has_tail:
         tail, *rest = rest
     else:
         tail = None
-    gain, wk_m, wk_t, out, kv_acc, sq_acc = rest
+    gain, wk_m, wk_t, kv_out, inv_out, kv_acc, sq_acc = rest
     step = pl.program_id(0)
     c = core[0]
 
@@ -99,28 +99,26 @@
 
     total, squares = kv_acc[...], sq_acc[...]
     for j in range(PER):
-        x = rows_of((mine, tail), j, c)
-        square = x * x
-        squares += square[:, :128] + square[:, 128:]
-        scaled = (x * gain[2 * j + c]).astype(jnp.bfloat16)
-        at = pl.ds(pl.multiple_of((2 * j + c) * FS, FS), FS)
-        w = jnp.concatenate([wk_m[:, at], wk_t[:, at]], axis=0)
-        total += lax.dot_general(scaled, w, (((1,), (1,)), ((), ())), preferred_element_type=jnp.float32)
+        for x_ref, side in ((mine, c), (theirs, 1 - c)):
+            x = rows_of((x_ref, tail), j, side)
+            square = x * x
+            squares += square[:, :128] + square[:, 128:]
+            scaled = (x * gain[2 * j + side]).astype(jnp.bfloat16)
+            at = pl.ds(pl.multiple_of((2 * j + side) * FS, FS), FS)
+            w = jnp.concatenate([wk_m[:, at], wk_t[:, at]], axis=0)
+            total += lax.dot_general(
+                scaled, w, (((1,), (1,)), ((), ())), preferred_element_type=jnp.float32
+            )
     kv_acc[...] = total
     sq_acc[...] = squares
 
     @pl.when(step == STEPS - 1)
     def _():
-        turned = jnp.concatenate([total[:, KVS:], total[:, :KVS]], axis=1)
-        out[:, :HD] = jnp.where(c == 0, total, turned)
-        out[:, HD:] = squares
-
-
-def join_kernel(mine, theirs, kv_out, inv_out):
-    total = mine[...] + theirs[...]
-    inverse = lax.rsqrt(jnp.sum(total[:, HD:], axis=1, keepdims=True) / D + EPS)
-    kv_out[...] = (total[:, :HD] * inverse).astype(jnp.bfloat16)
-    inv_out[...] = jnp.broadcast_to(inverse, inv_out.shape)
+        inverse = lax.rsqrt(jnp.sum(squares, axis=1, keepdims=True) / D + EPS)
+        out = total * inverse
+        turned = jnp.concatenate([out[:, KVS:], out[:, :KVS]], axis=1)
+        kv_out[...] = jnp.where(c == 0, out, turned).astype(jnp.bfloat16)
+        inv_out[...] = jnp.broadcast_to(inverse, inv_out.shape)
 
 
 def q_kernel(has_tail, core, mine, theirs, *rest):
@@ -173,37 +171,29 @@
     return specs
 
 
-def project_kv(core, mine, tail, gain, wk_m, wk_t):
+def project_kv(core, mine, theirs, tail, gain, wk_m, wk_t):
     rows = mine.shape[1] + (0 if tail is None else tail.shape[1])
+    whole = pl.BlockSpec((rows, HD), lambda i, c: (0, 0))
     wk_spec = pl.BlockSpec((KVS, 2 * PER * FS), lambda i, c: (0, i))
-    part = pl.pallas_call(
+    return pl.pallas_call(
         functools.partial(kv_kernel, tail is not None),
         grid_spec=pltpu.PrefetchScalarGridSpec(
             num_scalar_prefetch=1,
             grid=(STEPS,),
-            in_specs=x_specs([mine], tail) + [wk_spec, wk_spec],
-            out_specs=pl.BlockSpec((rows, 2 * HD), lambda i, c: (0, 0)),
+            in_specs=x_specs([mine, theirs], tail) + [wk_spec, wk_spec],
+            out_specs=[whole, whole],
             scratch_shapes=[pltpu.VMEM((rows, HD), jnp.float32), pltpu.VMEM((rows, HD), jnp.float32)],
         ),
-        out_shape=jax.ShapeDtypeStruct((rows, 2 * HD), jnp.float32),
-        compiler_params=pltpu.CompilerParams(vmem_limit_bytes=VMEM),
-        cost_estimate=pl.CostEstimate(
-            flops=rows * D * HD, bytes_accessed=D * (rows + 2 * HD), transcendentals=0
-        ),
-        name="project_kv",
-    )(core, mine, *([] if tail is None else [tail]), gain, wk_m, wk_t)
-    vm = pl.BlockSpec(memory_space=pltpu.VMEM)
-    return pl.pallas_call(
-        join_kernel,
-        in_specs=[vm, vm],
-        out_specs=[vm, vm],
         out_shape=[
             jax.ShapeDtypeStruct((rows, HD), jnp.bfloat16),
             jax.ShapeDtypeStruct((rows, HD), jnp.float32),
         ],
         compiler_params=pltpu.CompilerParams(vmem_limit_bytes=VMEM),
-        name="join_kv",
-    )(part, swap(part))
+        cost_estimate=pl.CostEstimate(
+            flops=2 * rows * D * HD, bytes_accessed=2 * D * (rows + HD), transcendentals=rows
+        ),
+        name="project_kv",
+    )(core, mine, theirs, *([] if tail is None else [tail]), gain, wk_m, wk_t)
 
 
 def project_q(core, mine, theirs, tail, gain, wq, inverse, lengths):
@@ -433,9 +423,9 @@
     mine, tail = gather_rows(rollout, rows)
     gain = norm_gain.reshape(NT, 1, FS)
     wk = keyval_weight.T
-    mine, tail, wk_theirs = lax.optimization_barrier((mine, tail, swap(wk)))
+    mine, tail, wk = lax.optimization_barrier((mine, tail, wk))
     theirs = swap(mine)
-    keyval, inverse = project_kv(core, mine, tail, gain, wk, wk_theirs)
+    keyval, inverse = project_kv(core, mine, theirs, tail, gain, wk, swap(wk))
     first = lax.ppermute(keyval, "tensor", kv_pairs(True))
     second = lax.ppermute(keyval, "tensor", kv_pairs(False))
     q, cosine, sine, bias = project_q(core, mine, theirs, tail, gain, query_weight, inverse, lengths)
@@ -451,11 +441,25 @@
     return jnp.dot(in_pick, incoming, preferred_element_type=jnp.float32).astype(jnp.bfloat16)
 
 
+def size_kernel(lengths, size):
+    longest = jnp.max(jnp.sum(lengths[...].astype(jnp.float32), axis=1, keepdims=True))
+    at = jnp.int32(0)
+    for cap in CAPS[:-1]:
+        at += (longest > cap).astype(jnp.int32)
+    size[0] = at
+
+
 def body(rollout, lengths, packing, norm_gain, query_weight, keyval_weight, out_weight):
-    longest = jnp.max(jnp.sum(lengths, axis=1))
-    size = sum((longest > cap).astype(jnp.int32) for cap in CAPS[:-1])
+    size = pl.pallas_call(
+        size_kernel,
+        in_specs=[pl.BlockSpec(memory_space=pltpu.VMEM)],
+        out_specs=pl.BlockSpec(memory_space=pltpu.SMEM),
+        out_shape=jax.ShapeDtypeStruct((1,), jnp.int32),
+        compiler_params=pltpu.CompilerParams(vmem_limit_bytes=VMEM),
+        name="size",
+    )(lengths)
     return lax.switch(
-        size,
+        size[0],
         [functools.partial(layer, cap) for cap in CAPS],
         rollout, lengths, packing, norm_gain, query_weight, keyval_weight, out_weight,
     )

time: 153 us -> 138 us (0.902)
  the two profiles are of different devices: /device:TPU:64 before, /device:TPU:8 now
where the time goes in v6:
time: 138 us; the launch traced here: 137 us
  blocking collectives  83.7 us (61%)
  starting transfers between devices  17.9 us (13%)
  Pallas kernels  17 us (12%)
  waiting for transfers between devices  14.3 us (10%)
  local copies, waits for them, and re-layouts  1.67 us (1%)
    all_gather x1, blocking collectives, gather_rows(): lax.all_gather(head, 'tensor', axis=0, axis_index_groups=Z_GROUPS)  40.9 us
    all_to_all x1, blocking collectives, sum_over_chips(): lax.all_to_all(three, 'tensor', split_axis=0, concat_axis=0, tiled=True,...  23.3 us
    all_to_all x1, blocking collectives, layer(): lax.all_to_all(outgoing.reshape(RPS, MAXLEN, FS), 'dp', split_axis=0, con...  19.5 us
    ppermute x4, starting transfers between devices, swap(): return lax.ppermute(v, 'tensor', SWAP)  8.29 us
    ppermute x1, waiting for transfers between devices, layer(): second = lax.ppermute(keyval, 'tensor', kv_pairs(False))  5.51 us
    pallas_call x2, Pallas kernels, out_project(): pl.pallas_call(out_kernel, grid_spec=pltpu.PrefetchScalarGridSpec(num_sca...  4.9 us
    pallas_call x1, Pallas kernels, project_q(): pl.pallas_call(functools.partial(q_kernel, tail is not None), grid_spec=p...  4.16 us
    pallas_call x1, Pallas kernels, project_kv(): pl.pallas_call(functools.partial(kv_kernel, tail is not None), grid_spec=...  4.05 us
  transfers between devices with their start and end apart: 8, of which 5 were waited for; matrix products, arithmetic and copies ran while one was open for 1% of the time, Pallas kernels for 9%

profile of v6, /device:TPU:8, one launch (start us, length us, event | category | flops | bytes accessed | tf_op | source)
XLA Modules:
  0.0 137.5 jit_solution(1364325340877352582)
XLA Ops:
  0.0 1.4 size.1
  2.0 134.8 %conditional.2 = (bf16[256,256]{1,0:T(8,128)(2,1)S(1)}) conditional(s32[]{:T(128)} %bitcast.40, (bf16[256,256]{1,0:T(8,128)(2,1)}, bf16[6144,64]{0,1:T(8,128)(2,1)}, f32[6144]{0:T(1024)}, bf16[6144,256]{1,0:T(8,128)(2,1)}, s32[32,32]{1,0:T(8,128)}, /*index=5*/f32[8,128]{1,0:T(8,128)}, f32[8,128]{1,0:T(8,128)}, ...), branch_computations={%region_0.2_spmd, %region_2.4_spmd, %region_4.6_spmd, %region_6.8_... | conditional | flops 2149777408 | bytes 80688144
  2.1 2.1 %collective-permute-start.5 = (bf16[256,6144]{1,0:T(8,128)(2,1)}, bf16[256,6144]{1,0:T(8,128)(2,1)S(1)}, u32[]{:S(2)}, u32[]{:S(2)}) collective-permute-start(bf16[256,6144]{1,0:T(8,128)(2,1)} %get-tuple-element.99.rest_0_.rest_1_.rest_2_.rest_3_), channel_id=1, source_target_pairs={{0,1},{1,0},{2,3},{3,2},{4,5},{5,4},{6,7},{7,6},{8,9},{9,8},{10,11... | collective-permute-start | bytes 9437192 | tf_op jit(solution)/shard_map/cond/branch_0_fun/ppermute | solution.py:75
  5.0 40.9 %all-gather = bf16[2016,256]{1,0:T(8,128)(2,1)} all-gather(bf16[168,256]{1,0:T(8,128)(2,1)S(1)} %slice.6), channel_id=2, replica_groups={{0,2,4,6,8,10,12,14,16,18,20,22},{1,3,5,7,9,11,13,15,17,19,21,23},{24,2..., dimensions={0}, use_global_device_ids=true | all-gather | bytes 1118208 | tf_op jit(solution)/shard_map/cond/branch_0_fun/all_gather | solution.py:353
  45.9 1.9 %collective-permute-start = (bf16[12,168,256]{2,1,0:T(8,128)(2,1)}, bf16[12,168,256]{2,1,0:T(8,128)(2,1)}, u32[]{:S(2)}, u32[]{:S(2)}) collective-permute-start(bf16[12,168,256]{2,1,0:T(8,128)(2,1)} %bitcast.4.mine), channel_id=1, source_target_pairs={{0,1},{1,0},{2,3},{3,2},{4,5},{5,4},{6,7},{7,6},{8,9},{9,8},{10,11... | collective-permute-start | bytes 3096584 | tf_op jit(solution)/shard_map/cond/branch_0_fun/ppermute | solution.py:75
  47.8 2.4 %collective-permute-start.1 = (bf16[64,6144]{1,0:T(8,128)(2,1)}, bf16[64,6144]{1,0:T(8,128)(2,1)}, u32[]{:S(2)}, u32[]{:S(2)}) collective-permute-start(bf16[64,6144]{1,0:T(8,128)(2,1)} %bitcast.78), channel_id=1, source_target_pairs={{0,1},{1,0},{2,3},{3,2},{4,5},{5,4},{6,7},{7,6},{8,9},{9,8},{10,11... | collective-permute-start | bytes 2359304 | tf_op jit(solution)/shard_map/cond/branch_0_fun/ppermute | solution.py:75
  50.4 2.1 %collective-permute-done.1.rest_2_ = bf16[64,6144]{1,0:T(8,128)(2,1)} collective-permute-done((bf16[64,6144]{1,0:T(8,128)(2,1)}, bf16[64,6144]{1,0:T(8,128)(2,1)}, u32[]{:S(2)}, u32[]{:S(2)}) %collective-permute-start.1) | collective-permute-done | bytes 786464 | tf_op jit(solution)/shard_map/cond/branch_0_fun/ppermute | solution.py:75
  52.5 4.0 %project_kv.4 = (bf16[168,128]{1,0:T(8,128)(2,1)S(1)}, f32[168,128]{1,0:T(8,128)S(1)}) custom-call(s32[4]{0:T(128)S(1)} %pad_add_fusion.core.place, bf16[12,168,256]{2,1,0:T(8,128)(2,1)} %bitcast.4.mine, bf16[12,168,256]{2,1,0:T(8,128)(2,1)} %collective-permute-done.theirs, f32[24,1,256]{2,1,0:T(1,128)} %bitcast.86, bf16[64,6144]{1,0:T(8,128)(2,1)} %bitcast.79, ...), custom_call_target="tpu_custom_call" | custom-call | flops 264241152 | bytes 3637248 | tf_op jit(solution)/shard_map/cond/branch_0_fun/project_kv/pallas_call | solution.py:178
  56.6 1.9 %collective-permute-start.3 = (bf16[168,128]{1,0:T(8,128)(2,1)S(1)}, bf16[168,128]{1,0:T(8,128)(2,1)S(1)}, u32[]{:S(2)}, u32[]{:S(2)}) collective-permute-start(bf16[168,128]{1,0:T(8,128)(2,1)S(1)} %get-tuple-element.95), channel_id=1, source_target_pairs={{0,2},{1,3},{2,6},{3,7},{4,10},{5,11},{6,14},{7,15},{8,18},{9,19},... | collective-permute-start | bytes 129032 | tf_op jit(solution)/shard_map/cond/branch_0_fun/ppermute | solution.py:430
  59.2 4.2 %project_q.4 = (bf16[168,256]{1,0:T(8,128)(2,1)S(1)}, f32[168,128]{1,0:T(8,128)S(1)}, f32[168,128]{1,0:T(8,128)S(1)}, f32[168,168]{1,0:T(8,128)S(1)}) custom-call(s32[4]{0:T(128)S(1)} %pad_add_fusion.core.place, bf16[12,168,256]{2,1,0:T(8,128)(2,1)} %bitcast.4.mine, bf16[12,168,256]{2,1,0:T(8,128)(2,1)} %collective-permute-done.theirs, ...), custom_call_target="tpu_custom_call" | custom-call | flops 528482304 | bytes 5210112 | tf_op jit(solution)/shard_map/cond/branch_0_fun/project_q/pallas_call | solution.py:204
  63.4 5.5 %collective-permute-done.3.second = bf16[168,128]{1,0:T(8,128)(2,1)S(1)} collective-permute-done((bf16[168,128]{1,0:T(8,128)(2,1)S(1)}, bf16[168,128]{1,0:T(8,128)(2,1)S(1)}, u32[]{:S(2)}, u32[]{:S(2)}) %collective-permute-start.3) | collective-permute-done | bytes 43040 | tf_op jit(solution)/shard_map/cond/branch_0_fun/ppermute | solution.py:430
  68.9 1.4 %attend.4.mine = bf16[168,256]{1,0:T(8,128)(2,1)S(1)} custom-call(s32[4]{0:T(128)S(1)} %pad_add_fusion.core.place, bf16[168,256]{1,0:T(8,128)(2,1)S(1)} %get-tuple-element.94.q_ref, bf16[168,128]{1,0:T(8,128)(2,1)S(1)} %collective-permute-done.2.first, bf16[168,128]{1,0:T(8,128)(2,1)S(1)} %collective-permute-done.3.second, ...), custom_call_target="tpu_custom_call" | custom-call | flops 28901376 | bytes 172032 | tf_op jit(solution)/shard_map/cond/branch_0_fun/attend/pallas_call | solution.py:261
  70.4 1.9 %collective-permute-start.4 = (bf16[168,256]{1,0:T(8,128)(2,1)S(1)}, bf16[168,256]{1,0:T(8,128)(2,1)S(1)}, u32[]{:S(2)}, u32[]{:S(2)}) collective-permute-start(bf16[168,256]{1,0:T(8,128)(2,1)S(1)} %attend.4.mine), channel_id=1, source_target_pairs={{0,1},{1,0},{2,3},{3,2},{4,5},{5,4},{6,7},{7,6},{8,9},{9,8},{10,11... | collective-permute-start | bytes 258056 | tf_op jit(solution)/shard_map/cond/branch_0_fun/ppermute | solution.py:75
  72.3 1.2 collective-permute-done.4.theirs
  73.5 2.9 %out_project.9 = (bf16[4,168,256]{2,1,0:T(8,128)(2,1)}, bf16[4,168,256]{2,1,0:T(8,128)(2,1)}) custom-call(s32[4]{0:T(128)S(1)} %pad_add_fusion.core.place, bf16[168,256]{1,0:T(8,128)(2,1)S(1)} %attend.4.mine, bf16[168,256]{1,0:T(8,128)(2,1)S(1)} %collective-permute-done.4.theirs, bf16[256,6144]{1,0:T(8,128)(2,1)S(1)} %copy-done.4, ...), custom_call_target="tpu_custom_call" | custom-call | flops 352321536 | bytes 2785280 | tf_op jit(solution)/shard_map/cond/branch_0_fun/out_project/pallas_call | solution.py:294
  76.4 3.7 %collective-permute-start.6 = (bf16[4,168,256]{2,1,0:T(8,128)(2,1)}, bf16[4,168,256]{2,1,0:T(8,128)(2,1)}, u32[]{:S(2)}, u32[]{:S(2)}) collective-permute-start(bf16[4,168,256]{2,1,0:T(8,128)(2,1)} %get-tuple-element.102), channel_id=1, source_target_pairs={{0,2},{1,3},{2,4},{3,5},{4,6},{5,7},{6,8},{7,9},{8,10},{9,11},{10,... | collective-permute-start | bytes 1032200 | tf_op jit(solution)/shard_map/cond/branch_0_fun/ppermute | solution.py:317
  80.1 3.4 %collective-permute-start.7 = (bf16[4,168,256]{2,1,0:T(8,128)(2,1)}, bf16[4,168,256]{2,1,0:T(8,128)(2,1)}, u32[]{:S(2)}, u32[]{:S(2)}) collective-permute-start(bf16[4,168,256]{2,1,0:T(8,128)(2,1)} %get-tuple-element.103), channel_id=1, source_target_pairs={{0,22},{1,23},{2,0},{3,1},{4,2},{5,3},{6,4},{7,5},{8,6},{9,7},{10,... | collective-permute-start | bytes 1032200 | tf_op jit(solution)/shard_map/cond/branch_0_fun/ppermute | solution.py:318
  83.6 1.1 make_picks.4
  84.7 2.0 %out_project.8 = bf16[4,168,256]{2,1,0:T(8,128)(2,1)S(1)} custom-call(s32[4]{0:T(128)S(1)} %pad_add_fusion.core.place, bf16[168,256]{1,0:T(8,128)(2,1)S(1)} %attend.4.mine, bf16[168,256]{1,0:T(8,128)(2,1)S(1)} %collective-permute-done.4.theirs, bf16[256,6144]{1,0:T(8,128)(2,1)} %get-tuple-element.99.rest_0_.rest_1_.rest_2_.rest_3_, ...), custom_call_target="tpu_custom_call" | custom-call | flops 176160768 | bytes 1392640 | tf_op jit(solution)/shard_map/cond/branch_0_fun/out_project/pallas_call | solution.py:294
  86.7 3.2 %collective-permute-done.6 = bf16[4,168,256]{2,1,0:T(8,128)(2,1)} collective-permute-done((bf16[4,168,256]{2,1,0:T(8,128)(2,1)}, bf16[4,168,256]{2,1,0:T(8,128)(2,1)}, u32[]{:S(2)}, u32[]{:S(2)}) %collective-permute-start.6) | collective-permute-done | bytes 344096 | tf_op jit(solution)/shard_map/cond/branch_0_fun/ppermute | solution.py:317
  89.9 2.2 %collective-permute-done.7 = bf16[4,168,256]{2,1,0:T(8,128)(2,1)} collective-permute-done((bf16[4,168,256]{2,1,0:T(8,128)(2,1)}, bf16[4,168,256]{2,1,0:T(8,128)(2,1)}, u32[]{:S(2)}, u32[]{:S(2)}) %collective-permute-start.7) | collective-permute-done | bytes 344096 | tf_op jit(solution)/shard_map/cond/branch_0_fun/ppermute | solution.py:318
  92.2 1.2 add_convert_fusion
  93.4 23.3 %all_to_all.44 = bf16[4,168,256]{2,1,0:T(8,128)(2,1)S(1)} all-to-all(bf16[4,168,256]{2,1,0:T(8,128)(2,1)S(1)} %add_convert_fusion), channel_id=1, replica_groups={{0,6,12,18},{1,7,13,19},{2,8,14,20},{3,9,15,21},{4,10,16,22},{5,11,17,2..., dimensions={0} | all-to-all | bytes 688128 | tf_op jit(solution)/shard_map/cond/branch_0_fun/all_to_all | solution.py:322
  116.9 19.5 %all_to_all.45 = bf16[32,8,256]{2,1,0:T(8,128)(2,1)S(1)} all-to-all(bf16[32,8,256]{2,1,0:T(8,128)(2,1)S(1)} %fusion), channel_id=1, replica_groups=mesh['dp'=32,'tensor'=24] {'dp'}, dimensions={0} | all-to-all | bytes 262144 | tf_op jit(solution)/shard_map/cond/branch_0_fun/all_to_all | solution.py:438
  (28 shorter events, 2.8 us)
Async XLA Ops:
  2.0 57.1 %copy-start.16 = (f32[6144]{0:T(1024)S(1)}, f32[6144]{0:T(1024)}, u32[]{:S(2)}) copy-start(f32[6144]{0:T(1024)} %get-tuple-element.87) | copy-start | bytes 73732 | tf_op jit(solution)/shard_map/conditional
  2.0 57.1 %copy-start.20 = (s32[32,32]{1,0:T(8,128)S(1)}, s32[32,32]{1,0:T(8,128)}, u32[]{:S(2)}) copy-start(s32[32,32]{1,0:T(8,128)} %get-tuple-element.104.rest_4_.lengths) | copy-start | bytes 12292 | tf_op jit(solution)/shard_map/conditional
  2.1 57.1 %copy-start.25 = (f32[8,128]{1,0:T(8,128)S(1)}, f32[8,128]{1,0:T(8,128)}, u32[]{:S(2)}) copy-start(f32[8,128]{1,0:T(8,128)} %get-tuple-element.93.rest_6_) | copy-start | bytes 12292 | tf_op jit(solution)/shard_map/conditional
  2.1 57.1 %copy-start.29 = (f32[8,128]{1,0:T(8,128)S(1)}, f32[8,128]{1,0:T(8,128)}, u32[]{:S(2)}) copy-start(f32[8,128]{1,0:T(8,128)} %get-tuple-element.92.rest_5_) | copy-start | bytes 12292 | tf_op jit(solution)/shard_map/conditional
  2.1 71.5 %collective-permute-start.5 = (bf16[256,6144]{1,0:T(8,128)(2,1)}, bf16[256,6144]{1,0:T(8,128)(2,1)S(1)}, u32[]{:S(2)}, u32[]{:S(2)}) collective-permute-start(bf16[256,6144]{1,0:T(8,128)(2,1)} %get-tuple-element.99.rest_0_.rest_1_.rest_2_.rest_3_), channel_id=1, source_target_pairs={{0,1},{1,0},{2,3},{3,2},{4,5},{5,4},{6,7},{7,6},{8,9},{9,8},{10,11... | collective-permute-start | bytes 9437192 | tf_op jit(solution)/shard_map/cond/branch_0_fun/ppermute | solution.py:75
  45.9 6.6 %collective-permute-start = (bf16[12,168,256]{2,1,0:T(8,128)(2,1)}, bf16[12,168,256]{2,1,0:T(8,128)(2,1)}, u32[]{:S(2)}, u32[]{:S(2)}) collective-permute-start(bf16[12,168,256]{2,1,0:T(8,128)(2,1)} %bitcast.4.mine), channel_id=1, source_target_pairs={{0,1},{1,0},{2,3},{3,2},{4,5},{5,4},{6,7},{7,6},{8,9},{9,8},{10,11... | collective-permute-start | bytes 3096584 | tf_op jit(solution)/shard_map/cond/branch_0_fun/ppermute | solution.py:75
  47.8 4.6 %collective-permute-start.1 = (bf16[64,6144]{1,0:T(8,128)(2,1)}, bf16[64,6144]{1,0:T(8,128)(2,1)}, u32[]{:S(2)}, u32[]{:S(2)}) collective-permute-start(bf16[64,6144]{1,0:T(8,128)(2,1)} %bitcast.78), channel_id=1, source_target_pairs={{0,1},{1,0},{2,3},{3,2},{4,5},{5,4},{6,7},{7,6},{8,9},{9,8},{10,11... | collective-permute-start | bytes 2359304 | tf_op jit(solution)/shard_map/cond/branch_0_fun/ppermute | solution.py:75
  50.3 8.9 %copy-start.8 = (bf16[6144,256]{1,0:T(8,128)(2,1)S(1)}, bf16[6144,256]{1,0:T(8,128)(2,1)}, u32[]{:S(2)}) copy-start(bf16[6144,256]{1,0:T(8,128)(2,1)} %get-tuple-element.88) | copy-start | bytes 9437188 | tf_op jit(solution)/shard_map/conditional
  56.6 12.3 %collective-permute-start.3 = (bf16[168,128]{1,0:T(8,128)(2,1)S(1)}, bf16[168,128]{1,0:T(8,128)(2,1)S(1)}, u32[]{:S(2)}, u32[]{:S(2)}) collective-permute-start(bf16[168,128]{1,0:T(8,128)(2,1)S(1)} %get-tuple-element.95), channel_id=1, source_target_pairs={{0,2},{1,3},{2,6},{3,7},{4,10},{5,11},{6,14},{7,15},{8,18},{9,19},... | collective-permute-start | bytes 129032 | tf_op jit(solution)/shard_map/cond/branch_0_fun/ppermute | solution.py:430
  58.5 10.4 %collective-permute-start.2 = (bf16[168,128]{1,0:T(8,128)(2,1)S(1)}, bf16[168,128]{1,0:T(8,128)(2,1)S(1)}, u32[]{:S(2)}, u32[]{:S(2)}) collective-permute-start(bf16[168,128]{1,0:T(8,128)(2,1)S(1)} %get-tuple-element.95), channel_id=1, source_target_pairs={{0,0},{1,1},{2,4},{3,5},{4,8},{5,9},{6,12},{7,13},{8,16},{9,17},{1... | collective-permute-start | bytes 129032 | tf_op jit(solution)/shard_map/cond/branch_0_fun/ppermute | solution.py:429
  59.2 14.3 %copy-start.4 = (bf16[256,6144]{1,0:T(8,128)(2,1)S(1)}, bf16[256,6144]{1,0:T(8,128)(2,1)}, u32[]{:S(2)}) copy-start(bf16[256,6144]{1,0:T(8,128)(2,1)} %get-tuple-element.99.rest_0_.rest_1_.rest_2_.rest_3_) | copy-start | bytes 9437188 | tf_op jit(solution)/shard_map/conditional
  70.3 13.1 %copy-start.33 = (s32[1024]{0:T(1024)S(1)}, s32[1024]{0:T(1024)}, u32[]{:S(2)}) copy-start(s32[1024]{0:T(1024)} %get-tuple-element.105) | copy-start | bytes 12292 | tf_op jit(solution)/shard_map/conditional
  70.4 3.2 %collective-permute-start.4 = (bf16[168,256]{1,0:T(8,128)(2,1)S(1)}, bf16[168,256]{1,0:T(8,128)(2,1)S(1)}, u32[]{:S(2)}, u32[]{:S(2)}) collective-permute-start(bf16[168,256]{1,0:T(8,128)(2,1)S(1)} %attend.4.mine), channel_id=1, source_target_pairs={{0,1},{1,0},{2,3},{3,2},{4,5},{5,4},{6,7},{7,6},{8,9},{9,8},{10,11... | collective-permute-start | bytes 258056 | tf_op jit(solution)/shard_map/cond/branch_0_fun/ppermute | solution.py:75
  76.4 13.5 %collective-permute-start.6 = (bf16[4,168,256]{2,1,0:T(8,128)(2,1)}, bf16[4,168,256]{2,1,0:T(8,128)(2,1)}, u32[]{:S(2)}, u32[]{:S(2)}) collective-permute-start(bf16[4,168,256]{2,1,0:T(8,128)(2,1)} %get-tuple-element.102), channel_id=1, source_target_pairs={{0,2},{1,3},{2,4},{3,5},{4,6},{5,7},{6,8},{7,9},{8,10},{9,11},{10,... | collective-permute-start | bytes 1032200 | tf_op jit(solution)/shard_map/cond/branch_0_fun/ppermute | solution.py:317
  80.1 12.1 %collective-permute-start.7 = (bf16[4,168,256]{2,1,0:T(8,128)(2,1)}, bf16[4,168,256]{2,1,0:T(8,128)(2,1)}, u32[]{:S(2)}, u32[]{:S(2)}) collective-permute-start(bf16[4,168,256]{2,1,0:T(8,128)(2,1)} %get-tuple-element.103), channel_id=1, source_target_pairs={{0,22},{1,23},{2,0},{3,1},{4,2},{5,3},{6,4},{7,5},{8,6},{9,7},{10,... | collective-permute-start | bytes 1032200 | tf_op jit(solution)/shard_map/cond/branch_0_fun/ppermute | solution.py:318
  84.7 32.0 %copy-start.12 = (bf16[256,256]{1,0:T(8,128)(2,1)S(1)}, bf16[256,256]{1,0:T(8,128)(2,1)}, u32[]{:S(2)}) copy-start(bf16[256,256]{1,0:T(8,128)(2,1)} %get-tuple-element.84) | copy-start | bytes 393220 | tf_op jit(solution)/shard_map/conditional
  136.8 0.7 copy-start.24

commit v7 on v6

--- a/solution.py
+++ b/solution.py
@@ -286,9 +286,9 @@
 def out_project(place, mine, theirs, w_mine, w_theirs, shifts):
     rows = mine.shape[0]
     context = pl.BlockSpec((rows, FS), lambda i, p: (0, 0))
-    first = shifts[0]
+    turn_round = (lambda i, p: 1 + i + p[0] * (1 - 2 * i)) if len(shifts) == 2 else (lambda i, p: 0)
     weights = [
-        pl.BlockSpec((FS, FS), lambda i, p, k=k: (0, 2 * (3 * k + lax.rem(p[1] + first + i, 3)) + p[0]))
+        pl.BlockSpec((FS, FS), lambda i, p, k=k: (0, 2 * (3 * k + lax.rem(p[1] + turn_round(i, p), 3)) + p[0]))
         for k in range(FAR)
     ]
     return pl.pallas_call(
@@ -311,11 +311,11 @@
 
 
 def sum_over_chips(place, context, theirs, w_mine, w_theirs, lengths, packing):
-    up, down = out_project(place, context, theirs, w_mine, w_theirs, (1, 2))
-    up, lengths, packing = lax.optimization_barrier((up, lengths, packing))
+    one, two = out_project(place, context, theirs, w_mine, w_theirs, (1, 2))
+    one, lengths, packing = lax.optimization_barrier((one, lengths, packing))
     picks = make_picks(place, lengths, packing, context.shape[0])
-    below = lax.ppermute(up, "tensor", [(t, (t + 2) % NT) for t in range(NT)])
-    above = lax.ppermute(down, "tensor", [(t, (t - 2) % NT) for t in range(NT)])
+    below = lax.ppermute(one, "tensor", [(t, (t + 2 - 4 * (t % 2)) % NT) for t in range(NT)])
+    above = lax.ppermute(two, "tensor", [(t, (t - 2 + 4 * (t % 2)) % NT) for t in range(NT)])
     (own,) = out_project(place, context, theirs, w_mine, w_theirs, (0,))
     three = own.astype(jnp.float32) + below.astype(jnp.float32) + above.astype(jnp.float32)
     three, *picks = lax.optimization_barrier((three.astype(jnp.bfloat16), *picks))

time: 138 us -> 149 us (1.080)
  starting transfers between devices: 17.9 us -> 34.7 us
  blocking collectives: 83.7 us -> 78.5 us
  waiting for transfers between devices: 14.3 us -> 12.1 us
    all_to_all x0 -> x1, starting transfers between devices: none -> 15.5 us  [gather_rows(): lax.all_to_all(last, 'tensor', split_axis=0, concat_axis=0, tiled=True)]
    all_gather x1, blocking collectives: 40.9 us -> 32 us  [gather_rows(): lax.all_gather(head, 'tensor', axis=0, axis_index_groups=Z_GROUPS)]
    all_to_all x1, blocking collectives: 23.3 us -> 27 us  [sum_over_chips(): lax.all_to_all(three, 'tensor', split_axis=0, concat_axis=0, tiled=True,...]
    pallas_call x0 -> x1, Pallas kernels: none -> 1.55 us  [gather_rows(): pl.pallas_call(split_kernel, in_specs=[vm], out_specs=[vm, vm], out_shape...]
  transfers between devices with their start and end apart: 8 -> 9, of which waited for: 5 -> 5; matrix products, arithmetic and copies ran while one was open for 1% -> 0% of each run, Pallas kernels for 9% -> 10%
where the time goes in v7:
time: 149 us
  blocking collectives  78.5 us (53%)
  starting transfers between devices  34.7 us (23%)
  Pallas kernels  18.4 us (12%)
  waiting for transfers between devices  12.1 us (8%)
  local copies, waits for them, and re-layouts  1.99 us (1%)
    all_gather x1, blocking collectives, gather_rows(): lax.all_gather(head, 'tensor', axis=0, axis_index_groups=Z_GROUPS)  32 us
    all_to_all x1, blocking collectives, sum_over_chips(): lax.all_to_all(three, 'tensor', split_axis=0, concat_axis=0, tiled=True,...  27 us
    all_to_all x1, blocking collectives, layer(): lax.all_to_all(outgoing.reshape(RPS, MAXLEN, FS), 'dp', split_axis=0, con...  19.5 us
    all_to_all x1, starting transfers between devices, gather_rows(): lax.all_to_all(last, 'tensor', split_axis=0, concat_axis=0, tiled=True)  15.5 us
    ppermute x4, starting transfers between devices, swap(): return lax.ppermute(v, 'tensor', SWAP)  8.3 us
    pallas_call x2, Pallas kernels, out_project(): pl.pallas_call(out_kernel, grid_spec=pltpu.PrefetchScalarGridSpec(num_sca...  4.91 us
    ppermute x1, waiting for transfers between devices, layer(): second = lax.ppermute(keyval, 'tensor', kv_pairs(False))  4.75 us
    ppermute x1, starting transfers between devices, sum_over_chips(): lax.ppermute(one, 'tensor', [(t, (t + 2 - 4 * (t % 2)) % NT) for t in ran...  4.43 us
  transfers between devices with their start and end apart: 9, of which 5 were waited for; matrix products, arithmetic and copies ran while one was open for 0% of the time, Pallas kernels for 10%

profile of v7, /device:TPU:8, one launch (start us, length us, event | category | flops | bytes accessed | tf_op | source)
XLA Modules:
  0.0 148.7 jit_solution(17498314795944868658)
XLA Ops:
  0.0 1.4 size.1
  2.0 146.0 %conditional.2 = (bf16[256,256]{1,0:T(8,128)(2,1)S(1)}) conditional(s32[]{:T(128)} %bitcast.40, (bf16[256,256]{1,0:T(8,128)(2,1)}, bf16[6144,64]{0,1:T(8,128)(2,1)}, f32[6144]{0:T(1024)}, bf16[6144,256]{1,0:T(8,128)(2,1)}, s32[32,32]{1,0:T(8,128)}, /*index=5*/f32[8,128]{1,0:T(8,128)}, f32[8,128]{1,0:T(8,128)}, ...), branch_computations={%region_0.2_spmd, %region_2.4_spmd, %region_4.6_spmd, %region_6.8_... | conditional | flops 2149777408 | bytes 80688144
  2.1 2.1 %collective-permute-start.13 = (bf16[256,6144]{1,0:T(8,128)(2,1)}, bf16[256,6144]{1,0:T(8,128)(2,1)S(1)}, u32[]{:S(2)}, u32[]{:S(2)}) collective-permute-start(bf16[256,6144]{1,0:T(8,128)(2,1)} %get-tuple-element.129.rest_0_.rest_1_.rest_2_.rest_3_), channel_id=1, source_target_pairs={{0,1},{1,0},{2,3},{3,2},{4,5},{5,4},{6,7},{7,6},{8,9},{9,8},{10,11... | collective-permute-start | bytes 9437192 | tf_op jit(solution)/shard_map/cond/branch_1_fun/ppermute | solution.py:75
  4.2 1.6 %split_rows.3 = (bf16[168,256]{1,0:T(8,128)(2,1)S(1)}, bf16[24,8,256]{2,1,0:T(8,128)(2,1)}) custom-call(bf16[256,256]{1,0:T(8,128)(2,1)} %get-tuple-element.111.x_ref), custom_call_target="tpu_custom_call" | custom-call | tf_op jit(solution)/shard_map/cond/branch_1_fun/split_rows/pallas_call | solution.py:341
  5.7 15.5 %all-to-all-start.2 = ((bf16[24,8,256]{2,1,0:T(8,128)(2,1)}), bf16[24,8,256]{2,1,0:T(8,128)(2,1)S(1)}, u32[]{:S(2)}, u32[]{:S(2)}) async-start(bf16[24,8,256]{2,1,0:T(8,128)(2,1)} %get-tuple-element.113), calls=%async_computation.2 | async-start | bytes 196608 | tf_op jit(solution)/shard_map/cond/branch_1_fun/all_to_all | solution.py:352
  21.2 32.0 %all-gather.1 = bf16[2016,256]{1,0:T(8,128)(2,1)} all-gather(bf16[168,256]{1,0:T(8,128)(2,1)S(1)} %get-tuple-element.112), channel_id=3, replica_groups={{0,2,4,6,8,10,12,14,16,18,20,22},{1,3,5,7,9,11,13,15,17,19,21,23},{24,2..., dimensions={0}, use_global_device_ids=true | all-gather | bytes 1118208 | tf_op jit(solution)/shard_map/cond/branch_1_fun/all_gather | solution.py:353
  53.2 1.9 %collective-permute-start.8 = (bf16[12,168,256]{2,1,0:T(8,128)(2,1)}, bf16[12,168,256]{2,1,0:T(8,128)(2,1)}, u32[]{:S(2)}, u32[]{:S(2)}) collective-permute-start(bf16[12,168,256]{2,1,0:T(8,128)(2,1)} %bitcast.64), channel_id=1, source_target_pairs={{0,1},{1,0},{2,3},{3,2},{4,5},{5,4},{6,7},{7,6},{8,9},{9,8},{10,11... | collective-permute-start | bytes 3096584 | tf_op jit(solution)/shard_map/cond/branch_1_fun/ppermute | solution.py:75
  55.1 2.4 %collective-permute-start.9 = (bf16[64,6144]{1,0:T(8,128)(2,1)}, bf16[64,6144]{1,0:T(8,128)(2,1)}, u32[]{:S(2)}, u32[]{:S(2)}) collective-permute-start(bf16[64,6144]{1,0:T(8,128)(2,1)} %bitcast.80), channel_id=1, source_target_pairs={{0,1},{1,0},{2,3},{3,2},{4,5},{5,4},{6,7},{7,6},{8,9},{9,8},{10,11... | collective-permute-start | bytes 2359304 | tf_op jit(solution)/shard_map/cond/branch_1_fun/ppermute | solution.py:75
  57.7 2.1 %collective-permute-done.9.rest_3_ = bf16[64,6144]{1,0:T(8,128)(2,1)} collective-permute-done((bf16[64,6144]{1,0:T(8,128)(2,1)}, bf16[64,6144]{1,0:T(8,128)(2,1)}, u32[]{:S(2)}, u32[]{:S(2)}) %collective-permute-start.9) | collective-permute-done | bytes 786464 | tf_op jit(solution)/shard_map/cond/branch_1_fun/ppermute | solution.py:75
  61.0 4.0 %project_kv.5 = (bf16[176,128]{1,0:T(8,128)(2,1)S(1)}, f32[176,128]{1,0:T(8,128)S(1)}) custom-call(s32[4]{0:T(128)S(1)} %pad_add_fusion.1.core.place, bf16[12,168,256]{2,1,0:T(8,128)(2,1)S(1)} %bitcast.65, bf16[12,168,256]{2,1,0:T(8,128)(2,1)} %collective-permute-done.8.theirs, bf16[24,8,256]{2,1,0:T(8,128)(2,1)S(1)} %all-to-all-done.2.rest_0_, ...), custom_call_target="tpu_custom_call" | custom-call | flops 276824064 | bytes 3735552 | tf_op jit(solution)/shard_map/cond/branch_1_fun/project_kv/pallas_call | solution.py:178
  65.1 2.8 %collective-permute-start.11 = (bf16[176,128]{1,0:T(8,128)(2,1)S(1)}, bf16[176,128]{1,0:T(8,128)(2,1)S(1)}, u32[]{:S(2)}, u32[]{:S(2)}) collective-permute-start(bf16[176,128]{1,0:T(8,128)(2,1)S(1)} %get-tuple-element.125), channel_id=1, source_target_pairs={{0,2},{1,3},{2,6},{3,7},{4,10},{5,11},{6,14},{7,15},{8,18},{9,19},... | collective-permute-start | bytes 135176 | tf_op jit(solution)/shard_map/cond/branch_1_fun/ppermute | solution.py:430
  68.6 4.0 %project_q.5 = (bf16[176,256]{1,0:T(8,128)(2,1)S(1)}, f32[176,128]{1,0:T(8,128)S(1)}, f32[176,128]{1,0:T(8,128)S(1)}, f32[176,176]{1,0:T(8,128)S(1)}) custom-call(s32[4]{0:T(128)S(1)} %pad_add_fusion.1.core.place, bf16[12,168,256]{2,1,0:T(8,128)(2,1)S(1)} %bitcast.66, bf16[12,168,256]{2,1,0:T(8,128)(2,1)} %collective-permute-done.8.theirs, ...), custom_call_target="tpu_custom_call" | custom-call | flops 553648128 | bytes 5308416 | tf_op jit(solution)/shard_map/cond/branch_1_fun/project_q/pallas_call | solution.py:204
  72.6 4.7 %collective-permute-done.11.second = bf16[176,128]{1,0:T(8,128)(2,1)S(1)} collective-permute-done((bf16[176,128]{1,0:T(8,128)(2,1)S(1)}, bf16[176,128]{1,0:T(8,128)(2,1)S(1)}, u32[]{:S(2)}, u32[]{:S(2)}) %collective-permute-start.11) | collective-permute-done | bytes 45088 | tf_op jit(solution)/shard_map/cond/branch_1_fun/ppermute | solution.py:430
  77.3 1.4 attend.5.mine
  78.8 1.9 %collective-permute-start.12 = (bf16[176,256]{1,0:T(8,128)(2,1)S(1)}, bf16[176,256]{1,0:T(8,128)(2,1)S(1)}, u32[]{:S(2)}, u32[]{:S(2)}) collective-permute-start(bf16[176,256]{1,0:T(8,128)(2,1)S(1)} %attend.5.mine), channel_id=1, source_target_pairs={{0,1},{1,0},{2,3},{3,2},{4,5},{5,4},{6,7},{7,6},{8,9},{9,8},{10,11... | collective-permute-start | bytes 270344 | tf_op jit(solution)/shard_map/cond/branch_1_fun/ppermute | solution.py:75
  80.7 1.3 collective-permute-done.12.theirs
  82.0 2.9 %out_project.11 = (bf16[4,176,256]{2,1,0:T(8,128)(2,1)}, bf16[4,176,256]{2,1,0:T(8,128)(2,1)}) custom-call(s32[4]{0:T(128)S(1)} %pad_add_fusion.1.core.place, bf16[176,256]{1,0:T(8,128)(2,1)S(1)} %attend.5.mine, bf16[176,256]{1,0:T(8,128)(2,1)S(1)} %collective-permute-done.12.theirs, bf16[256,6144]{1,0:T(8,128)(2,1)S(1)} %copy-done.5, ...), custom_call_target="tpu_custom_call" | custom-call | flops 369098752 | bytes 2818048 | tf_op jit(solution)/shard_map/cond/branch_1_fun/out_project/pallas_call | solution.py:294
  84.9 4.4 %collective-permute-start.14 = (bf16[4,176,256]{2,1,0:T(8,128)(2,1)}, bf16[4,176,256]{2,1,0:T(8,128)(2,1)}, u32[]{:S(2)}, u32[]{:S(2)}) collective-permute-start(bf16[4,176,256]{2,1,0:T(8,128)(2,1)} %get-tuple-element.132), channel_id=1, source_target_pairs={{0,2},{1,23},{2,4},{3,1},{4,6},{5,3},{6,8},{7,5},{8,10},{9,7},{10,... | collective-permute-start | bytes 1081352 | tf_op jit(solution)/shard_map/cond/branch_1_fun/ppermute | solution.py:317
  89.3 3.1 %collective-permute-start.15 = (bf16[4,176,256]{2,1,0:T(8,128)(2,1)}, bf16[4,176,256]{2,1,0:T(8,128)(2,1)}, u32[]{:S(2)}, u32[]{:S(2)}) collective-permute-start(bf16[4,176,256]{2,1,0:T(8,128)(2,1)} %get-tuple-element.133), channel_id=1, source_target_pairs={{0,22},{1,3},{2,0},{3,5},{4,2},{5,7},{6,4},{7,9},{8,6},{9,11},{10,... | collective-permute-start | bytes 1081352 | tf_op jit(solution)/shard_map/cond/branch_1_fun/ppermute | solution.py:318
  93.6 2.0 %out_project.10 = bf16[4,176,256]{2,1,0:T(8,128)(2,1)S(1)} custom-call(s32[4]{0:T(128)S(1)} %pad_add_fusion.1.core.place, bf16[176,256]{1,0:T(8,128)(2,1)S(1)} %attend.5.mine, bf16[176,256]{1,0:T(8,128)(2,1)S(1)} %collective-permute-done.12.theirs, bf16[256,6144]{1,0:T(8,128)(2,1)} %get-tuple-element.129.rest_0_.rest_1_.rest_2_.rest_3_, ...), custom_call_target="tpu_custom_call" | custom-call | flops 184549376 | bytes 1409024 | tf_op jit(solution)/shard_map/cond/branch_1_fun/out_project/pallas_call | solution.py:294
  96.1 3.5 %collective-permute-done.15 = bf16[4,176,256]{2,1,0:T(8,128)(2,1)} collective-permute-done((bf16[4,176,256]{2,1,0:T(8,128)(2,1)}, bf16[4,176,256]{2,1,0:T(8,128)(2,1)}, u32[]{:S(2)}, u32[]{:S(2)}) %collective-permute-start.15) | collective-permute-done | bytes 360480 | tf_op jit(solution)/shard_map/cond/branch_1_fun/ppermute | solution.py:318
  99.6 1.2 add_convert_fusion.3
  100.8 27.0 %all_to_all.46 = bf16[4,176,256]{2,1,0:T(8,128)(2,1)S(1)} all-to-all(bf16[4,176,256]{2,1,0:T(8,128)(2,1)S(1)} %add_convert_fusion.3), channel_id=1, replica_groups={{0,6,12,18},{1,7,13,19},{2,8,14,20},{3,9,15,21},{4,10,16,22},{5,11,17,2..., dimensions={0} | all-to-all | bytes 720896 | tf_op jit(solution)/shard_map/cond/branch_1_fun/all_to_all | solution.py:322
  128.1 19.5 %all_to_all.47 = bf16[32,8,256]{2,1,0:T(8,128)(2,1)S(1)} all-to-all(bf16[32,8,256]{2,1,0:T(8,128)(2,1)S(1)} %fusion.4), channel_id=1, replica_groups=mesh['dp'=32,'tensor'=24] {'dp'}, dimensions={0} | all-to-all | bytes 262144 | tf_op jit(solution)/shard_map/cond/branch_1_fun/all_to_all | solution.py:438
  (32 shorter events, 4.8 us)
Async XLA Ops:
  2.0 66.5 %copy-start.17 = (f32[6144]{0:T(1024)S(1)}, f32[6144]{0:T(1024)}, u32[]{:S(2)}) copy-start(f32[6144]{0:T(1024)} %get-tuple-element.117) | copy-start | bytes 73732 | tf_op jit(solution)/shard_map/conditional
  2.1 66.5 %copy-start.21 = (s32[32,32]{1,0:T(8,128)S(1)}, s32[32,32]{1,0:T(8,128)}, u32[]{:S(2)}) copy-start(s32[32,32]{1,0:T(8,128)} %get-tuple-element.134.rest_5_.lengths) | copy-start | bytes 12292 | tf_op jit(solution)/shard_map/conditional
  2.1 66.5 %copy-start.26 = (f32[8,128]{1,0:T(8,128)S(1)}, f32[8,128]{1,0:T(8,128)}, u32[]{:S(2)}) copy-start(f32[8,128]{1,0:T(8,128)} %get-tuple-element.123.rest_7_) | copy-start | bytes 12292 | tf_op jit(solution)/shard_map/conditional
  2.1 66.5 %copy-start.30 = (f32[8,128]{1,0:T(8,128)S(1)}, f32[8,128]{1,0:T(8,128)}, u32[]{:S(2)}) copy-start(f32[8,128]{1,0:T(8,128)} %get-tuple-element.122.rest_6_) | copy-start | bytes 12292 | tf_op jit(solution)/shard_map/conditional
  2.1 79.9 %collective-permute-start.13 = (bf16[256,6144]{1,0:T(8,128)(2,1)}, bf16[256,6144]{1,0:T(8,128)(2,1)S(1)}, u32[]{:S(2)}, u32[]{:S(2)}) collective-permute-start(bf16[256,6144]{1,0:T(8,128)(2,1)} %get-tuple-element.129.rest_0_.rest_1_.rest_2_.rest_3_), channel_id=1, source_target_pairs={{0,1},{1,0},{2,3},{3,2},{4,5},{5,4},{6,7},{7,6},{8,9},{9,8},{10,11... | collective-permute-start | bytes 9437192 | tf_op jit(solution)/shard_map/cond/branch_1_fun/ppermute | solution.py:75
  5.7 47.5 %all-to-all-start.2 = ((bf16[24,8,256]{2,1,0:T(8,128)(2,1)}), bf16[24,8,256]{2,1,0:T(8,128)(2,1)S(1)}, u32[]{:S(2)}, u32[]{:S(2)}) async-start(bf16[24,8,256]{2,1,0:T(8,128)(2,1)} %get-tuple-element.113), calls=%async_computation.2 | async-start | bytes 196608 | tf_op jit(solution)/shard_map/cond/branch_1_fun/all_to_all | solution.py:352
  53.2 6.6 %collective-permute-start.8 = (bf16[12,168,256]{2,1,0:T(8,128)(2,1)}, bf16[12,168,256]{2,1,0:T(8,128)(2,1)}, u32[]{:S(2)}, u32[]{:S(2)}) collective-permute-start(bf16[12,168,256]{2,1,0:T(8,128)(2,1)} %bitcast.64), channel_id=1, source_target_pairs={{0,1},{1,0},{2,3},{3,2},{4,5},{5,4},{6,7},{7,6},{8,9},{9,8},{10,11... | collective-permute-start | bytes 3096584 | tf_op jit(solution)/shard_map/cond/branch_1_fun/ppermute | solution.py:75
  55.1 4.6 %collective-permute-start.9 = (bf16[64,6144]{1,0:T(8,128)(2,1)}, bf16[64,6144]{1,0:T(8,128)(2,1)}, u32[]{:S(2)}, u32[]{:S(2)}) collective-permute-start(bf16[64,6144]{1,0:T(8,128)(2,1)} %bitcast.80), channel_id=1, source_target_pairs={{0,1},{1,0},{2,3},{3,2},{4,5},{5,4},{6,7},{7,6},{8,9},{9,8},{10,11... | collective-permute-start | bytes 2359304 | tf_op jit(solution)/shard_map/cond/branch_1_fun/ppermute | solution.py:75
  59.8 1.2 copy-start.1
  61.0 7.6 %copy-start.9 = (bf16[6144,256]{1,0:T(8,128)(2,1)S(1)}, bf16[6144,256]{1,0:T(8,128)(2,1)}, u32[]{:S(2)}) copy-start(bf16[6144,256]{1,0:T(8,128)(2,1)} %get-tuple-element.118) | copy-start | bytes 9437188 | tf_op jit(solution)/shard_map/conditional
  65.1 12.3 %collective-permute-start.11 = (bf16[176,128]{1,0:T(8,128)(2,1)S(1)}, bf16[176,128]{1,0:T(8,128)(2,1)S(1)}, u32[]{:S(2)}, u32[]{:S(2)}) collective-permute-start(bf16[176,128]{1,0:T(8,128)(2,1)S(1)} %get-tuple-element.125), channel_id=1, source_target_pairs={{0,2},{1,3},{2,6},{3,7},{4,10},{5,11},{6,14},{7,15},{8,18},{9,19},... | collective-permute-start | bytes 135176 | tf_op jit(solution)/shard_map/cond/branch_1_fun/ppermute | solution.py:430
  67.9 9.4 %collective-permute-start.10 = (bf16[176,128]{1,0:T(8,128)(2,1)S(1)}, bf16[176,128]{1,0:T(8,128)(2,1)S(1)}, u32[]{:S(2)}, u32[]{:S(2)}) collective-permute-start(bf16[176,128]{1,0:T(8,128)(2,1)S(1)} %get-tuple-element.125), channel_id=1, source_target_pairs={{0,0},{1,1},{2,4},{3,5},{4,8},{5,9},{6,12},{7,13},{8,16},{9,17},{1... | collective-permute-start | bytes 135176 | tf_op jit(solution)/shard_map/cond/branch_1_fun/ppermute | solution.py:429
  68.6 13.4 %copy-start.5 = (bf16[256,6144]{1,0:T(8,128)(2,1)S(1)}, bf16[256,6144]{1,0:T(8,128)(2,1)}, u32[]{:S(2)}) copy-start(bf16[256,6144]{1,0:T(8,128)(2,1)} %get-tuple-element.129.rest_0_.rest_1_.rest_2_.rest_3_) | copy-start | bytes 9437188 | tf_op jit(solution)/shard_map/conditional
  78.8 13.6 %copy-start.34 = (s32[1024]{0:T(1024)S(1)}, s32[1024]{0:T(1024)}, u32[]{:S(2)}) copy-start(s32[1024]{0:T(1024)} %get-tuple-element.135) | copy-start | bytes 12292 | tf_op jit(solution)/shard_map/conditional
  78.8 3.2 %collective-permute-start.12 = (bf16[176,256]{1,0:T(8,128)(2,1)S(1)}, bf16[176,256]{1,0:T(8,128)(2,1)S(1)}, u32[]{:S(2)}, u32[]{:S(2)}) collective-permute-start(bf16[176,256]{1,0:T(8,128)(2,1)S(1)} %attend.5.mine), channel_id=1, source_target_pairs={{0,1},{1,0},{2,3},{3,2},{4,5},{5,4},{6,7},{7,6},{8,9},{9,8},{10,11... | collective-permute-start | bytes 270344 | tf_op jit(solution)/shard_map/cond/branch_1_fun/ppermute | solution.py:75
  84.9 11.3 %collective-permute-start.14 = (bf16[4,176,256]{2,1,0:T(8,128)(2,1)}, bf16[4,176,256]{2,1,0:T(8,128)(2,1)}, u32[]{:S(2)}, u32[]{:S(2)}) collective-permute-start(bf16[4,176,256]{2,1,0:T(8,128)(2,1)} %get-tuple-element.132), channel_id=1, source_target_pairs={{0,2},{1,23},{2,4},{3,1},{4,6},{5,3},{6,8},{7,5},{8,10},{9,7},{10,... | collective-permute-start | bytes 1081352 | tf_op jit(solution)/shard_map/cond/branch_1_fun/ppermute | solution.py:317
  89.3 10.3 %collective-permute-start.15 = (bf16[4,176,256]{2,1,0:T(8,128)(2,1)}, bf16[4,176,256]{2,1,0:T(8,128)(2,1)}, u32[]{:S(2)}, u32[]{:S(2)}) collective-permute-start(bf16[4,176,256]{2,1,0:T(8,128)(2,1)} %get-tuple-element.133), channel_id=1, source_target_pairs={{0,22},{1,3},{2,0},{3,5},{4,2},{5,7},{6,4},{7,9},{8,6},{9,11},{10,... | collective-permute-start | bytes 1081352 | tf_op jit(solution)/shard_map/cond/branch_1_fun/ppermute | solution.py:318
  93.6 34.3 %copy-start.13 = (bf16[256,256]{1,0:T(8,128)(2,1)S(1)}, bf16[256,256]{1,0:T(8,128)(2,1)}, u32[]{:S(2)}) copy-start(bf16[256,256]{1,0:T(8,128)(2,1)} %get-tuple-element.111.x_ref) | copy-start | bytes 393220 | tf_op jit(solution)/shard_map/conditional
  148.0 0.7 copy-start.24

commit v8 on v7

--- a/solution.py
+++ b/solution.py
@@ -24,7 +24,10 @@
 
 Z_GROUPS = [[z * 2 + c for z in range(NZ)] for c in range(2)]
 FAR = 4
-FAR_GROUPS = [[(3 * k + r) * 2 + c for k in range(FAR)] for r in range(3) for c in range(2)]
+NDP = 32
+WIDE_GROUPS = [
+    [d * NT + (3 * k + r) * 2 + c for d in range(NDP) for k in range(FAR)] for r in range(3) for c in range(2)
+]
 SWAP = [(t, t ^ 1) for t in range(NT)]
 
 
@@ -310,20 +313,26 @@
     )(place, mine, theirs, *[w_mine] * FAR, *[w_theirs] * FAR)
 
 
-def sum_over_chips(place, context, theirs, w_mine, w_theirs, lengths, packing):
+def move_and_sum(place, x, context, theirs, w_mine, w_theirs, lengths, packing):
     one, two = out_project(place, context, theirs, w_mine, w_theirs, (1, 2))
     one, lengths, packing = lax.optimization_barrier((one, lengths, packing))
     picks = make_picks(place, lengths, packing, context.shape[0])
     below = lax.ppermute(one, "tensor", [(t, (t + 2 - 4 * (t % 2)) % NT) for t in range(NT)])
     above = lax.ppermute(two, "tensor", [(t, (t - 2 + 4 * (t % 2)) % NT) for t in range(NT)])
     (own,) = out_project(place, context, theirs, w_mine, w_theirs, (0,))
+    at_home = jnp.arange(FAR)[:, None, None] == lax.axis_index("tensor") // 6
     three = own.astype(jnp.float32) + below.astype(jnp.float32) + above.astype(jnp.float32)
-    three, *picks = lax.optimization_barrier((three.astype(jnp.bfloat16), *picks))
+    three += jnp.where(at_home, x.astype(jnp.float32)[None], 0.0)
+    three, out_pick, in_pick = lax.optimization_barrier((three.astype(jnp.bfloat16), *picks))
+    moved = jnp.stack(
+        [jnp.dot(out_pick, three[k], preferred_element_type=jnp.float32).astype(jnp.bfloat16) for k in range(FAR)]
+    )
+    moved = moved.reshape(FAR, RPS, MAXLEN, FS).transpose(1, 0, 2, 3).reshape(RPS * FAR, MAXLEN, FS)
     parts = lax.all_to_all(
-        three, "tensor", split_axis=0, concat_axis=0, tiled=True,
-        axis_index_groups=FAR_GROUPS,
-    )
-    return jnp.sum(parts.astype(jnp.float32), axis=0), *picks
+        moved, ("dp", "tensor"), split_axis=0, concat_axis=0, tiled=True, axis_index_groups=WIDE_GROUPS
+    ).reshape(RPS, FAR, MAXLEN, FS)
+    incoming = jnp.sum(parts.astype(jnp.float32), axis=1).astype(jnp.bfloat16).reshape(RPS * MAXLEN, FS)
+    return jnp.dot(in_pick, incoming, preferred_element_type=jnp.float32).astype(jnp.bfloat16)
 
 
 def split_kernel(x_ref, head, tail):
@@ -430,15 +439,9 @@
     second = lax.ppermute(keyval, "tensor", kv_pairs(False))
     q, cosine, sine, bias = project_q(core, mine, theirs, tail, gain, query_weight, inverse, lengths)
     context = attend(core, q, first, second, cosine, sine, bias)
-    summed, out_pick, in_pick = sum_over_chips(
-        core, context, swap(context), out_weight, swap(out_weight), lengths, packing
+    return move_and_sum(
+        core, x, context, swap(context), out_weight, swap(out_weight), lengths, packing
     )
-    result = (summed + x.astype(jnp.float32)).astype(jnp.bfloat16)
-    outgoing = jnp.dot(out_pick, result, preferred_element_type=jnp.float32).astype(jnp.bfloat16)
-    incoming = lax.all_to_all(
-        outgoing.reshape(RPS, MAXLEN, FS), "dp", split_axis=0, concat_axis=0, tiled=True
-    ).reshape(RPS * MAXLEN, FS)
-    return jnp.dot(in_pick, incoming, preferred_element_type=jnp.float32).astype(jnp.bfloat16)
 
 
 def size_kernel(lengths, size):

time: 149 us -> 139 us (0.933)
  the two profiles are of different devices: /device:TPU:8 before, /device:TPU:64 now
where the time goes in v8:
time: 139 us; the launch traced here: 138 us
  blocking collectives  81.3 us (58%)
  starting transfers between devices  26.2 us (19%)
  Pallas kernels  17 us (12%)
  waiting for transfers between devices  7.37 us (5%)
  other arithmetic  3.06 us (2%)
    all_to_all x1, blocking collectives, move_and_sum(): lax.all_to_all(moved, ('dp', 'tensor'), split_axis=0, concat_axis=0, tile...  44.4 us
    all_gather x1, blocking collectives, gather_rows(): lax.all_gather(head, 'tensor', axis=0, axis_index_groups=Z_GROUPS)  37 us
    ppermute x4, starting transfers between devices, swap(): return lax.ppermute(v, 'tensor', SWAP)  8.29 us
    ppermute x1, starting transfers between devices, move_and_sum(): lax.ppermute(two, 'tensor', [(t, (t - 2 + 4 * (t % 2)) % NT) for t in ran...  8.14 us
    pallas_call x2, Pallas kernels, out_project(): pl.pallas_call(out_kernel, grid_spec=pltpu.PrefetchScalarGridSpec(num_sca...  4.87 us
    ppermute x1, starting transfers between devices, layer(): first = lax.ppermute(keyval, 'tensor', kv_pairs(True))  4.31 us
    pallas_call x1, Pallas kernels, project_q(): pl.pallas_call(functools.partial(q_kernel, tail is not None), grid_spec=p...  4.16 us
    pallas_call x1, Pallas kernels, project_kv(): pl.pallas_call(functools.partial(kv_kernel, tail is not None), grid_spec=...  4.05 us
  transfers between devices with their start and end apart: 8, of which 4 were waited for; matrix products, arithmetic and copies ran while one was open for 1% of the time, Pallas kernels for 9%

profile of v8, /device:TPU:64, one launch (start us, length us, event | category | flops | bytes accessed | tf_op | source)
XLA Modules:
  0.0 138.1 jit_solution(15852177147971803270)
XLA Ops:
  0.0 1.4 size.1
  2.0 135.5 %conditional.2 = (bf16[256,256]{1,0:T(8,128)(2,1)S(1)}) conditional(s32[]{:T(128)} %bitcast.96, (bf16[256,256]{1,0:T(8,128)(2,1)}, bf16[6144,64]{0,1:T(8,128)(2,1)}, f32[6144]{0:T(1024)}, bf16[6144,256]{1,0:T(8,128)(2,1)}, s32[32,32]{1,0:T(8,128)}, /*index=5*/f32[8,128]{1,0:T(8,128)}, f32[8,128]{1,0:T(8,128)}, ...), branch_computations={%region_0.2_spmd, %region_2.4_spmd, %region_4.6_spmd, %region_6.8_... | conditional | flops 2251554816 | bytes 83965048
  2.1 2.1 %collective-permute-start.5 = (bf16[256,6144]{1,0:T(8,128)(2,1)}, bf16[256,6144]{1,0:T(8,128)(2,1)S(1)}, u32[]{:S(2)}, u32[]{:S(2)}) collective-permute-start(bf16[256,6144]{1,0:T(8,128)(2,1)} %get-tuple-element.99.rest_0_.rest_1_.rest_2_.rest_3_), channel_id=1, source_target_pairs={{0,1},{1,0},{2,3},{3,2},{4,5},{5,4},{6,7},{7,6},{8,9},{9,8},{10,11... | collective-permute-start | bytes 9437192 | tf_op jit(solution)/shard_map/cond/branch_0_fun/ppermute | solution.py:78
  4.1 1.6 %slice_convert_fusion = (f32[168,256]{1,0:T(8,128)}, bf16[168,256]{1,0:T(8,128)(2,1)S(1)}) fusion(bf16[256,256]{1,0:T(8,128)(2,1)} %get-tuple-element.84), kind=kLoop, calls=%fused_computation.23 | loop fusion | flops 43008 | bytes 344064 | tf_op jit(solution)/shard_map/cond/branch_0_fun/convert_element_type | solution.py:325
  5.7 37.0 %all-gather = bf16[2016,256]{1,0:T(8,128)(2,1)} all-gather(bf16[168,256]{1,0:T(8,128)(2,1)S(1)} %get-tuple-element.202), channel_id=2, replica_groups={{0,2,4,6,8,10,12,14,16,18,20,22},{1,3,5,7,9,11,13,15,17,19,21,23},{24,2..., dimensions={0}, use_global_device_ids=true | all-gather | bytes 1118208 | tf_op jit(solution)/shard_map/cond/branch_0_fun/all_gather | solution.py:362
  42.7 1.9 %collective-permute-start = (bf16[12,168,256]{2,1,0:T(8,128)(2,1)}, bf16[12,168,256]{2,1,0:T(8,128)(2,1)}, u32[]{:S(2)}, u32[]{:S(2)}) collective-permute-start(bf16[12,168,256]{2,1,0:T(8,128)(2,1)} %bitcast.4.mine), channel_id=1, source_target_pairs={{0,1},{1,0},{2,3},{3,2},{4,5},{5,4},{6,7},{7,6},{8,9},{9,8},{10,11... | collective-permute-start | bytes 3096584 | tf_op jit(solution)/shard_map/cond/branch_0_fun/ppermute | solution.py:78
  44.6 2.4 %collective-permute-start.1 = (bf16[64,6144]{1,0:T(8,128)(2,1)}, bf16[64,6144]{1,0:T(8,128)(2,1)}, u32[]{:S(2)}, u32[]{:S(2)}) collective-permute-start(bf16[64,6144]{1,0:T(8,128)(2,1)} %bitcast.214), channel_id=1, source_target_pairs={{0,1},{1,0},{2,3},{3,2},{4,5},{5,4},{6,7},{7,6},{8,9},{9,8},{10,11... | collective-permute-start | bytes 2359304 | tf_op jit(solution)/shard_map/cond/branch_0_fun/ppermute | solution.py:78
  47.2 2.1 %collective-permute-done.1.rest_2_ = bf16[64,6144]{1,0:T(8,128)(2,1)} collective-permute-done((bf16[64,6144]{1,0:T(8,128)(2,1)}, bf16[64,6144]{1,0:T(8,128)(2,1)}, u32[]{:S(2)}, u32[]{:S(2)}) %collective-permute-start.1) | collective-permute-done | bytes 786464 | tf_op jit(solution)/shard_map/cond/branch_0_fun/ppermute | solution.py:78
  49.3 4.0 %project_kv.4 = (bf16[168,128]{1,0:T(8,128)(2,1)S(1)}, f32[168,128]{1,0:T(8,128)S(1)}) custom-call(s32[4]{0:T(128)S(1)} %pad_add_fusion.core.place, bf16[12,168,256]{2,1,0:T(8,128)(2,1)} %bitcast.4.mine, bf16[12,168,256]{2,1,0:T(8,128)(2,1)} %collective-permute-done.theirs, f32[24,1,256]{2,1,0:T(1,128)} %bitcast.226, bf16[64,6144]{1,0:T(8,128)(2,1)} %bitcast.215, ...), custom_call_target="tpu_custom_call" | custom-call | flops 264241152 | bytes 3637248 | tf_op jit(solution)/shard_map/cond/branch_0_fun/project_kv/pallas_call | solution.py:181
  53.3 4.3 %collective-permute-start.2 = (bf16[168,128]{1,0:T(8,128)(2,1)S(1)}, bf16[168,128]{1,0:T(8,128)(2,1)S(1)}, u32[]{:S(2)}, u32[]{:S(2)}) collective-permute-start(bf16[168,128]{1,0:T(8,128)(2,1)S(1)} %get-tuple-element.95), channel_id=1, source_target_pairs={{0,0},{1,1},{2,4},{3,5},{4,8},{5,9},{6,12},{7,13},{8,16},{9,17},{1... | collective-permute-start | bytes 129032 | tf_op jit(solution)/shard_map/cond/branch_0_fun/ppermute | solution.py:438
  57.6 3.3 %collective-permute-start.3 = (bf16[168,128]{1,0:T(8,128)(2,1)S(1)}, bf16[168,128]{1,0:T(8,128)(2,1)S(1)}, u32[]{:S(2)}, u32[]{:S(2)}) collective-permute-start(bf16[168,128]{1,0:T(8,128)(2,1)S(1)} %get-tuple-element.95), channel_id=1, source_target_pairs={{0,2},{1,3},{2,6},{3,7},{4,10},{5,11},{6,14},{7,15},{8,18},{9,19},... | collective-permute-start | bytes 129032 | tf_op jit(solution)/shard_map/cond/branch_0_fun/ppermute | solution.py:439
  61.0 4.2 %project_q.4 = (bf16[168,256]{1,0:T(8,128)(2,1)S(1)}, f32[168,128]{1,0:T(8,128)S(1)}, f32[168,128]{1,0:T(8,128)S(1)}, f32[168,168]{1,0:T(8,128)S(1)}) custom-call(s32[4]{0:T(128)S(1)} %pad_add_fusion.core.place, bf16[12,168,256]{2,1,0:T(8,128)(2,1)} %bitcast.4.mine, bf16[12,168,256]{2,1,0:T(8,128)(2,1)} %collective-permute-done.theirs, ...), custom_call_target="tpu_custom_call" | custom-call | flops 528482304 | bytes 5210112 | tf_op jit(solution)/shard_map/cond/branch_0_fun/project_q/pallas_call | solution.py:207
  65.2 1.4 %attend.4.mine = bf16[168,256]{1,0:T(8,128)(2,1)S(1)} custom-call(s32[4]{0:T(128)S(1)} %pad_add_fusion.core.place, bf16[168,256]{1,0:T(8,128)(2,1)S(1)} %get-tuple-element.94.q_ref, bf16[168,128]{1,0:T(8,128)(2,1)S(1)} %collective-permute-done.2.first, bf16[168,128]{1,0:T(8,128)(2,1)S(1)} %collective-permute-done.3.second, ...), custom_call_target="tpu_custom_call" | custom-call | flops 28901376 | bytes 172032 | tf_op jit(solution)/shard_map/cond/branch_0_fun/attend/pallas_call | solution.py:264
  66.7 1.9 %collective-permute-start.4 = (bf16[168,256]{1,0:T(8,128)(2,1)S(1)}, bf16[168,256]{1,0:T(8,128)(2,1)S(1)}, u32[]{:S(2)}, u32[]{:S(2)}) collective-permute-start(bf16[168,256]{1,0:T(8,128)(2,1)S(1)} %attend.4.mine), channel_id=1, source_target_pairs={{0,1},{1,0},{2,3},{3,2},{4,5},{5,4},{6,7},{7,6},{8,9},{9,8},{10,11... | collective-permute-start | bytes 258056 | tf_op jit(solution)/shard_map/cond/branch_0_fun/ppermute | solution.py:78
  68.6 1.2 collective-permute-done.4.theirs
  69.8 2.8 %out_project.9 = (bf16[4,168,256]{2,1,0:T(8,128)(2,1)}, bf16[4,168,256]{2,1,0:T(8,128)(2,1)}) custom-call(s32[4]{0:T(128)S(1)} %pad_add_fusion.core.place, bf16[168,256]{1,0:T(8,128)(2,1)S(1)} %attend.4.mine, bf16[168,256]{1,0:T(8,128)(2,1)S(1)} %collective-permute-done.4.theirs, bf16[256,6144]{1,0:T(8,128)(2,1)S(1)} %copy-done.4, ...), custom_call_target="tpu_custom_call" | custom-call | flops 352321536 | bytes 2785280 | tf_op jit(solution)/shard_map/cond/branch_0_fun/out_project/pallas_call | solution.py:297
  72.7 8.1 %collective-permute-start.7 = (bf16[4,168,256]{2,1,0:T(8,128)(2,1)}, bf16[4,168,256]{2,1,0:T(8,128)(2,1)}, u32[]{:S(2)}, u32[]{:S(2)}) collective-permute-start(bf16[4,168,256]{2,1,0:T(8,128)(2,1)} %get-tuple-element.103), channel_id=1, source_target_pairs={{0,22},{1,3},{2,0},{3,5},{4,2},{5,7},{6,4},{7,9},{8,6},{9,11},{10,... | collective-permute-start | bytes 1032200 | tf_op jit(solution)/shard_map/cond/branch_0_fun/ppermute | solution.py:321
  80.8 2.1 %collective-permute-start.6 = (bf16[4,168,256]{2,1,0:T(8,128)(2,1)}, bf16[4,168,256]{2,1,0:T(8,128)(2,1)}, u32[]{:S(2)}, u32[]{:S(2)}) collective-permute-start(bf16[4,168,256]{2,1,0:T(8,128)(2,1)} %get-tuple-element.102), channel_id=1, source_target_pairs={{0,2},{1,23},{2,4},{3,1},{4,6},{5,3},{6,8},{7,5},{8,10},{9,7},{10,... | collective-permute-start | bytes 1032200 | tf_op jit(solution)/shard_map/cond/branch_0_fun/ppermute | solution.py:320
  83.1 1.1 make_picks.4
  84.2 2.0 %out_project.8 = bf16[4,168,256]{2,1,0:T(8,128)(2,1)S(1)} custom-call(s32[4]{0:T(128)S(1)} %pad_add_fusion.core.place, bf16[168,256]{1,0:T(8,128)(2,1)S(1)} %attend.4.mine, bf16[168,256]{1,0:T(8,128)(2,1)S(1)} %collective-permute-done.4.theirs, bf16[256,6144]{1,0:T(8,128)(2,1)} %get-tuple-element.99.rest_0_.rest_1_.rest_2_.rest_3_, ...), custom_call_target="tpu_custom_call" | custom-call | flops 176160768 | bytes 1392640 | tf_op jit(solution)/shard_map/cond/branch_0_fun/out_project/pallas_call | solution.py:297
  86.3 2.0 %collective-permute-done.7 = bf16[4,168,256]{2,1,0:T(8,128)(2,1)} collective-permute-done((bf16[4,168,256]{2,1,0:T(8,128)(2,1)}, bf16[4,168,256]{2,1,0:T(8,128)(2,1)}, u32[]{:S(2)}, u32[]{:S(2)}) %collective-permute-start.7) | collective-permute-done | bytes 344096 | tf_op jit(solution)/shard_map/cond/branch_0_fun/ppermute | solution.py:321
  88.2 2.1 %collective-permute-done.6 = bf16[4,168,256]{2,1,0:T(8,128)(2,1)} collective-permute-done((bf16[4,168,256]{2,1,0:T(8,128)(2,1)}, bf16[4,168,256]{2,1,0:T(8,128)(2,1)}, u32[]{:S(2)}, u32[]{:S(2)}) %collective-permute-start.6) | collective-permute-done | bytes 344096 | tf_op jit(solution)/shard_map/cond/branch_0_fun/ppermute | solution.py:320
  90.3 1.3 add_convert_fusion
  92.4 44.4 %all_to_all.28 = bf16[128,8,256]{2,1,0:T(8,128)(2,1)S(1)} all-to-all(bf16[128,8,256]{2,1,0:T(8,128)(2,1)S(1)} %bitcast.222), channel_id=1, replica_groups={{0,6,12,18,24,30,36,42,48,54,60,66,72,78,84,90,96,102,108,114,120,126,1..., dimensions={0} | all-to-all | bytes 1048576 | tf_op jit(solution)/shard_map/cond/branch_0_fun/all_to_all | solution.py:331
  (32 shorter events, 1.9 us)
Async XLA Ops:
  2.0 58.9 %copy-start.13 = (f32[6144]{0:T(1024)S(1)}, f32[6144]{0:T(1024)}, u32[]{:S(2)}) copy-start(f32[6144]{0:T(1024)} %get-tuple-element.87) | copy-start | bytes 73732 | tf_op jit(solution)/shard_map/conditional
  2.0 58.9 %copy-start.17 = (s32[32,32]{1,0:T(8,128)S(1)}, s32[32,32]{1,0:T(8,128)}, u32[]{:S(2)}) copy-start(s32[32,32]{1,0:T(8,128)} %get-tuple-element.104.rest_4_.lengths) | copy-start | bytes 12292 | tf_op jit(solution)/shard_map/conditional
  2.1 58.9 %copy-start.25 = (f32[8,128]{1,0:T(8,128)S(1)}, f32[8,128]{1,0:T(8,128)}, u32[]{:S(2)}) copy-start(f32[8,128]{1,0:T(8,128)} %get-tuple-element.92.rest_5_) | copy-start | bytes 12292 | tf_op jit(solution)/shard_map/conditional
  2.1 58.9 %copy-start.29 = (f32[8,128]{1,0:T(8,128)S(1)}, f32[8,128]{1,0:T(8,128)}, u32[]{:S(2)}) copy-start(f32[8,128]{1,0:T(8,128)} %get-tuple-element.93.rest_6_) | copy-start | bytes 12292 | tf_op jit(solution)/shard_map/conditional
  2.1 67.8 %collective-permute-start.5 = (bf16[256,6144]{1,0:T(8,128)(2,1)}, bf16[256,6144]{1,0:T(8,128)(2,1)S(1)}, u32[]{:S(2)}, u32[]{:S(2)}) collective-permute-start(bf16[256,6144]{1,0:T(8,128)(2,1)} %get-tuple-element.99.rest_0_.rest_1_.rest_2_.rest_3_), channel_id=1, source_target_pairs={{0,1},{1,0},{2,3},{3,2},{4,5},{5,4},{6,7},{7,6},{8,9},{9,8},{10,11... | collective-permute-start | bytes 9437192 | tf_op jit(solution)/shard_map/cond/branch_0_fun/ppermute | solution.py:78
  42.7 6.6 %collective-permute-start = (bf16[12,168,256]{2,1,0:T(8,128)(2,1)}, bf16[12,168,256]{2,1,0:T(8,128)(2,1)}, u32[]{:S(2)}, u32[]{:S(2)}) collective-permute-start(bf16[12,168,256]{2,1,0:T(8,128)(2,1)} %bitcast.4.mine), channel_id=1, source_target_pairs={{0,1},{1,0},{2,3},{3,2},{4,5},{5,4},{6,7},{7,6},{8,9},{9,8},{10,11... | collective-permute-start | bytes 3096584 | tf_op jit(solution)/shard_map/cond/branch_0_fun/ppermute | solution.py:78
  44.6 4.6 %collective-permute-start.1 = (bf16[64,6144]{1,0:T(8,128)(2,1)}, bf16[64,6144]{1,0:T(8,128)(2,1)}, u32[]{:S(2)}, u32[]{:S(2)}) collective-permute-start(bf16[64,6144]{1,0:T(8,128)(2,1)} %bitcast.214), channel_id=1, source_target_pairs={{0,1},{1,0},{2,3},{3,2},{4,5},{5,4},{6,7},{7,6},{8,9},{9,8},{10,11... | collective-permute-start | bytes 2359304 | tf_op jit(solution)/shard_map/cond/branch_0_fun/ppermute | solution.py:78
  47.1 13.9 %copy-start.7 = (bf16[6144,256]{1,0:T(8,128)(2,1)S(1)}, bf16[6144,256]{1,0:T(8,128)(2,1)}, u32[]{:S(2)}) copy-start(bf16[6144,256]{1,0:T(8,128)(2,1)} %get-tuple-element.88) | copy-start | bytes 9437188 | tf_op jit(solution)/shard_map/conditional
  53.3 11.9 %collective-permute-start.2 = (bf16[168,128]{1,0:T(8,128)(2,1)S(1)}, bf16[168,128]{1,0:T(8,128)(2,1)S(1)}, u32[]{:S(2)}, u32[]{:S(2)}) collective-permute-start(bf16[168,128]{1,0:T(8,128)(2,1)S(1)} %get-tuple-element.95), channel_id=1, source_target_pairs={{0,0},{1,1},{2,4},{3,5},{4,8},{5,9},{6,12},{7,13},{8,16},{9,17},{1... | collective-permute-start | bytes 129032 | tf_op jit(solution)/shard_map/cond/branch_0_fun/ppermute | solution.py:438
  57.6 7.6 %collective-permute-start.3 = (bf16[168,128]{1,0:T(8,128)(2,1)S(1)}, bf16[168,128]{1,0:T(8,128)(2,1)S(1)}, u32[]{:S(2)}, u32[]{:S(2)}) collective-permute-start(bf16[168,128]{1,0:T(8,128)(2,1)S(1)} %get-tuple-element.95), channel_id=1, source_target_pairs={{0,2},{1,3},{2,6},{3,7},{4,10},{5,11},{6,14},{7,15},{8,18},{9,19},... | collective-permute-start | bytes 129032 | tf_op jit(solution)/shard_map/cond/branch_0_fun/ppermute | solution.py:439
  61.0 8.8 %copy-start.4 = (bf16[256,6144]{1,0:T(8,128)(2,1)S(1)}, bf16[256,6144]{1,0:T(8,128)(2,1)}, u32[]{:S(2)}) copy-start(bf16[256,6144]{1,0:T(8,128)(2,1)} %get-tuple-element.99.rest_0_.rest_1_.rest_2_.rest_3_) | copy-start | bytes 9437188 | tf_op jit(solution)/shard_map/conditional
  66.6 16.4 %copy-start.33 = (s32[1024]{0:T(1024)S(1)}, s32[1024]{0:T(1024)}, u32[]{:S(2)}) copy-start(s32[1024]{0:T(1024)} %get-tuple-element.105) | copy-start | bytes 12292 | tf_op jit(solution)/shard_map/conditional
  66.7 3.2 %collective-permute-start.4 = (bf16[168,256]{1,0:T(8,128)(2,1)S(1)}, bf16[168,256]{1,0:T(8,128)(2,1)S(1)}, u32[]{:S(2)}, u32[]{:S(2)}) collective-permute-start(bf16[168,256]{1,0:T(8,128)(2,1)S(1)} %attend.4.mine), channel_id=1, source_target_pairs={{0,1},{1,0},{2,3},{3,2},{4,5},{5,4},{6,7},{7,6},{8,9},{9,8},{10,11... | collective-permute-start | bytes 258056 | tf_op jit(solution)/shard_map/cond/branch_0_fun/ppermute | solution.py:78
  72.7 15.5 %collective-permute-start.7 = (bf16[4,168,256]{2,1,0:T(8,128)(2,1)}, bf16[4,168,256]{2,1,0:T(8,128)(2,1)}, u32[]{:S(2)}, u32[]{:S(2)}) collective-permute-start(bf16[4,168,256]{2,1,0:T(8,128)(2,1)} %get-tuple-element.103), channel_id=1, source_target_pairs={{0,22},{1,3},{2,0},{3,5},{4,2},{5,7},{6,4},{7,9},{8,6},{9,11},{10,... | collective-permute-start | bytes 1032200 | tf_op jit(solution)/shard_map/cond/branch_0_fun/ppermute | solution.py:321
  80.8 9.5 %collective-permute-start.6 = (bf16[4,168,256]{2,1,0:T(8,128)(2,1)}, bf16[4,168,256]{2,1,0:T(8,128)(2,1)}, u32[]{:S(2)}, u32[]{:S(2)}) collective-permute-start(bf16[4,168,256]{2,1,0:T(8,128)(2,1)} %get-tuple-element.102), channel_id=1, source_target_pairs={{0,2},{1,23},{2,4},{3,1},{4,6},{5,3},{6,8},{7,5},{8,10},{9,7},{10,... | collective-permute-start | bytes 1032200 | tf_op jit(solution)/shard_map/cond/branch_0_fun/ppermute | solution.py:320
  84.2 6.1 %copy-start.23 = (f32[168,256]{1,0:T(8,128)S(1)}, f32[168,256]{1,0:T(8,128)}, u32[]{:S(2)}) copy-start(f32[168,256]{1,0:T(8,128)} %get-tuple-element.201) | copy-start | bytes 516100 | tf_op jit(solution)/shard_map/conditional
  137.5 0.7 copy-start.24
